TPU v7x, 256 devices: a whole 4x4x8 slice. The times are simulated.
256 devices in a mesh: grp: 2 (over core), seq: 16 (over y, z_hi), fsdp: 8 (over x, z_lo).
Axes of the slice: x: 4, y: 4, z: 8 (z_hi: 4, z_lo: 2; z = z_hi * 2 + z_lo), core: 2. Of those that a mesh axis runs over, the one named last changes fastest.
Arguments:
- new_rows: bfloat16 [2048, 5120], P('seq'), may hold values from -6 to 6
- cache_keys: bfloat16 [4, 1024, 3072], P(None, None, 'fsdp'), may hold values from -16 to 16
- cache_values: bfloat16 [4, 1024, 3072], P(None, None, 'fsdp'), may hold values from -6 to 6
- cache_frames: int32 [3], replicated, may hold values from 0 to 3
- real_bank: bfloat16 [2, 2048, 5120], P(None, 'seq'), may hold values from -6 to 6
- real_pick: int32 [2048], P('seq'), may hold values from 0 to 1
- attn_weights: bfloat16 [2, 3, 5120, 3072], P('grp', None, 'seq', 'fsdp'), may hold values from -1 to 1
- out_weights: bfloat16 [2, 3072, 5120], P('grp', 'seq', 'fsdp'), may hold values from -0.109375 to 0.109375
- norm_gains: float32 [2, 5120], P('grp'), may hold values from 0.5 to 1.5
- head_in: bfloat16 [5120, 128], P('fsdp'), may hold values from -0.078125 to 0.078125
- head_out: float32 [128], replicated, may hold values from -0.5 to 0.5
Outputs:
- wo_grads: bfloat16 [2, 3072, 5120], P('grp', 'seq', 'fsdp')
- losses: bfloat16 [2], P('grp')
All inputs are finite; a program needn't handle non-finite values.
Results may differ from a plain program's by a relative error of at most 0.014.
The roundings to bfloat16 on the way count: a program that leaves them out, or rounds other values in their place, can miss the bound.
Values may be sent and summed in bfloat16 or wider, within the bound.
No kernel may reach another device: no remote copies, remote signals or barrier semaphores. Data moves between devices by JAX's collectives and lax.ppermute only.
A program may use at most 128 MiB of HBM per device.

v0:
```python
import jax
import jax.numpy as jnp
from jax import lax
from jax.sharding import PartitionSpec as P

HD = 128


EPS = 1e-06
NEG = -1e30


def passed_along(value, axis, steps):
    count = lax.axis_size(axis)
    leading, last = (max(0, -steps), min(count, count - steps))
    return lax.ppermute(value, axis, [(source, source + steps) for source in range(leading, last)])


def attend(queries, key_set, value_set, allowed):
    head_size = queries.shape[-1]
    scores = jnp.einsum(
        "rhd,khd->hrk", queries, key_set, preferred_element_type=jnp.float32
    ) * head_size ** (-0.5)
    if allowed is not None:
        scores = jnp.where(allowed[None], scores, NEG)
    row_max = jnp.max(scores, axis=-1, keepdims=True)
    raised = jnp.exp(scores - row_max)
    weights = raised / jnp.sum(raised, axis=-1, keepdims=True)
    result = jnp.einsum(
        "hrk,khd->rhd", weights.astype(jnp.bfloat16), value_set, preferred_element_type=jnp.float32
    )
    return (result, weights)


def project(row_block, gain_vector, weight_set):
    lifted = row_block.astype(jnp.float32)
    inverse = lax.rsqrt(jnp.mean(lifted * lifted, axis=-1, keepdims=True) + EPS)
    normed = (lifted * inverse * gain_vector).astype(jnp.bfloat16)
    projected = jnp.einsum("rd,cde->cre", normed, weight_set, preferred_element_type=jnp.float32)
    return (projected.astype(jnp.bfloat16), lifted, inverse)


def unit_direction(unit_values, head_out, head_cols):
    _, gelu_back = jax.vjp(jax.nn.gelu, unit_values)
    unit_grad = gelu_back(jnp.broadcast_to(head_out, unit_values.shape))[0].astype(jnp.bfloat16)
    return jnp.einsum("ru,cu->rc", unit_grad, head_cols, preferred_element_type=jnp.float32)


def pick_rows(real_bank, real_pick):
    chosen = jnp.zeros(real_bank.shape[1:], real_bank.dtype)
    for entry in range(real_bank.shape[0]):
        chosen = jnp.where((real_pick == entry)[:, None], real_bank[entry], chosen)
    return chosen


def local(
    new_rows,
    cache_keys,
    cache_values,
    cache_frames,
    real_bank,
    real_pick,
    attn_weights,
    out_weights,
    norm_gains,
    head_in,
    head_out,
):
    is_gen = lax.axis_index("grp") == 0
    seq_at = lax.axis_index("seq")
    fsdp_at = lax.axis_index("fsdp")
    row_count = new_rows.shape[0]
    local_weights = attn_weights[0]
    local_out = out_weights[0]
    col_count = local_out.shape[1]
    heads_width = local_weights.shape[2]
    head_count = heads_width // HD
    gain_vector = norm_gains[0]
    full_weights = lax.all_gather(local_weights, "seq", axis=1, tiled=True)
    full_out = lax.all_gather(local_out, "seq", axis=0, tiled=True)
    real_rows = pick_rows(real_bank, real_pick)
    first_rows = jnp.where(is_gen, new_rows, real_rows)
    first_proj, _, _ = project(first_rows, gain_vector, full_weights)
    first_keys, first_values = (
        lax.all_gather(first_proj[1], "seq", axis=0, tiled=True),
        lax.all_gather(first_proj[2], "seq", axis=0, tiled=True),
    )
    key_count = first_keys.shape[0]
    frame_len = key_count // 2
    first_query = first_proj[0].reshape(row_count, head_count, HD)
    own_keys = first_keys.reshape(key_count, head_count, HD)
    own_values = first_values.reshape(key_count, head_count, HD)

    def generator_attend(operand):
        picked_keys = jnp.take(cache_keys, cache_frames, axis=0).reshape(-1, head_count, HD)
        picked_values = jnp.take(cache_values, cache_frames, axis=0).reshape(-1, head_count, HD)
        query_frame = (seq_at * row_count + jnp.arange(row_count)) // frame_len
        key_frame = jnp.arange(key_count) // frame_len
        allowed = jnp.concatenate(
            [
                jnp.ones((row_count, picked_keys.shape[0]), jnp.bool_),
                key_frame[None, :] <= query_frame[:, None],
            ],
            axis=1,
        )
        all_keys = jnp.concatenate([picked_keys, own_keys], axis=0)
        all_values = jnp.concatenate([picked_values, own_values], axis=0)
        return attend(first_query, all_keys, all_values, allowed)[0].astype(jnp.bfloat16)

    def critic_attend(operand):
        return attend(first_query, own_keys, own_values, None)[0].astype(jnp.bfloat16)

    first_heads = lax.cond(is_gen, generator_attend, critic_attend, 0).reshape(
        row_count, heads_width
    )
    first_all = lax.all_gather(first_heads, "fsdp", axis=1, tiled=True)
    start_col = fsdp_at * col_count
    first_cols = lax.dynamic_slice_in_dim(first_rows, start_col, col_count, 1).astype(jnp.float32)
    first_out = (
        first_cols + jnp.dot(first_all, full_out, preferred_element_type=jnp.float32)
    ).astype(jnp.bfloat16)
    real_units = jnp.dot(first_out, head_in, preferred_element_type=jnp.float32)
    whole_rows = lax.all_gather(first_out, "fsdp", axis=1, tiled=True)
    second_rows = passed_along(whole_rows, "grp", 1)
    second_proj, second_lifted, second_inverse = project(second_rows, gain_vector, full_weights)
    second_keys, second_values = (
        lax.all_gather(second_proj[1], "seq", axis=0, tiled=True),
        lax.all_gather(second_proj[2], "seq", axis=0, tiled=True),
    )
    keys_two = second_keys.reshape(key_count, head_count, HD)
    values_two = second_values.reshape(key_count, head_count, HD)
    query_two = second_proj[0].reshape(row_count, head_count, HD)
    second_result, second_weights = attend(query_two, keys_two, values_two, None)
    second_heads = second_result.astype(jnp.bfloat16).reshape(row_count, heads_width)
    second_all = lax.all_gather(second_heads, "fsdp", axis=1, tiled=True)
    second_cols = lax.dynamic_slice_in_dim(second_lifted, start_col, col_count, 1)
    second_out = (
        second_cols + jnp.dot(second_all, full_out, preferred_element_type=jnp.float32)
    ).astype(jnp.bfloat16)
    fake_units = jnp.dot(second_out, head_in, preferred_element_type=jnp.float32)
    real_units, fake_units = (
        lax.psum(real_units.astype(jnp.bfloat16), "fsdp").astype(jnp.float32),
        lax.psum(fake_units.astype(jnp.bfloat16), "fsdp").astype(jnp.float32),
    )
    real_part = jnp.sum(jax.nn.gelu(real_units) * head_out)
    fake_part = jnp.sum(jax.nn.gelu(fake_units) * head_out)
    real_score, fake_score = lax.psum((real_part, fake_part), "seq")
    margin = (real_score - fake_score) / (row_count * lax.axis_size("seq"))
    loss_pair = jnp.stack([jax.nn.softplus(margin), jax.nn.softplus(-margin)]).astype(jnp.bfloat16)
    real_dir = unit_direction(real_units, head_out, head_in)
    fake_dir = unit_direction(fake_units, head_out, head_in)
    real_cot = (-jax.nn.sigmoid(-margin) * real_dir).astype(jnp.bfloat16)
    fake_cot = (jax.nn.sigmoid(-margin) * fake_dir).astype(jnp.bfloat16)
    gen_cot = (-jax.nn.sigmoid(margin) * fake_dir).astype(jnp.bfloat16)
    head_terms = jnp.einsum("rc,hc->rh", gen_cot, full_out, preferred_element_type=jnp.float32)
    head_grad = lax.psum_scatter(
        head_terms.astype(jnp.bfloat16), "fsdp", scatter_dimension=1, tiled=True
    ).reshape(row_count, head_count, HD)
    scale = HD ** (-0.5)
    slopes = jnp.einsum("rhd,khd->hrk", head_grad, values_two, preferred_element_type=jnp.float32)
    centred = jnp.sum(slopes * second_weights, axis=-1, keepdims=True)
    score_grad = (second_weights * (slopes - centred)).astype(jnp.bfloat16)
    query_grad = (
        jnp.einsum("hrk,khd->rhd", score_grad, keys_two, preferred_element_type=jnp.float32) * scale
    )
    key_part = (
        jnp.einsum("hrk,rhd->khd", score_grad, query_two, preferred_element_type=jnp.float32)
        * scale
    )
    value_part = jnp.einsum(
        "hrk,rhd->khd",
        second_weights.astype(jnp.bfloat16),
        head_grad,
        preferred_element_type=jnp.float32,
    )
    key_grad, value_grad = (
        lax.psum_scatter(
            key_part.reshape(key_count, heads_width).astype(jnp.bfloat16),
            "seq",
            scatter_dimension=0,
            tiled=True,
        ).astype(jnp.float32),
        lax.psum_scatter(
            value_part.reshape(key_count, heads_width).astype(jnp.bfloat16),
            "seq",
            scatter_dimension=0,
            tiled=True,
        ).astype(jnp.float32),
    )
    stacked_grads = jnp.stack(
        [query_grad.reshape(row_count, heads_width), key_grad, value_grad]
    ).astype(jnp.bfloat16)
    row_terms = jnp.einsum(
        "cre,cde->rd", stacked_grads, full_weights, preferred_element_type=jnp.float32
    )
    row_grad = lax.psum_scatter(
        row_terms.astype(jnp.bfloat16), "fsdp", scatter_dimension=1, tiled=True
    ).astype(jnp.float32)
    gain_cols = lax.dynamic_slice_in_dim(gain_vector, start_col, col_count, 0)
    lifted_grad = row_grad * gain_cols
    input_grad = (second_inverse * lifted_grad + gen_cot.astype(jnp.float32)).astype(jnp.bfloat16)
    back_grad, back_pair = passed_along((input_grad, loss_pair), "grp", -1)
    lead_cot = jnp.where(is_gen, back_grad, real_cot)
    tail_cot = jnp.where(is_gen, jnp.zeros_like(fake_cot), fake_cot)
    lead_term = jnp.einsum("rh,rc->hc", first_all, lead_cot, preferred_element_type=jnp.float32)
    tail_term = jnp.einsum("rh,rc->hc", second_all, tail_cot, preferred_element_type=jnp.float32)
    summed = lax.psum_scatter(
        (lead_term + tail_term).astype(jnp.bfloat16), "seq", scatter_dimension=0, tiled=True
    )
    losses = jnp.where(is_gen, back_pair[0], loss_pair[1])
    return (summed[None], losses[None])


def solution(mesh):
    placed = (
        P("seq", None),
        P(None, None, "fsdp"),
        P(None, None, "fsdp"),
        P(),
        P(None, "seq", None),
        P("seq"),
        P("grp", None, "seq", "fsdp"),
        P("grp", "seq", "fsdp"),
        P("grp", None),
        P("fsdp", None),
        P(),
    )
    return jax.shard_map(
        local,
        mesh=mesh,
        in_specs=placed,
        out_specs=(P("grp", "seq", "fsdp"), P("grp")),
        check_vma=False,
    )
```

profile of v0, /device:TPU:32, one launch (start us, length us, event | category | flops | bytes accessed | tf_op | source)
XLA Modules:
  0.0 1097.6 jit_solution(7726610988487512555)
XLA Ops:
  11.8 151.6 %all-gather.16.cloned.1.call-done = bf16[1,3,5120,384]{3,2,1,0:T(8,128)(2,1)} async-done(((bf16[1,3,320,384]{3,2,1,0:T(8,128)(2,1)}), bf16[1,3,5120,384]{3,2,1,0:T(8,128)(2,1)}) %all-gather.16.cloned.1.call-update) | async-done | bytes 11796496 | tf_op jit(solution)/shard_map/all_gather | solution.py:79
  163.3 6.3 fusion.81
  171.9 52.9 %all-gather.18.cloned.1.call-done = bf16[1,2048,384]{2,1,0:T(8,128)(2,1)} async-done(((bf16[1,128,384]{2,1,0:T(8,128)(2,1)}), bf16[1,2048,384]{2,1,0:T(8,128)(2,1)}) %all-gather.18.cloned.1.call-update) | async-done | bytes 1572880 | tf_op jit(solution)/shard_map/all_gather | solution.py:85
  226.5 55.1 %all-gather.20.cloned.1.call-done = bf16[1,2048,384]{2,1,0:T(8,128)(2,1)} async-done(((bf16[1,128,384]{2,1,0:T(8,128)(2,1)}), bf16[1,2048,384]{2,1,0:T(8,128)(2,1)}) %all-gather.20.cloned.1.call-update) | async-done | bytes 1572880 | tf_op jit(solution)/shard_map/all_gather | solution.py:86
  283.3 50.1 %conditional.2 = (bf16[128,3,128]{0,2,1:T(8,128)(2,1)S(1)}) conditional(s32[]{:T(128)} %convert_element_type.127, (bf16[128,3,128]{0,2,1:T(8,128)(2,1)S(1)}, bf16[2048,3,128]{0,2,1:T(8,128)(2,1)S(1)}, bf16[2048,3,128]{0,2,1:T(8,128)(2,1)S(1)}) %tuple.72, (bf16[4,1024,384]{2,1,0:T(8,128)(2,1)}, s32[3]{0:T(128)S(1)}, ...), branch_computations={%region_1.4_spmd, %region_4.8_spmd} | conditional | flops 1036804096 | bytes 88563848
  283.5 4.8 gather_fusion
  288.4 4.4 gather_fusion.1
  292.7 5.2 broadcast_select_fusion.1
  297.9 7.0 reshape.94
  305.0 3.6 copy.55
  313.1 5.1 fusion.186
  318.1 5.9 reshape.93
  327.7 5.7 fusion.17
  333.4 41.4 %all_gather.30 = bf16[128,3072]{0,1:T(8,128)(2,1)S(1)} all-gather(bf16[128,384]{0,1:T(8,128)(2,1)S(1)} %bitcast.149), channel_id=1, replica_groups=mesh['grp'=2,'seq'=16,'fsdp'=8] {'fsdp'}, dimensions={1}, use_global_device_ids=true | all-gather | bytes 884736 | tf_op jit(solution)/shard_map/all_gather | solution.py:116
  374.8 3.9 fusion.87
  378.7 41.0 %all-gather.14.cloned.1.call-done = bf16[128,5120]{1,0:T(8,128)(2,1)} async-done(((bf16[128,640]{1,0:T(8,128)(2,1)}), bf16[128,5120]{1,0:T(8,128)(2,1)}) %all-gather.14.cloned.1.call-update) | async-done | bytes 1310736 | tf_op jit(solution)/shard_map/all_gather | solution.py:123
  424.3 6.3 fusion.76
  435.0 52.3 %all-gather.24.cloned.1.call-done = bf16[1,2048,384]{2,1,0:T(8,128)(2,1)} async-done(((bf16[1,128,384]{2,1,0:T(8,128)(2,1)}), bf16[1,2048,384]{2,1,0:T(8,128)(2,1)}) %all-gather.24.cloned.1.call-update) | async-done | bytes 1572880 | tf_op jit(solution)/shard_map/all_gather | solution.py:127
  491.9 51.7 %all-gather.26.cloned.1.call-done = bf16[1,2048,384]{2,1,0:T(8,128)(2,1)} async-done(((bf16[1,128,384]{2,1,0:T(8,128)(2,1)}), bf16[1,2048,384]{2,1,0:T(8,128)(2,1)}) %all-gather.26.cloned.1.call-update) | async-done | bytes 1572880 | tf_op jit(solution)/shard_map/all_gather | solution.py:128
  548.5 30.9 %all_gather.35 = bf16[128,3072]{0,1:T(8,128)(2,1)S(1)} all-gather(bf16[128,384]{0,1:T(8,128)(2,1)S(1)} %bitcast.155), channel_id=1, replica_groups=mesh['grp'=2,'seq'=16,'fsdp'=8] {'fsdp'}, dimensions={1}, use_global_device_ids=true | all-gather | bytes 884736 | tf_op jit(solution)/shard_map/all_gather | solution.py:135
  579.4 4.0 convolution_convert_fusion.2
  583.5 73.2 %all-reduce.5.cloned.1.call-done = (bf16[128,128]{1,0:T(8,128)(2,1)}, bf16[128,128]{1,0:T(8,128)(2,1)}) async-done(((bf16[128,128]{1,0:T(8,128)(2,1)}, bf16[128,128]{1,0:T(8,128)(2,1)}), (bf16[128,128]{1,0:T(8,128)(2,1)}, bf16[128,128]{1,0:T(8,128)(2,1)})) %all-reduce.5.cloned.1.call-update) | async-done | bytes 65552 | tf_op jit(solution)/shard_map/psum | solution.py:143
  658.1 46.0 %all-reduce.1 = (f32[]{:T(128)}, f32[]{:T(128)}) all-reduce(f32[]{:T(128)} %get-tuple-element.75, f32[]{:T(128)} %get-tuple-element.74), channel_id=1, replica_groups=mesh['grp'=2,'seq'=16,'fsdp'=8] {'seq'}, use_global_device_ids=true, to_apply=%region_12.14 | all-reduce | flops 2 | bytes 16 | tf_op jit(solution)/shard_map/psum | solution.py:147
  711.9 33.6 %reduce-scatter.16.cloned.1.call-done = bf16[384,128]{1,0:T(8,128)(2,1)} async-done(((bf16[3072,128]{1,0:T(8,128)(2,1)}), bf16[384,128]{1,0:T(8,128)(2,1)}) %reduce-scatter.16.cloned.1.call-update) | async-done | bytes 98320
  753.9 3.7 convolution_convert_fusion
  761.0 80.6 %reduce-scatter.18.cloned.1.call-done = bf16[128,384]{1,0:T(8,128)(2,1)} async-done(((bf16[2048,384]{1,0:T(8,128)(2,1)}), bf16[128,384]{1,0:T(8,128)(2,1)}) %reduce-scatter.18.cloned.1.call-update) | async-done | bytes 98320 | tf_op jit(solution)/shard_map/reduce_scatter | solution.py:177
  841.6 88.2 %reduce-scatter.20.cloned.1.call-done = bf16[128,384]{1,0:T(8,128)(2,1)} async-done(((bf16[2048,384]{1,0:T(8,128)(2,1)}), bf16[128,384]{1,0:T(8,128)(2,1)}) %reduce-scatter.20.cloned.1.call-update) | async-done | bytes 98320 | tf_op jit(solution)/shard_map/reduce_scatter | solution.py:183
  929.8 8.3 fusion.35
  939.8 41.0 %reduce-scatter.22.cloned.1.call-done = bf16[640,128]{1,0:T(8,128)(2,1)} async-done(((bf16[5120,128]{1,0:T(8,128)(2,1)}), bf16[640,128]{1,0:T(8,128)(2,1)}) %reduce-scatter.22.cloned.1.call-update) | async-done | bytes 163856
  983.7 4.2 fusion.104
  987.9 6.5 add_convert_fusion
  997.8 92.1 %reduce-scatter.14.cloned.1.call-done = bf16[192,640]{1,0:T(8,128)(2,1)} async-done(((bf16[3072,640]{1,0:T(8,128)(2,1)}), bf16[192,640]{1,0:T(8,128)(2,1)}) %reduce-scatter.14.cloned.1.call-update) | async-done | bytes 245776 | tf_op jit(solution)/shard_map/reduce_scatter | solution.py:207
  (111 shorter events, 63.6 us)
Async XLA Ops:
  7.2 425.2 %copy-start = (bf16[640,128]{1,0:T(8,128)(2,1)S(1)}, bf16[640,128]{1,0:T(8,128)(2,1)}, u32[]{:S(2)}) copy-start(bf16[640,128]{1,0:T(8,128)(2,1)} %param.24) | copy-start | bytes 491524
  7.2 156.2 %all-gather.16.cloned.1.call-start = ((), (), s32[]{:S(2)}) async-start(), calls=%async_computation.7 | async-start | bytes 12533760 | tf_op jit(solution)/shard_map/all_gather | solution.py:79
  7.9 216.8 %all-gather.18.cloned.1.call-start = ((), (), s32[]{:S(2)}) async-start(), calls=%async_computation.8 | async-start | bytes 1671168 | tf_op jit(solution)/shard_map/all_gather | solution.py:85
  8.6 154.7 %copy-start.13 = (f32[1,5120]{1,0:T(1,128)S(1)}, f32[1,5120]{1,0:T(1,128)}, u32[]{:S(2)}) copy-start(f32[1,5120]{1,0:T(1,128)} %param.23) | copy-start | bytes 61444
  11.7 157.9 %copy-start.6 = (bf16[128,5120]{1,0:T(8,128)(2,1)}, bf16[128,5120]{1,0:T(8,128)(2,1)S(1)}, u32[]{:S(2)}) copy-start(bf16[128,5120]{1,0:T(8,128)(2,1)S(1)} %get-tuple-element.81) | copy-start | bytes 3932164
  170.4 111.2 %all-gather.20.cloned.1.call-start = ((), (), s32[]{:S(2)}) async-start(), calls=%async_computation.9 | async-start | bytes 1671168 | tf_op jit(solution)/shard_map/all_gather | solution.py:86
  171.1 203.7 %all-gather.22.cloned.1.call-start = ((), (), s32[]{:S(2)}) async-start(), calls=%async_computation.10 | async-start | bytes 4177920 | tf_op jit(solution)/shard_map/all_gather | solution.py:80
  171.7 248.1 %all-gather.14.cloned.1.call-start = ((), (), s32[]{:S(2)}) async-start(), calls=%async_computation.5 | async-start | bytes 1474560 | tf_op jit(solution)/shard_map/all_gather | solution.py:123
  171.9 111.4 %copy-start.16 = (s32[3]{0:T(128)S(1)}, s32[3]{0:T(128)}, u32[]{:S(2)}) copy-start(s32[3]{0:T(128)} %param.18) | copy-start | bytes 40
  283.5 9.2 copy-start.10
  374.8 4.0 copy-start.4
  378.7 108.7 %all-gather.24.cloned.1.call-start = ((), (), s32[]{:S(2)}) async-start(), calls=%async_computation.11 | async-start | bytes 1671168 | tf_op jit(solution)/shard_map/all_gather | solution.py:127
  419.8 4.1 collective-permute-start
  424.2 8.1 copy-start.11
  431.3 112.3 %all-gather.26.cloned.1.call-start = ((), (), s32[]{:S(2)}) async-start(), calls=%async_computation.12 | async-start | bytes 1671168 | tf_op jit(solution)/shard_map/all_gather | solution.py:128
  432.1 224.6 %all-reduce.5.cloned.1.call-start = ((), (), s32[]{:S(2)}) async-start(), calls=%async_computation.17 | async-start | bytes 131072 | tf_op jit(solution)/shard_map/psum | solution.py:143
  545.3 3.1 copy-start.9
  579.4 4.0 copy-start.2
  579.4 4.1 copy-start.14
  583.4 162.1 %reduce-scatter.16.cloned.1.call-start = ((), (), s32[]{:S(2)}) async-start(), calls=%async_computation.13 | async-start | bytes 884736
  711.9 129.7 %reduce-scatter.18.cloned.1.call-start = ((), (), s32[]{:S(2)}) async-start(), calls=%async_computation.14 | async-start | bytes 1671168 | tf_op jit(solution)/shard_map/reduce_scatter | solution.py:177
  745.6 3.3 copy-start.1
  751.2 2.7 copy-start.15
  753.8 176.0 %reduce-scatter.20.cloned.1.call-start = ((), (), s32[]{:S(2)}) async-start(), calls=%async_computation.15 | async-start | bytes 1671168 | tf_op jit(solution)/shard_map/reduce_scatter | solution.py:183
  760.2 220.5 %reduce-scatter.22.cloned.1.call-start = ((), (), s32[]{:S(2)}) async-start(), calls=%async_computation.16 | async-start | bytes 1474560
  938.1 43.7 %copy-start.8 = (f32[128,640]{1,0:T(8,128)S(1)}, f32[128,640]{1,0:T(8,128)}, u32[]{:S(2)}) copy-start(f32[128,640]{1,0:T(8,128)} %copy-done.7) | copy-start | bytes 983044
  938.1 45.5 %copy-start.3 = (bf16[128,3072]{0,1:T(8,128)(2,1)S(1)}, bf16[128,3072]{0,1:T(8,128)(2,1)}, u32[]{:S(2)}) copy-start(bf16[128,3072]{0,1:T(8,128)(2,1)} %copy-done.2) | copy-start | bytes 2359300
  939.6 150.3 %reduce-scatter.14.cloned.1.call-start = ((), (), s32[]{:S(2)}) async-start(), calls=%async_computation.6 | async-start | bytes 4177920 | tf_op jit(solution)/shard_map/reduce_scatter | solution.py:207
  982.0 5.9 copy-start.5
  982.0 5.9 copy-start.12
  982.0 5.9 collective-permute-start.1
  994.8 3.0 collective-permute-start.2
  (1 other events, 0.7 us)
Sparse Core Ops, SparseCore 0:
  10.4 152.8 all-gather.15
  170.5 54.2 all-gather.17
  227.8 53.7 all-gather.19
  283.9 76.1 all-gather.21
  378.8 40.8 all-gather.13
  431.4 55.8 all-gather.23
  489.8 53.7 all-gather.25
  583.6 73.0 all-reduce.4
  712.0 33.5 reduce-scatter.15
  753.9 87.5 reduce-scatter.17
  845.1 84.6 reduce-scatter.19
  939.7 40.9 reduce-scatter.21
  994.6 95.2 reduce-scatter.13
where the time goes:
time: 1100 us
  waiting for transfers between devices  821 us (75%)
  blocking collectives  118 us (11%)
  matrix products  68.8 us (6%)
  local copies, waits for them, and re-layouts  48.8 us (4%)
  other arithmetic  18.6 us (2%)
  between operations  17.1 us (2%)
    all_gather x1, waiting for transfers between devices, local(): full_weights = lax.all_gather(local_weights, 'seq', axis=1, tiled=True)  152 us
    reduce_scatter x1, waiting for transfers between devices, local(): lax.psum_scatter((lead_term + tail_term).astype(jnp.bfloat16), 'seq', sca...  92.1 us
    reduce_scatter x1, waiting for transfers between devices, local(): lax.psum_scatter(value_part.reshape(key_count, heads_width).astype(jnp.bf...  88.2 us
    reduce_scatter x1, waiting for transfers between devices, local(): lax.psum_scatter(key_part.reshape(key_count, heads_width).astype(jnp.bflo...  80.6 us
    unnamed x15, waiting for transfers between devices  77.4 us
    psum x1, waiting for transfers between devices, local(): lax.psum(fake_units.astype(jnp.bfloat16), 'fsdp').astype(jnp.float32)  73.2 us
    all_gather x1, waiting for transfers between devices, local(): lax.all_gather(first_proj[2], 'seq', axis=0, tiled=True)  55.1 us
    all_gather x1, waiting for transfers between devices, local(): lax.all_gather(first_proj[1], 'seq', axis=0, tiled=True)  52.9 us
  transfers between devices with their start and end apart: 16, of which 14 were waited for; matrix products, arithmetic and copies ran while one was open for 7% of the time, Pallas kernels for 0%

commit v1 on v0

v1 whole, which is shorter than its diff:
```python
import jax
import jax.numpy as jnp
from jax import lax
from jax.experimental import pallas as pl
from jax.experimental.pallas import tpu as pltpu
from jax.sharding import PartitionSpec as P

HD = 128
EPS = 1e-06
NEG = -1e30
AXES = ("grp", "seq", "fsdp")
VMEM = pltpu.CompilerParams(vmem_limit_bytes=50 * 2**20)
F32, BF16 = jnp.float32, jnp.bfloat16


def moved(value, step, groups=(0, 1), cross=False):
    dy, dz, dx, dw = step
    pairs = []
    for g in groups:
        for y in range(4):
            for z in range(4):
                for x in range(4):
                    for w in range(2):
                        there = 1 - g if cross else g
                        source = g * 128 + (4 * y + z) * 8 + 2 * x + w
                        target = (
                            there * 128
                            + (4 * ((y + dy) % 4) + (z + dz) % 4) * 8
                            + 2 * ((x + dx) % 4)
                            + (w + dw) % 2
                        )
                        pairs.append((source, target))
    return lax.ppermute(value, AXES, pairs)


def along(axis, k):
    step = [0, 0, 0, 0]
    step[axis] = k
    return tuple(step)


def ring4(value, axis, groups):
    one = moved(value, along(axis, 1), groups)
    three = moved(value, along(axis, -1), groups)
    cut = value.ndim - 2
    half = value.shape[cut] // 2
    low = lax.slice_in_dim(one, 0, half, axis=cut)
    high = lax.slice_in_dim(three, half, 2 * half, axis=cut)
    low = moved(low, along(axis, 1), groups)
    high = moved(high, along(axis, -1), groups)
    return jnp.stack([value, one, jnp.concatenate([low, high], axis=cut), three])


def direct4(value, axis, groups):
    return jnp.stack([value] + [moved(value, along(axis, k), groups) for k in (1, 2, 3)])


def gather_seq(value, groups, step=ring4):
    return step(step(value, 1, groups), 0, groups).reshape((4, 4) + value.shape)


def gather_fsdp(value, groups):
    pair = jnp.stack([value, moved(value, along(3, 1), groups)])
    return direct4(pair, 2, groups)


def swap_seq(blocks, groups):
    rows = [blocks[0]] + [moved(blocks[k], along(0, k), groups) for k in (1, 2, 3)]
    rows = jnp.stack(rows)
    cols = [rows[:, 0]] + [moved(rows[:, k], along(1, k), groups) for k in (1, 2, 3)]
    return jnp.stack(cols, axis=1)


def scatter_fsdp(blocks, groups):
    total = blocks[0].astype(F32)
    for k in (2, 1, 3):
        total = total + moved(blocks[k], along(2, k), groups).astype(F32)
    return total[0] + moved(total[1], along(3, 1), groups)


def ordered(relative, x, w):
    backward = jnp.stack([relative[k] for k in (0, 3, 2, 1)])
    return jnp.roll(backward, (x, w), (0, 1))


def mm(a, b, ca, cb):
    return lax.dot_general(a, b, (((ca,), (cb,)), ((), ())), preferred_element_type=F32)


def generator_kernel(frames, mask, q, k0, k1, k2, v0, v1, v2, own_k, own_v, out):
    scale = HD ** (-0.5)
    query = q[...]
    parts = [mm(query, k[0], 1, 1) * scale for k in (k0, k1, k2)]
    own = mm(query, own_k[...], 1, 1) * scale
    parts.append(jnp.where(mask[0:1, :] > 0.5, own, NEG))
    top = parts[0].max(axis=-1, keepdims=True)
    for part in parts[1:]:
        top = jnp.maximum(top, part.max(axis=-1, keepdims=True))
    parts = [jnp.exp(part - top) for part in parts]
    total = sum(part.sum(axis=-1, keepdims=True) for part in parts)
    inverse = 1.0 / total
    values = [v0[0], v1[0], v2[0], own_v[...]]
    result = jnp.zeros(out.shape, F32)
    for part, value in zip(parts, values):
        result = result + mm((part * inverse).astype(BF16), value, 1, 0)
    out[...] = result.astype(BF16)


def generator_attention(frames, mask, query, cache_keys, cache_values, key_value):
    rows, width = query.shape
    heads = width // HD
    count, length = key_value.shape[0], cache_keys.shape[1]

    def picked(i):
        return pl.BlockSpec((1, length, HD), lambda h, f: (f[i], 0, h))

    return pl.pallas_call(
        generator_kernel,
        grid_spec=pltpu.PrefetchScalarGridSpec(
            num_scalar_prefetch=1,
            grid=(heads,),
            in_specs=[
                pl.BlockSpec(mask.shape, lambda h, f: (0, 0)),
                pl.BlockSpec((rows, HD), lambda h, f: (0, h)),
                picked(0),
                picked(1),
                picked(2),
                picked(0),
                picked(1),
                picked(2),
                pl.BlockSpec((count, HD), lambda h, f: (0, h)),
                pl.BlockSpec((count, HD), lambda h, f: (0, heads + h)),
            ],
            out_specs=pl.BlockSpec((rows, HD), lambda h, f: (0, h)),
        ),
        out_shape=jax.ShapeDtypeStruct((rows, width), BF16),
        compiler_params=VMEM,
    )(
        frames, mask, query,
        cache_keys, cache_keys, cache_keys,
        cache_values, cache_values, cache_values,
        key_value, key_value,
    )


def critic_kernel(q, k, v, out, lse):
    scores = mm(q[...], k[...], 1, 1) * HD ** (-0.5)
    top = scores.max(axis=-1, keepdims=True)
    raised = jnp.exp(scores - top)
    total = raised.sum(axis=-1, keepdims=True)
    out[...] = mm((raised * (1.0 / total)).astype(BF16), v[...], 1, 0).astype(BF16)
    lse[...] = jnp.broadcast_to(top + jnp.log(total), lse.shape)


def critic_attention(query, key_value):
    rows, width = query.shape
    heads, count = width // HD, key_value.shape[0]
    own = pl.BlockSpec((rows, HD), lambda h: (0, h))
    return pl.pallas_call(
        critic_kernel,
        grid=(heads,),
        in_specs=[
            own,
            pl.BlockSpec((count, HD), lambda h: (0, h)),
            pl.BlockSpec((count, HD), lambda h: (0, heads + h)),
        ],
        out_specs=(own, own),
        out_shape=(
            jax.ShapeDtypeStruct((rows, width), BF16),
            jax.ShapeDtypeStruct((rows, width), F32),
        ),
        compiler_params=VMEM,
    )(query, key_value, key_value)


def query_kernel(q, kv, lse, u, high, low, score, grad, sent):
    scale = HD ** (-0.5)
    width = q.shape[1]
    unit = u[...]
    stats = []
    for start in range(0, width, HD):
        here = slice(start, start + HD)
        keys = kv[:, here]
        head_grad = (mm(unit, high[here, :], 1, 1) + mm(unit, low[here, :], 1, 1)).astype(BF16)
        logs = lse[:, start : start + 1]
        weights = jnp.exp(mm(q[:, here], keys, 1, 1) * scale - logs)
        slopes = mm(head_grad, kv[:, width + start : width + start + HD], 1, 1)
        centred = jnp.sum(slopes * weights, axis=-1, keepdims=True)
        score_grad = (weights * (slopes - centred)).astype(BF16)
        grad[:, here] = (mm(score_grad, keys, 1, 0) * scale).astype(BF16)
        stats += [centred, logs]
    stats.append(score[...])
    lane = lax.broadcasted_iota(jnp.int32, (q.shape[0], HD), 1)
    table = jnp.zeros((q.shape[0], HD), F32)
    for i, stat in enumerate(stats):
        for j in range(3):
            term = stat.astype(BF16).astype(F32)
            table = jnp.where(lane == 3 * i + j, term, table)
            stat = stat - term
    sent[:, :HD] = unit
    sent[:, HD:] = table.astype(BF16)


def query_grads(query, key_value, lse, unit, high, low, score):
    rows, width = query.shape
    return pl.pallas_call(
        query_kernel,
        out_shape=(
            jax.ShapeDtypeStruct((rows, width), BF16),
            jax.ShapeDtypeStruct((rows, 2 * HD), BF16),
        ),
        compiler_params=VMEM,
    )(query, key_value, lse, unit, high, low, score)


def key_kernel(k, v, q, sent, high, low, key_grad, value_grad):
    scale = HD ** (-0.5)
    width = k.shape[1]
    unit = sent[:, :HD]
    table = sent[:, HD:].astype(F32)

    def stat(i):
        return table[:, 3 * i : 3 * i + 1] + table[:, 3 * i + 1 : 3 * i + 2] + table[:, 3 * i + 2 : 3 * i + 3]

    for head, start in enumerate(range(0, width, HD)):
        here = slice(start, start + HD)
        queries = q[:, here]
        head_grad = (mm(unit, high[here, :], 1, 1) + mm(unit, low[here, :], 1, 1)).astype(BF16)
        weights = jnp.exp(mm(queries, k[:, here], 1, 1) * scale - stat(2 * head + 1))
        slopes = mm(head_grad, v[:, here], 1, 1)
        score_grad = (weights * (slopes - stat(2 * head))).astype(BF16)
        key_grad[:, here] = (mm(score_grad, queries, 0, 0) * scale).astype(BF16)
        value_grad[:, here] = mm(weights.astype(BF16), head_grad, 0, 0).astype(BF16)


def key_grads(keys, values, queries, sent, high, low):
    shape = jax.ShapeDtypeStruct(keys.shape, BF16)
    return pl.pallas_call(key_kernel, out_shape=(shape, shape), compiler_params=VMEM)(
        keys, values, queries, sent, high, low
    )


def split(value):
    high = lax.reduce_precision(value, 8, 7)
    return high.astype(BF16), (value - high).astype(BF16)


def project(row_block, gain_vector, weight_set):
    lifted = row_block.astype(F32)
    inverse = lax.rsqrt(jnp.mean(lifted * lifted, axis=-1, keepdims=True) + EPS)
    normed = (lifted * inverse * gain_vector).astype(BF16)
    parts = [jnp.dot(normed, weight_set[c], preferred_element_type=F32) for c in range(3)]
    return [part.astype(BF16) for part in parts], inverse


def unit_terms(units, head_out):
    active, back = jax.vjp(jax.nn.gelu, units)
    score = jnp.sum(active * head_out, axis=-1, keepdims=True)
    return score, back(jnp.broadcast_to(head_out, units.shape))[0].astype(BF16)


def pick_rows(real_bank, real_pick):
    chosen = jnp.zeros(real_bank.shape[1:], real_bank.dtype)
    for entry in range(real_bank.shape[0]):
        chosen = jnp.where((real_pick == entry)[:, None], real_bank[entry], chosen)
    return chosen


GEN, CRIT = (0,), (1,)


def local(
    new_rows, cache_keys, cache_values, cache_frames, real_bank, real_pick,
    attn_weights, out_weights, norm_gains, head_in, head_out,
):
    is_gen = lax.axis_index("grp") == 0
    seq_at, fsdp_at = lax.axis_index("seq"), lax.axis_index("fsdp")
    y, z, x, w = seq_at // 4, seq_at % 4, fsdp_at // 2, fsdp_at % 2
    rows, model = new_rows.shape
    cols = out_weights.shape[2]
    width = attn_weights.shape[3]
    tokens = rows * 16
    gains = norm_gains[0]
    start = fsdp_at * cols

    weights = lax.all_gather(attn_weights[0], "seq", axis=1, tiled=True)
    full_out = lax.all_gather(out_weights[0], "seq", axis=0, tiled=True)

    real_rows = pick_rows(real_bank, real_pick)
    first_rows = jnp.where(is_gen, new_rows, real_rows)
    (first_q, first_k, first_v), _ = project(first_rows, gains, weights)
    first_kv = gather_seq(jnp.concatenate([first_k, first_v], axis=1), (0, 1))
    first_kv = first_kv.reshape(tokens, 2 * width)
    key_y = (y - jnp.arange(tokens) // (4 * rows)) % 4
    mask = jnp.broadcast_to((key_y // 2 <= y // 2).astype(F32)[None], (8, tokens))
    first_heads = lax.cond(
        is_gen,
        lambda a: generator_attention(*a),
        lambda a: critic_attention(a[2], a[5])[0],
        (cache_frames, mask, first_q, cache_keys, cache_values, first_kv),
    )

    gathered = ordered(gather_fsdp(first_heads, GEN), x, w).reshape(8, rows, width)
    first_all = gathered.transpose(1, 0, 2).reshape(rows, 8 * width)
    first_cols = lax.dynamic_slice_in_dim(first_rows, start, cols, 1).astype(F32)
    generated = (first_cols + jnp.dot(first_all, full_out, preferred_element_type=F32)).astype(BF16)
    pair = jnp.stack([generated, moved(generated, along(3, 1), GEN)])
    crossed = jnp.stack([moved(pair, along(2, k), GEN, cross=True) for k in range(4)])
    crossed = ordered(crossed, x, w).reshape(8, rows, cols)
    second_rows = crossed.transpose(1, 0, 2).reshape(rows, model)

    to_seq = first_all.reshape(rows, 4, 4, 192).transpose(1, 2, 0, 3)
    gen_heads = swap_seq(jnp.roll(to_seq, (-y, -z), (0, 1)), GEN).reshape(tokens, 192)

    joint = jnp.dot(full_out, head_in, preferred_element_type=F32).reshape(4, 2, width, -1)
    joint = scatter_fsdp(jnp.roll(joint, (-x, -w), (0, 1)), CRIT)
    high, low = split(joint)

    def units_of(row_cols, heads):
        part = jnp.dot(row_cols, head_in, preferred_element_type=F32)
        part = part + jnp.dot(heads, high, preferred_element_type=F32)
        part = part + jnp.dot(heads, low, preferred_element_type=F32)
        return jnp.sum(gather_fsdp(part, CRIT), axis=(0, 1))

    real_cols = lax.dynamic_slice_in_dim(first_rows, start, cols, 1)
    real_score, real_unit = unit_terms(units_of(real_cols, first_heads), head_out)

    (second_q, second_k, second_v), inverse = project(second_rows, gains, weights)
    every = gather_seq(jnp.concatenate([second_k, second_v, second_q], axis=1), CRIT)
    every = every.reshape(tokens, 3 * width)
    second_heads, lse = critic_attention(second_q, every)
    second_cols = lax.dynamic_slice_in_dim(second_rows, start, cols, 1)
    fake_score, fake_unit = unit_terms(units_of(second_cols, second_heads), head_out)
    query_grad, sent = query_grads(
        second_q, every, lse, fake_unit, high, low, real_score - fake_score
    )
    sent = gather_seq(sent, CRIT, direct4).reshape(tokens, 2 * HD)
    key_grad, value_grad = key_grads(
        second_k, second_v, every[:, 2 * width :], sent, high, low
    )
    row_terms = sum(
        mm(grad, weights[c], 1, 1) for c, grad in enumerate((query_grad, key_grad, value_grad))
    ).astype(BF16)
    blocks = row_terms.reshape(rows, 4, 2, cols).transpose(1, 2, 0, 3)
    row_grad = scatter_fsdp(jnp.roll(blocks, (-x, -w), (0, 1)), CRIT)
    gain_cols = lax.dynamic_slice_in_dim(gains, start, cols, 0)
    direction = mm(fake_unit, head_in, 1, 1)
    input_grad = (inverse * row_grad * gain_cols + direction).astype(BF16)

    four = ring4(input_grad, 1, CRIT)
    back = jnp.stack([moved(four, along(0, k), CRIT, cross=True) for k in range(4)])
    back = back.reshape(tokens, cols)
    term_gen = mm(gen_heads, back, 0, 0)

    product = mm(second_heads, fake_unit, 0, 0) - mm(first_heads, real_unit, 0, 0)
    product = ordered(gather_fsdp(product.astype(BF16), CRIT), x, w).reshape(4, 4, 192, -1)
    product = swap_seq(jnp.roll(product, (-y, -z), (0, 1)), CRIT)
    product_high, product_low = split(jnp.sum(product.astype(F32), axis=(0, 1)))
    term_crit = mm(product_high, head_in, 1, 1) + mm(product_low, head_in, 1, 1)

    stats = sent[:, HD:].astype(F32)
    margin = jnp.sum(stats[:, 18:21]) / tokens
    margin_back = moved(jnp.broadcast_to(margin, (8, HD)), (0, 0, 0, 0), CRIT, cross=True)[0, 0]
    margin = jnp.where(is_gen, margin_back, margin)
    signed = jnp.where(is_gen, margin, -margin)
    factor = jnp.where(is_gen, -1.0, 1.0) * jax.nn.sigmoid(signed)
    grads = (jnp.where(is_gen, term_gen, term_crit) * factor).astype(BF16)
    losses = jax.nn.softplus(signed).astype(BF16)
    return (grads[None], losses[None])


def solution(mesh):
    placed = (
        P("seq", None),
        P(None, None, "fsdp"),
        P(None, None, "fsdp"),
        P(),
        P(None, "seq", None),
        P("seq"),
        P("grp", None, "seq", "fsdp"),
        P("grp", "seq", "fsdp"),
        P("grp", None),
        P("fsdp", None),
        P(),
    )
    return jax.shard_map(
        local,
        mesh=mesh,
        in_specs=placed,
        out_specs=(P("grp", "seq", "fsdp"), P("grp")),
        check_vma=False,
    )
```

time: 1100 us -> 585 us (0.53)
  the two profiles are of different devices: /device:TPU:32 before, /device:TPU:6 now
where the time goes in v1:
time: 585 us; the launch traced here: 574 us
  waiting for transfers between devices  327 us (56%)
  starting transfers between devices  116 us (20%)
  matrix products  40.5 us (7%)
  other arithmetic  30.3 us (5%)
  local copies, waits for them, and re-layouts  22.3 us (4%)
  Pallas kernels  19.4 us (3%)
  between operations  18.8 us (3%)
    ppermute x72, waiting for transfers between devices, moved(): return lax.ppermute(value, AXES, pairs)  181 us
    all_gather x1, waiting for transfers between devices, local(): weights = lax.all_gather(attn_weights[0], 'seq', axis=1, tiled=True)  144 us
    ppermute x72, starting transfers between devices, moved(): return lax.ppermute(value, AXES, pairs)  116 us
    dot_general x6, matrix products, project(): jnp.dot(normed, weight_set[c], preferred_element_type=F32)  18.5 us
    dot_general x9, matrix products, mm(): lax.dot_general(a, b, (((ca,), (cb,)), ((), ())), preferred_element_type=...  14.6 us
  transfers between devices with their start and end apart: 74, of which 16 were waited for; matrix products, arithmetic and copies ran while one was open for 12% of the time, Pallas kernels for 2%

profile of v1, /device:TPU:6, one launch (start us, length us, event | category | flops | bytes accessed | tf_op | source)
XLA Modules:
  0.0 574.3 jit_solution(16865793497224907011)
XLA Ops:
  12.5 144.0 %all-gather.5.cloned.1.call-done = bf16[1,3,5120,384]{3,2,1,0:T(8,128)(2,1)} async-done(((bf16[1,3,320,384]{3,2,1,0:T(8,128)(2,1)}), bf16[1,3,5120,384]{3,2,1,0:T(8,128)(2,1)}) %all-gather.5.cloned.1.call-update) | async-done | bytes 11796496 | tf_op jit(solution)/shard_map/all_gather | solution.py:286
  164.4 9.2 %collective-permute-start.2 = (bf16[128,768]{1,0:T(8,128)(2,1)S(1)}, bf16[128,768]{1,0:T(8,128)(2,1)S(1)}, u32[]{:S(2)}, u32[]{:S(2)}) collective-permute-start(bf16[128,768]{1,0:T(8,128)(2,1)S(1)} %get-tuple-element.89), channel_id=1, source_target_pairs={{0,24},{1,25},{2,26},{3,27},{4,28},{5,29},{6,30},{7,31},{8,0},{9,1... | collective-permute-start | bytes 589832 | tf_op jit(solution)/shard_map/ppermute | solution.py:33
  173.6 9.1 %collective-permute-done = bf16[128,768]{1,0:T(8,128)(2,1)S(1)} collective-permute-done((bf16[128,768]{1,0:T(8,128)(2,1)S(1)}, bf16[128,768]{1,0:T(8,128)(2,1)S(1)}, u32[]{:S(2)}, u32[]{:S(2)}) %collective-permute-start) | collective-permute-done | bytes 196640 | tf_op jit(solution)/shard_map/ppermute | solution.py:33
  185.1 4.7 collective-permute-start.3
  189.8 5.4 collective-permute-done.1
  200.8 25.7 %collective-permute-done.4 = bf16[4,128,768]{2,1,0:T(8,128)(2,1)S(1)} collective-permute-done((bf16[4,128,768]{2,1,0:T(8,128)(2,1)}, bf16[4,128,768]{2,1,0:T(8,128)(2,1)S(1)}, u32[]{:S(2)}, u32[]{:S(2)}) %collective-permute-start.4) | collective-permute-done | bytes 786464 | tf_op jit(solution)/shard_map/ppermute | solution.py:33
  229.9 3.3 collective-permute-start.7
  236.2 5.5 collective-permute-done.5
  245.1 7.3 %conditional.1 = (bf16[128,384]{1,0:T(8,128)(2,1)S(1)}) conditional(s32[]{:T(128)} %convert_element_type.107, (bf16[128,384]{1,0:T(8,128)(2,1)S(1)}, bf16[2048,768]{1,0:T(8,128)(2,1)S(1)}) %tuple.51, (s32[3]{0:T(128)S(1)}, f32[2048]{0:T(1024)S(1)}, bf16[128,384]{1,0:T(8,128)(2,1)S(1)}, bf16[4,1024,384]{2,1,0:T(8,128)(2,1)S(1)}, ...), branch_computations={%region_1.2_spmd, %region_2.3_spmd} | conditional | bytes 73736 | solution.py:296
  245.3 7.1 %branch_1_fun.1 = bf16[128,384]{1,0:T(8,128)(2,1)S(1)} custom-call(s32[3]{0:T(128)S(1)} %get-tuple-element.47.frames, f32[8,2048]{1,0:T(8,128)S(1)} %broadcast_in_dim.78.mask, bf16[128,384]{1,0:T(8,128)(2,1)S(1)} %get-tuple-element.25.q, bf16[4,1024,384]{2,1,0:T(8,128)(2,1)S(1)} %get-tuple-element.48.k0.k1.k2, ...), custom_call_target="tpu_custom_call" | custom-call | tf_op jit(solution)/shard_map/cond/branch_1_fun/pallas_call | solution.py:117
  255.0 4.0 collective-permute-done.8
  263.0 3.9 collective-permute-start.10
  266.9 4.2 collective-permute-start.11
  272.6 4.9 collective-permute-done.11
  285.2 3.8 collective-permute-done.18
  307.9 3.5 fusion.66.q
  341.0 4.7 collective-permute-start.13
  348.9 3.9 collective-permute-start.14
  356.9 3.7 pad_maximum_fusion
  360.6 4.3 shard_map.125
  375.9 4.6 shard_map.126
  383.6 3.5 fusion.5
  391.8 3.3 shard_map.127
  395.1 3.5 convolution_add_fusion.1
  398.6 3.5 fusion
  425.8 96.9 %collective-permute-done.71 = f32[8,128]{1,0:T(8,128)S(1)} collective-permute-done((f32[8,128]{1,0:T(8,128)S(1)}, f32[8,128]{1,0:T(8,128)S(1)}, u32[]{:S(2)}, u32[]{:S(2)}) %collective-permute-start.71) | collective-permute-done | bytes 4128 | tf_op jit(solution)/shard_map/ppermute | solution.py:33
  529.4 5.5 collective-permute-start.16
  535.1 9.5 %collective-permute-done.16 = bf16[4,128,192]{1,2,0:T(8,128)(2,1)S(1)} collective-permute-done((bf16[4,128,192]{1,2,0:T(8,128)(2,1)S(1)}, bf16[4,128,192]{1,2,0:T(8,128)(2,1)S(1)}, u32[]{:S(2)}, u32[]{:S(2)}) %collective-permute-start.16) | collective-permute-done | bytes 196640 | tf_op jit(solution)/shard_map/ppermute | solution.py:33
  544.6 5.5 collective-permute-start.15
  550.3 4.8 collective-permute-done.15
  556.0 6.9 %collective-permute-done.58 = bf16[4,128,640]{2,1,0:T(8,128)(2,1)} collective-permute-done((bf16[4,128,640]{2,1,0:T(8,128)(2,1)S(1)}, bf16[4,128,640]{2,1,0:T(8,128)(2,1)}, u32[]{:S(2)}, u32[]{:S(2)}) %collective-permute-start.58) | collective-permute-done | bytes 655392 | tf_op jit(solution)/shard_map/ppermute | solution.py:33
  563.0 3.2 fusion.58
  (285 shorter events, 149.9 us)
Async XLA Ops:
  7.2 149.3 %all-gather.5.cloned.1.call-start = ((), (), s32[]{:S(2)}) async-start(), calls=%async_computation | async-start | bytes 12533760 | tf_op jit(solution)/shard_map/all_gather | solution.py:286
  7.9 270.7 %all-gather.7.cloned.1.call-start = ((), (), s32[]{:S(2)}) async-start(), calls=%async_computation.1 | async-start | bytes 4177920 | tf_op jit(solution)/shard_map/all_gather | solution.py:287
  162.5 20.2 %collective-permute-start = (bf16[128,768]{1,0:T(8,128)(2,1)S(1)}, bf16[128,768]{1,0:T(8,128)(2,1)S(1)}, u32[]{:S(2)}, u32[]{:S(2)}) collective-permute-start(bf16[128,768]{1,0:T(8,128)(2,1)S(1)} %get-tuple-element.89), channel_id=1, source_target_pairs={{0,8},{1,9},{2,10},{3,11},{4,12},{5,13},{6,14},{7,15},{8,16},{9,17... | collective-permute-start | bytes 589832 | tf_op jit(solution)/shard_map/ppermute | solution.py:33
  164.4 20.7 %collective-permute-start.2 = (bf16[128,768]{1,0:T(8,128)(2,1)S(1)}, bf16[128,768]{1,0:T(8,128)(2,1)S(1)}, u32[]{:S(2)}, u32[]{:S(2)}) collective-permute-start(bf16[128,768]{1,0:T(8,128)(2,1)S(1)} %get-tuple-element.89), channel_id=1, source_target_pairs={{0,24},{1,25},{2,26},{3,27},{4,28},{5,29},{6,30},{7,31},{8,0},{9,1... | collective-permute-start | bytes 589832 | tf_op jit(solution)/shard_map/ppermute | solution.py:33
  182.7 12.5 %collective-permute-start.1 = (bf16[64,768]{1,0:T(8,128)(2,1)S(1)}, bf16[64,768]{1,0:T(8,128)(2,1)S(1)}, u32[]{:S(2)}, u32[]{:S(2)}) collective-permute-start(bf16[64,768]{1,0:T(8,128)(2,1)S(1)} %slice.202), channel_id=1, source_target_pairs={{0,8},{1,9},{2,10},{3,11},{4,12},{5,13},{6,14},{7,15},{8,16},{9,17... | collective-permute-start | bytes 294920 | tf_op jit(solution)/shard_map/ppermute | solution.py:33
  185.1 10.2 %collective-permute-start.3 = (bf16[64,768]{1,0:T(8,128)(2,1)S(1)}, bf16[64,768]{1,0:T(8,128)(2,1)S(1)}, u32[]{:S(2)}, u32[]{:S(2)}) collective-permute-start(bf16[64,768]{1,0:T(8,128)(2,1)S(1)} %slice.203), channel_id=1, source_target_pairs={{0,24},{1,25},{2,26},{3,27},{4,28},{5,29},{6,30},{7,31},{8,0},{9,1... | collective-permute-start | bytes 294920 | tf_op jit(solution)/shard_map/ppermute | solution.py:33
  196.3 30.2 %collective-permute-start.4 = (bf16[4,128,768]{2,1,0:T(8,128)(2,1)}, bf16[4,128,768]{2,1,0:T(8,128)(2,1)S(1)}, u32[]{:S(2)}, u32[]{:S(2)}) collective-permute-start(bf16[4,128,768]{2,1,0:T(8,128)(2,1)} %get-tuple-element.81), channel_id=1, source_target_pairs={{0,32},{1,33},{2,34},{3,35},{4,36},{5,37},{6,38},{7,39},{8,40},{9,... | collective-permute-start | bytes 2359304 | tf_op jit(solution)/shard_map/ppermute | solution.py:33
  199.3 29.5 %collective-permute-start.6 = (bf16[4,128,768]{2,1,0:T(8,128)(2,1)}, bf16[4,128,768]{2,1,0:T(8,128)(2,1)}, u32[]{:S(2)}, u32[]{:S(2)}) collective-permute-start(bf16[4,128,768]{2,1,0:T(8,128)(2,1)} %get-tuple-element.81), channel_id=1, source_target_pairs={{0,96},{1,97},{2,98},{3,99},{4,100},{5,101},{6,102},{7,103},{8,104... | collective-permute-start | bytes 2359304 | tf_op jit(solution)/shard_map/ppermute | solution.py:33
  226.5 15.2 %collective-permute-start.5 = (bf16[4,64,768]{2,1,0:T(8,128)(2,1)S(1)}, bf16[4,64,768]{2,1,0:T(8,128)(2,1)S(1)}, u32[]{:S(2)}, u32[]{:S(2)}) collective-permute-start(bf16[4,64,768]{2,1,0:T(8,128)(2,1)S(1)} %slice.204), channel_id=1, source_target_pairs={{0,32},{1,33},{2,34},{3,35},{4,36},{5,37},{6,38},{7,39},{8,40},{9,... | collective-permute-start | bytes 1179656 | tf_op jit(solution)/shard_map/ppermute | solution.py:33
  229.9 12.1 %collective-permute-start.7 = (bf16[4,64,768]{2,1,0:T(8,128)(2,1)S(1)}, bf16[4,64,768]{2,1,0:T(8,128)(2,1)S(1)}, u32[]{:S(2)}, u32[]{:S(2)}) collective-permute-start(bf16[4,64,768]{2,1,0:T(8,128)(2,1)S(1)} %slice.205), channel_id=1, source_target_pairs={{0,96},{1,97},{2,98},{3,99},{4,100},{5,101},{6,102},{7,103},{8,104... | collective-permute-start | bytes 1179656 | tf_op jit(solution)/shard_map/ppermute | solution.py:33
  259.0 12.2 %collective-permute-start.9 = (bf16[2,128,384]{2,1,0:T(8,128)(2,1)S(1)}, bf16[2,128,384]{2,1,0:T(8,128)(2,1)S(1)}, u32[]{:S(2)}, u32[]{:S(2)}) collective-permute-start(bf16[2,128,384]{2,1,0:T(8,128)(2,1)S(1)} %pad_maximum_fusion.12), channel_id=1, source_target_pairs={{0,6},{1,7},{2,0},{3,1},{4,2},{5,3},{6,4},{7,5},{8,14},{9,15},{10,... | collective-permute-start | bytes 589832 | tf_op jit(solution)/shard_map/ppermute | solution.py:33
  266.9 10.6 %collective-permute-start.11 = (bf16[2,128,384]{2,1,0:T(8,128)(2,1)S(1)}, bf16[2,128,384]{2,1,0:T(8,128)(2,1)S(1)}, u32[]{:S(2)}, u32[]{:S(2)}) collective-permute-start(bf16[2,128,384]{2,1,0:T(8,128)(2,1)S(1)} %pad_maximum_fusion.12), channel_id=1, source_target_pairs={{0,2},{1,3},{2,4},{3,5},{4,6},{5,7},{6,0},{7,1},{8,10},{9,11},{10,... | collective-permute-start | bytes 589832 | tf_op jit(solution)/shard_map/ppermute | solution.py:33
  291.6 9.7 %collective-permute-start.20 = (bf16[2,128,640]{2,1,0:T(8,128)(2,1)S(1)}, bf16[2,128,640]{2,1,0:T(8,128)(2,1)S(1)}, u32[]{:S(2)}, u32[]{:S(2)}) collective-permute-start(bf16[2,128,640]{2,1,0:T(8,128)(2,1)S(1)} %pad_maximum_fusion.8), channel_id=1, source_target_pairs={{0,134},{1,135},{2,128},{3,129},{4,130},{5,131},{6,132},{7,133},{8... | collective-permute-start | bytes 983048 | tf_op jit(solution)/shard_map/ppermute | solution.py:33
  296.7 23.3 %collective-permute-start.31 = (f32[2,384,128]{2,1,0:T(8,128)}, f32[2,384,128]{2,1,0:T(8,128)}, u32[]{:S(2)}, u32[]{:S(2)}) collective-permute-start(f32[2,384,128]{2,1,0:T(8,128)} %get-tuple-element.56), channel_id=1, source_target_pairs={{128,132},{129,133},{130,134},{131,135},{132,128},{133,129},{134,1... | collective-permute-start | bytes 1179656 | tf_op jit(solution)/shard_map/ppermute | solution.py:33
  298.1 21.9 %collective-permute-start.32 = (f32[2,384,128]{2,1,0:T(8,128)}, f32[2,384,128]{2,1,0:T(8,128)}, u32[]{:S(2)}, u32[]{:S(2)}) collective-permute-start(f32[2,384,128]{2,1,0:T(8,128)} %get-tuple-element.57), channel_id=1, source_target_pairs={{128,130},{129,131},{130,132},{131,133},{132,134},{133,135},{134,1... | collective-permute-start | bytes 1179656 | tf_op jit(solution)/shard_map/ppermute | solution.py:33
  299.5 20.5 %collective-permute-start.33 = (f32[2,384,128]{2,1,0:T(8,128)S(1)}, f32[2,384,128]{2,1,0:T(8,128)}, u32[]{:S(2)}, u32[]{:S(2)}) collective-permute-start(f32[2,384,128]{2,1,0:T(8,128)S(1)} %get-tuple-element.58), channel_id=1, source_target_pairs={{128,134},{129,135},{130,128},{131,129},{132,130},{133,131},{134,1... | collective-permute-start | bytes 1179656 | tf_op jit(solution)/shard_map/ppermute | solution.py:33
  335.0 20.5 %collective-permute-start.28 = (bf16[4,64,1152]{2,1,0:T(8,128)(2,1)}, bf16[4,64,1152]{2,1,0:T(8,128)(2,1)}, u32[]{:S(2)}, u32[]{:S(2)}) collective-permute-start(bf16[4,64,1152]{2,1,0:T(8,128)(2,1)} %slice.216), channel_id=1, source_target_pairs={{128,160},{129,161},{130,162},{131,163},{132,164},{133,165},{134,1... | collective-permute-start | bytes 1769480 | tf_op jit(solution)/shard_map/ppermute | solution.py:33
  338.4 17.1 %collective-permute-start.30 = (bf16[4,64,1152]{2,1,0:T(8,128)(2,1)}, bf16[4,64,1152]{2,1,0:T(8,128)(2,1)}, u32[]{:S(2)}, u32[]{:S(2)}) collective-permute-start(bf16[4,64,1152]{2,1,0:T(8,128)(2,1)} %slice.217), channel_id=1, source_target_pairs={{128,224},{129,225},{130,226},{131,227},{132,228},{133,229},{134,2... | collective-permute-start | bytes 1769480 | tf_op jit(solution)/shard_map/ppermute | solution.py:33
  341.0 24.8 %collective-permute-start.13 = (bf16[4,128,192]{1,2,0:T(8,128)(2,1)}, bf16[4,128,192]{1,2,0:T(8,128)(2,1)S(1)}, u32[]{:S(2)}, u32[]{:S(2)}) collective-permute-start(bf16[4,128,192]{1,2,0:T(8,128)(2,1)} %get-tuple-element.69), channel_id=1, source_target_pairs={{0,64},{1,65},{2,66},{3,67},{4,68},{5,69},{6,70},{7,71},{8,72},{9,... | collective-permute-start | bytes 589832 | tf_op jit(solution)/shard_map/ppermute | solution.py:33
  345.7 20.2 %collective-permute-start.12 = (bf16[4,128,192]{1,2,0:T(8,128)(2,1)}, bf16[4,128,192]{1,2,0:T(8,128)(2,1)}, u32[]{:S(2)}, u32[]{:S(2)}) collective-permute-start(bf16[4,128,192]{1,2,0:T(8,128)(2,1)} %get-tuple-element.70), channel_id=1, source_target_pairs={{0,32},{1,33},{2,34},{3,35},{4,36},{5,37},{6,38},{7,39},{8,40},{9,... | collective-permute-start | bytes 589832 | tf_op jit(solution)/shard_map/ppermute | solution.py:33
  348.9 17.0 %collective-permute-start.14 = (bf16[4,128,192]{1,2,0:T(8,128)(2,1)}, bf16[4,128,192]{1,2,0:T(8,128)(2,1)}, u32[]{:S(2)}, u32[]{:S(2)}) collective-permute-start(bf16[4,128,192]{1,2,0:T(8,128)(2,1)} %get-tuple-element.71), channel_id=1, source_target_pairs={{0,96},{1,97},{2,98},{3,99},{4,100},{5,101},{6,102},{7,103},{8,104... | collective-permute-start | bytes 589832 | tf_op jit(solution)/shard_map/ppermute | solution.py:33
  417.7 111.7 %collective-permute-start.17 = (bf16[4,128,192]{1,2,0:T(8,128)(2,1)S(1)}, bf16[4,128,192]{1,2,0:T(8,128)(2,1)}, u32[]{:S(2)}, u32[]{:S(2)}) collective-permute-start(bf16[4,128,192]{1,2,0:T(8,128)(2,1)S(1)} %copy-done.13), channel_id=1, source_target_pairs={{0,24},{1,25},{2,26},{3,27},{4,28},{5,29},{6,30},{7,31},{8,0},{9,1... | collective-permute-start | bytes 589832 | tf_op jit(solution)/shard_map/ppermute | solution.py:33
  419.6 103.0 %collective-permute-start.71 = (f32[8,128]{1,0:T(8,128)S(1)}, f32[8,128]{1,0:T(8,128)S(1)}, u32[]{:S(2)}, u32[]{:S(2)}) collective-permute-start(f32[8,128]{1,0:T(8,128)S(1)} %broadcast_in_dim.75), channel_id=1, source_target_pairs={{128,0},{129,1},{130,2},{131,3},{132,4},{133,5},{134,6},{135,7},{1... | collective-permute-start | bytes 12296 | tf_op jit(solution)/shard_map/ppermute | solution.py:33
  423.4 100.5 %collective-permute-start.68 = (bf16[4,192,128]{2,1,0:T(8,128)(2,1)S(1)}, bf16[4,192,128]{2,1,0:T(8,128)(2,1)S(1)}, u32[]{:S(2)}, u32[]{:S(2)}) collective-permute-start(bf16[4,192,128]{2,1,0:T(8,128)(2,1)S(1)} %get-tuple-element.73), channel_id=1, source_target_pairs={{128,136},{129,137},{130,138},{131,139},{132,140},{133,141},{134,1... | collective-permute-start | bytes 589832 | tf_op jit(solution)/shard_map/ppermute | solution.py:33
  424.3 101.0 %collective-permute-start.70 = (bf16[4,192,128]{2,1,0:T(8,128)(2,1)S(1)}, bf16[4,192,128]{2,1,0:T(8,128)(2,1)S(1)}, u32[]{:S(2)}, u32[]{:S(2)}) collective-permute-start(bf16[4,192,128]{2,1,0:T(8,128)(2,1)S(1)} %get-tuple-element.74), channel_id=1, source_target_pairs={{128,152},{129,153},{130,154},{131,155},{132,156},{133,157},{134,1... | collective-permute-start | bytes 589832 | tf_op jit(solution)/shard_map/ppermute | solution.py:33
  424.9 101.6 %collective-permute-start.69 = (bf16[4,192,128]{2,1,0:T(8,128)(2,1)S(1)}, bf16[4,192,128]{2,1,0:T(8,128)(2,1)S(1)}, u32[]{:S(2)}, u32[]{:S(2)}) collective-permute-start(bf16[4,192,128]{2,1,0:T(8,128)(2,1)S(1)} %get-tuple-element.75), channel_id=1, source_target_pairs={{128,144},{129,145},{130,146},{131,147},{132,148},{133,149},{134,1... | collective-permute-start | bytes 589832 | tf_op jit(solution)/shard_map/ppermute | solution.py:33
  522.7 32.4 %collective-permute-start.60 = (bf16[4,128,640]{2,1,0:T(8,128)(2,1)S(1)}, bf16[4,128,640]{2,1,0:T(8,128)(2,1)}, u32[]{:S(2)}, u32[]{:S(2)}) collective-permute-start(bf16[4,128,640]{2,1,0:T(8,128)(2,1)S(1)} %pad_maximum_fusion.7), channel_id=1, source_target_pairs={{128,96},{129,97},{130,98},{131,99},{132,100},{133,101},{134,102},... | collective-permute-start | bytes 1966088 | tf_op jit(solution)/shard_map/ppermute | solution.py:33
  524.0 32.1 %collective-permute-start.59 = (bf16[4,128,640]{2,1,0:T(8,128)(2,1)S(1)}, bf16[4,128,640]{2,1,0:T(8,128)(2,1)}, u32[]{:S(2)}, u32[]{:S(2)}) collective-permute-start(bf16[4,128,640]{2,1,0:T(8,128)(2,1)S(1)} %pad_maximum_fusion.7), channel_id=1, source_target_pairs={{128,64},{129,65},{130,66},{131,67},{132,68},{133,69},{134,70},{13... | collective-permute-start | bytes 1966088 | tf_op jit(solution)/shard_map/ppermute | solution.py:33
  525.3 37.7 %collective-permute-start.58 = (bf16[4,128,640]{2,1,0:T(8,128)(2,1)S(1)}, bf16[4,128,640]{2,1,0:T(8,128)(2,1)}, u32[]{:S(2)}, u32[]{:S(2)}) collective-permute-start(bf16[4,128,640]{2,1,0:T(8,128)(2,1)S(1)} %pad_maximum_fusion.7), channel_id=1, source_target_pairs={{128,32},{129,33},{130,34},{131,35},{132,36},{133,37},{134,38},{13... | collective-permute-start | bytes 1966088 | tf_op jit(solution)/shard_map/ppermute | solution.py:33
  526.6 36.4 %collective-permute-start.57 = (bf16[4,128,640]{2,1,0:T(8,128)(2,1)S(1)}, bf16[4,128,640]{2,1,0:T(8,128)(2,1)S(1)}, u32[]{:S(2)}, u32[]{:S(2)}) collective-permute-start(bf16[4,128,640]{2,1,0:T(8,128)(2,1)S(1)} %pad_maximum_fusion.7), channel_id=1, source_target_pairs={{128,0},{129,1},{130,2},{131,3},{132,4},{133,5},{134,6},{135,7},{1... | collective-permute-start | bytes 1966088 | tf_op jit(solution)/shard_map/ppermute | solution.py:33
  529.4 15.2 %collective-permute-start.16 = (bf16[4,128,192]{1,2,0:T(8,128)(2,1)S(1)}, bf16[4,128,192]{1,2,0:T(8,128)(2,1)S(1)}, u32[]{:S(2)}, u32[]{:S(2)}) collective-permute-start(bf16[4,128,192]{1,2,0:T(8,128)(2,1)S(1)} %copy-done.12), channel_id=1, source_target_pairs={{0,16},{1,17},{2,18},{3,19},{4,20},{5,21},{6,22},{7,23},{8,24},{9,... | collective-permute-start | bytes 589832 | tf_op jit(solution)/shard_map/ppermute | solution.py:33
  544.6 10.5 %collective-permute-start.15 = (bf16[4,128,192]{1,2,0:T(8,128)(2,1)S(1)}, bf16[4,128,192]{1,2,0:T(8,128)(2,1)S(1)}, u32[]{:S(2)}, u32[]{:S(2)}) collective-permute-start(bf16[4,128,192]{1,2,0:T(8,128)(2,1)S(1)} %copy-done.11), channel_id=1, source_target_pairs={{0,8},{1,9},{2,10},{3,11},{4,12},{5,13},{6,14},{7,15},{8,16},{9,17... | collective-permute-start | bytes 589832 | tf_op jit(solution)/shard_map/ppermute | solution.py:33
  (59 other events, 1245.4 us)
Sparse Core Ops, SparseCore 0:
  10.4 145.9 all-gather.4
  158.9 85.2 all-gather.6

commit v2 on v1

--- a/solution.py
+++ b/solution.py
@@ -59,9 +59,13 @@
     return step(step(value, 1, groups), 0, groups).reshape((4, 4) + value.shape)
 
 
-def gather_fsdp(value, groups):
-    pair = jnp.stack([value, moved(value, along(3, 1), groups)])
-    return direct4(pair, 2, groups)
+def gather_fsdp(value, groups, cross=False):
+    parts = []
+    for dx in range(4):
+        for dw in range(2):
+            stays = dx == dw == 0 and not cross
+            parts.append(value if stays else moved(value, (0, 0, dx, dw), groups, cross))
+    return jnp.stack(parts).reshape((4, 2) + value.shape)
 
 
 def swap_seq(blocks, groups):
@@ -72,10 +76,46 @@
 
 
 def scatter_fsdp(blocks, groups):
-    total = blocks[0].astype(F32)
-    for k in (2, 1, 3):
-        total = total + moved(blocks[k], along(2, k), groups).astype(F32)
-    return total[0] + moved(total[1], along(3, 1), groups)
+    total = blocks[0, 0].astype(F32)
+    for dx in range(4):
+        for dw in range(2):
+            if dx or dw:
+                total = total + moved(blocks[dx, dw], (0, 0, dx, dw), groups).astype(F32)
+    return total
+
+
+def after(value, other):
+    first = other[(slice(0, 1),) * other.ndim].reshape(())
+    return value + (first.astype(F32) * 0.0).astype(value.dtype)
+
+
+def ring_parts(value, axis, groups):
+    one = moved(value, along(axis, 1), groups)
+    three = moved(value, along(axis, -1), groups)
+    half = value.shape[0] // 2
+    low = moved(one[:half], along(axis, 1), groups)
+    high = moved(three[half:], along(axis, -1), groups)
+    return [(0, 0, value), (1, 0, one), (3, 0, three), (2, 0, low), (2, half, high)]
+
+
+def gather_weights(shard, groups, y, z):
+    depth, width = shard.shape
+    cut = 2 * width // 3
+    part = shard[:, :cut]
+    line = jnp.zeros((4, depth, cut), shard.dtype)
+    for back, first, piece in ring_parts(part, 1, groups):
+        line = lax.dynamic_update_slice(line, piece[None], ((z - back) % 4, first, 0))
+    lead = jnp.zeros((4, 4, depth, cut), shard.dtype)
+    for back, first, piece in ring_parts(line, 0, groups):
+        lead = lax.dynamic_update_slice(lead, piece[None], ((y - back) % 4, first, 0, 0))
+    part = shard[:, cut:]
+    line = jnp.zeros((4, depth, width - cut), shard.dtype)
+    for back, first, piece in ring_parts(part, 0, groups):
+        line = lax.dynamic_update_slice(line, piece[None], ((y - back) % 4, first, 0))
+    tail = jnp.zeros((4, 4, depth, width - cut), shard.dtype)
+    for back, first, piece in ring_parts(line, 1, groups):
+        tail = lax.dynamic_update_slice(tail, piece[:, None], (first, (z - back) % 4, 0, 0))
+    return lead.reshape(16 * depth, cut), tail.reshape(16 * depth, width - cut)
 
 
 def ordered(relative, x, w):
@@ -245,12 +285,15 @@
     return high.astype(BF16), (value - high).astype(BF16)
 
 
-def project(row_block, gain_vector, weight_set):
+def project(row_block, gain_vector, weights):
+    lead, tail = weights
+    width = tail.shape[1]
     lifted = row_block.astype(F32)
     inverse = lax.rsqrt(jnp.mean(lifted * lifted, axis=-1, keepdims=True) + EPS)
     normed = (lifted * inverse * gain_vector).astype(BF16)
-    parts = [jnp.dot(normed, weight_set[c], preferred_element_type=F32) for c in range(3)]
-    return [part.astype(BF16) for part in parts], inverse
+    pair = jnp.dot(normed, lead, preferred_element_type=F32).astype(BF16)
+    values = jnp.dot(normed, tail, preferred_element_type=F32).astype(BF16)
+    return (pair[:, :width], pair[:, width:], values), inverse
 
 
 def unit_terms(units, head_out):
@@ -283,33 +326,32 @@
     gains = norm_gains[0]
     start = fsdp_at * cols
 
-    weights = lax.all_gather(attn_weights[0], "seq", axis=1, tiled=True)
     full_out = lax.all_gather(out_weights[0], "seq", axis=0, tiled=True)
-
-    real_rows = pick_rows(real_bank, real_pick)
-    first_rows = jnp.where(is_gen, new_rows, real_rows)
-    (first_q, first_k, first_v), _ = project(first_rows, gains, weights)
-    first_kv = gather_seq(jnp.concatenate([first_k, first_v], axis=1), (0, 1))
+    shard = jnp.concatenate([attn_weights[0, c] for c in range(3)], axis=1)
+    gen_weights = gather_weights(shard, GEN, y, z)
+    arrived = moved(gen_weights[0][:8, :HD] + gen_weights[1][:8, :HD], (0, 0, 0, 0), GEN, cross=True)
+    weights = gather_weights(after(shard, arrived), CRIT, y, z)
+
+    (first_q, first_k, first_v), _ = project(new_rows, gains, gen_weights)
+    first_kv = gather_seq(jnp.concatenate([first_k, first_v], axis=1), GEN)
     first_kv = first_kv.reshape(tokens, 2 * width)
     key_y = (y - jnp.arange(tokens) // (4 * rows)) % 4
     mask = jnp.broadcast_to((key_y // 2 <= y // 2).astype(F32)[None], (8, tokens))
     first_heads = lax.cond(
         is_gen,
         lambda a: generator_attention(*a),
-        lambda a: critic_attention(a[2], a[5])[0],
+        lambda a: jnp.zeros_like(a[2]),
         (cache_frames, mask, first_q, cache_keys, cache_values, first_kv),
     )
 
     gathered = ordered(gather_fsdp(first_heads, GEN), x, w).reshape(8, rows, width)
     first_all = gathered.transpose(1, 0, 2).reshape(rows, 8 * width)
-    first_cols = lax.dynamic_slice_in_dim(first_rows, start, cols, 1).astype(F32)
+    first_cols = lax.dynamic_slice_in_dim(new_rows, start, cols, 1).astype(F32)
     generated = (first_cols + jnp.dot(first_all, full_out, preferred_element_type=F32)).astype(BF16)
-    pair = jnp.stack([generated, moved(generated, along(3, 1), GEN)])
-    crossed = jnp.stack([moved(pair, along(2, k), GEN, cross=True) for k in range(4)])
-    crossed = ordered(crossed, x, w).reshape(8, rows, cols)
+    crossed = ordered(gather_fsdp(generated, GEN, cross=True), x, w).reshape(8, rows, cols)
     second_rows = crossed.transpose(1, 0, 2).reshape(rows, model)
 
-    to_seq = first_all.reshape(rows, 4, 4, 192).transpose(1, 2, 0, 3)
+    to_seq = after(first_all, generated).reshape(rows, 4, 4, 192).transpose(1, 2, 0, 3)
     gen_heads = swap_seq(jnp.roll(to_seq, (-y, -z), (0, 1)), GEN).reshape(tokens, 192)
 
     joint = jnp.dot(full_out, head_in, preferred_element_type=F32).reshape(4, 2, width, -1)
@@ -322,8 +364,27 @@
         part = part + jnp.dot(heads, low, preferred_element_type=F32)
         return jnp.sum(gather_fsdp(part, CRIT), axis=(0, 1))
 
-    real_cols = lax.dynamic_slice_in_dim(first_rows, start, cols, 1)
-    real_score, real_unit = unit_terms(units_of(real_cols, first_heads), head_out)
+    real_rows = pick_rows(real_bank, real_pick)
+
+    def real_project(operands):
+        (real_q, real_k, real_v), _ = project(operands[0], operands[1], operands[2:])
+        return real_q, jnp.concatenate([real_k, real_v], axis=1)
+
+    real_q, real_kv = lax.cond(
+        is_gen,
+        lambda a: (jnp.zeros((rows, width), BF16), jnp.zeros((rows, 2 * width), BF16)),
+        real_project,
+        (real_rows, gains, *weights),
+    )
+    real_kv = gather_seq(real_kv, CRIT)
+    real_heads = lax.cond(
+        is_gen,
+        lambda a: jnp.zeros_like(a[0]),
+        lambda a: critic_attention(*a)[0],
+        (real_q, real_kv.reshape(tokens, 2 * width)),
+    )
+    real_cols = lax.dynamic_slice_in_dim(real_rows, start, cols, 1)
+    real_score, real_unit = unit_terms(units_of(real_cols, real_heads), head_out)
 
     (second_q, second_k, second_v), inverse = project(second_rows, gains, weights)
     every = gather_seq(jnp.concatenate([second_k, second_v, second_q], axis=1), CRIT)
@@ -338,24 +399,26 @@
     key_grad, value_grad = key_grads(
         second_k, second_v, every[:, 2 * width :], sent, high, low
     )
-    row_terms = sum(
-        mm(grad, weights[c], 1, 1) for c, grad in enumerate((query_grad, key_grad, value_grad))
-    ).astype(BF16)
+    lead, tail = weights
+    lead_grads = jnp.concatenate([query_grad, key_grad], axis=1)
+    row_terms = (mm(lead_grads, lead, 1, 1) + mm(value_grad, tail, 1, 1)).astype(BF16)
     blocks = row_terms.reshape(rows, 4, 2, cols).transpose(1, 2, 0, 3)
     row_grad = scatter_fsdp(jnp.roll(blocks, (-x, -w), (0, 1)), CRIT)
     gain_cols = lax.dynamic_slice_in_dim(gains, start, cols, 0)
     direction = mm(fake_unit, head_in, 1, 1)
     input_grad = (inverse * row_grad * gain_cols + direction).astype(BF16)
 
-    four = ring4(input_grad, 1, CRIT)
+    four = direct4(input_grad, 1, CRIT)
     back = jnp.stack([moved(four, along(0, k), CRIT, cross=True) for k in range(4)])
     back = back.reshape(tokens, cols)
     term_gen = mm(gen_heads, back, 0, 0)
 
-    product = mm(second_heads, fake_unit, 0, 0) - mm(first_heads, real_unit, 0, 0)
-    product = ordered(gather_fsdp(product.astype(BF16), CRIT), x, w).reshape(4, 4, 192, -1)
-    product = swap_seq(jnp.roll(product, (-y, -z), (0, 1)), CRIT)
-    product_high, product_low = split(jnp.sum(product.astype(F32), axis=(0, 1)))
+    product = mm(second_heads, fake_unit, 0, 0) - mm(real_heads, real_unit, 0, 0)
+    product = moved(product.astype(BF16), (0, 0, 0, 0), CRIT, cross=True)
+    product = ordered(gather_fsdp(product, GEN), x, w).reshape(4, 4, 192, -1)
+    product = swap_seq(jnp.roll(product, (-y, -z), (0, 1)), GEN)
+    product = jnp.sum(product.astype(F32), axis=(0, 1))
+    product_high, product_low = split(moved(product, (0, 0, 0, 0), GEN, cross=True))
     term_crit = mm(product_high, head_in, 1, 1) + mm(product_low, head_in, 1, 1)
 
     stats = sent[:, HD:].astype(F32)

time: 585 us -> 829 us (1.42)
  the two profiles are of different devices: /device:TPU:6 before, /device:TPU:32 now
where the time goes in v2:
time: 829 us; the launch traced here: 816 us
  starting transfers between devices  432 us (52%)
  waiting for transfers between devices  208 us (25%)
  local copies, waits for them, and re-layouts  74.1 us (9%)
  other arithmetic  33 us (4%)
  matrix products  27.1 us (3%)
  between operations  21.8 us (3%)
  Pallas kernels  20 us (2%)
    ppermute x135, starting transfers between devices, moved(): return lax.ppermute(value, AXES, pairs)  432 us
    ppermute x135, waiting for transfers between devices, moved(): return lax.ppermute(value, AXES, pairs)  208 us
  transfers between devices with their start and end apart: 136, of which 22 were waited for; matrix products, arithmetic and copies ran while one was open for 15% of the time, Pallas kernels for 2%

profile of v2, /device:TPU:32, one launch (start us, length us, event | category | flops | bytes accessed | tf_op | source)
XLA Modules:
  0.0 816.4 jit_solution(4459983012007432473)
XLA Ops:
  10.2 5.2 collective-permute-start
  47.3 5.4 collective-permute-start.13
  64.7 45.8 %collective-permute-done.2 = bf16[160,768]{1,0:T(8,128)(2,1)S(1)} collective-permute-done((bf16[160,768]{1,0:T(8,128)(2,1)S(1)}, bf16[160,768]{1,0:T(8,128)(2,1)S(1)}, u32[]{:S(2)}, u32[]{:S(2)}) %collective-permute-start.2) | collective-permute-done | bytes 245792 | tf_op jit(solution)/shard_map/ppermute | solution.py:33
  128.7 9.6 %collective-permute-done.14 = bf16[2,320,384]{2,1,0:T(8,128)(2,1)S(1)} collective-permute-done((bf16[2,320,384]{2,1,0:T(8,128)(2,1)S(1)}, bf16[2,320,384]{2,1,0:T(8,128)(2,1)S(1)}, u32[]{:S(2)}, u32[]{:S(2)}) %collective-permute-start.14) | collective-permute-done | bytes 491552 | tf_op jit(solution)/shard_map/ppermute | solution.py:33
  142.3 5.1 collective-permute-start.7
  148.8 8.7 %collective-permute-done.6 = bf16[2,320,768]{2,1,0:T(8,128)(2,1)S(1)} collective-permute-done((bf16[2,320,768]{2,1,0:T(8,128)(2,1)S(1)}, bf16[2,320,768]{2,1,0:T(8,128)(2,1)S(1)}, u32[]{:S(2)}, u32[]{:S(2)}) %collective-permute-start.6) | collective-permute-done | bytes 983072 | tf_op jit(solution)/shard_map/ppermute | solution.py:33
  161.8 6.5 collective-permute-start.18
  182.0 4.8 collective-permute-start.17
  193.8 9.0 %collective-permute-start.22 = (bf16[4,128,768]{2,1,0:T(8,128)(2,1)S(1)}, bf16[4,128,768]{2,1,0:T(8,128)(2,1)S(1)}, u32[]{:S(2)}, u32[]{:S(2)}) collective-permute-start(bf16[4,128,768]{2,1,0:T(8,128)(2,1)S(1)} %get-tuple-element.121), channel_id=1, source_target_pairs={{0,96},{1,97},{2,98},{3,99},{4,100},{5,101},{6,102},{7,103},{8,104... | collective-permute-start | bytes 2359304 | tf_op jit(solution)/shard_map/ppermute | solution.py:33
  212.3 5.6 collective-permute-start.23
  236.0 8.6 %conditional.3 = (bf16[128,384]{1,0:T(8,128)(2,1)}, bf16[1,128,384]{2,1,0:T(8,128)(2,1)S(1)}) conditional(s32[]{:T(128)} %convert_element_type.145, () %tuple.35, (s32[3]{0:T(128)S(1)}, f32[2048]{0:T(1024)S(1)}, bf16[128,768]{1,0:T(8,128)(2,1)S(1)}, bf16[4,1024,384]{2,1,0:T(8,128)(2,1)S(1)}, bf16[4,1024,384]{2,1,0:T(8,128)(2,1)S(1)}, ...), branch_computations={%region_1.2_spmd, %region_2.3_spmd} | conditional | bytes 466960 | solution.py:340
  236.0 7.7 branch_1_fun.1
  269.0 5.7 collective-permute-start.30
  304.6 7.7 collective-permute-start.38
  313.7 13.1 %collective-permute-start.40 = (bf16[128,640]{1,0:T(8,128)(2,1)}, bf16[128,640]{1,0:T(8,128)(2,1)S(1)}, u32[]{:S(2)}, u32[]{:S(2)}) collective-permute-start(bf16[128,640]{1,0:T(8,128)(2,1)} %fusion.52), channel_id=1, source_target_pairs={{0,135},{1,134},{2,129},{3,128},{4,131},{5,130},{6,133},{7,132},{8... | collective-permute-start | bytes 491528 | tf_op jit(solution)/shard_map/ppermute | solution.py:33
  329.5 13.3 %collective-permute-start.39 = (bf16[128,640]{1,0:T(8,128)(2,1)}, bf16[128,640]{1,0:T(8,128)(2,1)S(1)}, u32[]{:S(2)}, u32[]{:S(2)}) collective-permute-start(bf16[128,640]{1,0:T(8,128)(2,1)} %fusion.52), channel_id=1, source_target_pairs={{0,134},{1,135},{2,128},{3,129},{4,130},{5,131},{6,132},{7,133},{8... | collective-permute-start | bytes 491528 | tf_op jit(solution)/shard_map/ppermute | solution.py:33
  345.0 13.1 %collective-permute-start.42 = (bf16[128,640]{1,0:T(8,128)(2,1)}, bf16[128,640]{1,0:T(8,128)(2,1)S(1)}, u32[]{:S(2)}, u32[]{:S(2)}) collective-permute-start(bf16[128,640]{1,0:T(8,128)(2,1)} %fusion.52), channel_id=1, source_target_pairs={{0,133},{1,132},{2,135},{3,134},{4,129},{5,128},{6,131},{7,130},{8... | collective-permute-start | bytes 491528 | tf_op jit(solution)/shard_map/ppermute | solution.py:33
  360.2 17.9 %collective-permute-start.41 = (bf16[128,640]{1,0:T(8,128)(2,1)}, bf16[128,640]{1,0:T(8,128)(2,1)S(1)}, u32[]{:S(2)}, u32[]{:S(2)}) collective-permute-start(bf16[128,640]{1,0:T(8,128)(2,1)} %fusion.52), channel_id=1, source_target_pairs={{0,132},{1,133},{2,134},{3,135},{4,128},{5,129},{6,130},{7,131},{8... | collective-permute-start | bytes 491528 | tf_op jit(solution)/shard_map/ppermute | solution.py:33
  378.1 13.1 %collective-permute-start.44 = (bf16[128,640]{1,0:T(8,128)(2,1)}, bf16[128,640]{1,0:T(8,128)(2,1)S(1)}, u32[]{:S(2)}, u32[]{:S(2)}) collective-permute-start(bf16[128,640]{1,0:T(8,128)(2,1)} %fusion.52), channel_id=1, source_target_pairs={{0,131},{1,130},{2,133},{3,132},{4,135},{5,134},{6,129},{7,128},{8... | collective-permute-start | bytes 491528 | tf_op jit(solution)/shard_map/ppermute | solution.py:33
  391.3 13.1 %collective-permute-start.43 = (bf16[128,640]{1,0:T(8,128)(2,1)}, bf16[128,640]{1,0:T(8,128)(2,1)S(1)}, u32[]{:S(2)}, u32[]{:S(2)}) collective-permute-start(bf16[128,640]{1,0:T(8,128)(2,1)} %fusion.52), channel_id=1, source_target_pairs={{0,130},{1,131},{2,132},{3,133},{4,134},{5,135},{6,128},{7,129},{8... | collective-permute-start | bytes 491528 | tf_op jit(solution)/shard_map/ppermute | solution.py:33
  503.4 102.0 %collective-permute-done.119 = bf16[384,128]{1,0:T(8,128)(2,1)S(1)} collective-permute-done((bf16[384,128]{1,0:T(8,128)(2,1)S(1)}, bf16[384,128]{1,0:T(8,128)(2,1)S(1)}, u32[]{:S(2)}, u32[]{:S(2)}) %collective-permute-start.119) | collective-permute-done | bytes 98336 | tf_op jit(solution)/shard_map/ppermute | solution.py:33
  608.9 5.5 collective-permute-start.122
  617.2 4.9 collective-permute-start.124
  634.7 8.5 %collective-permute-start.103 = (bf16[4,128,256]{2,1,0:T(8,128)(2,1)S(1)}, bf16[4,128,256]{2,1,0:T(8,128)(2,1)S(1)}, u32[]{:S(2)}, u32[]{:S(2)}) collective-permute-start(bf16[4,128,256]{2,1,0:T(8,128)(2,1)S(1)} %get-tuple-element.128), channel_id=1, source_target_pairs={{128,192},{129,193},{130,194},{131,195},{132,196},{133,197},{134,1... | collective-permute-start | bytes 786440 | tf_op jit(solution)/shard_map/ppermute | solution.py:33
  661.9 5.9 fusion.5
  684.6 6.2 collective-permute-start.36
  707.1 24.7 %collective-permute-start.134 = (f32[8,128]{1,0:T(8,128)S(1)}, f32[8,128]{1,0:T(8,128)S(1)}, u32[]{:S(2)}, u32[]{:S(2)}) collective-permute-start(f32[8,128]{1,0:T(8,128)S(1)} %broadcast_in_dim.232), channel_id=1, source_target_pairs={{128,0},{129,1},{130,2},{131,3},{132,4},{133,5},{134,6},{135,7},{1... | collective-permute-start | bytes 12296 | tf_op jit(solution)/shard_map/ppermute | solution.py:33
  733.0 12.9 %collective-permute-start.118 = (bf16[4,128,640]{2,1,0:T(8,128)(2,1)S(1)}, bf16[4,128,640]{2,1,0:T(8,128)(2,1)}, u32[]{:S(2)}, u32[]{:S(2)}) collective-permute-start(bf16[4,128,640]{2,1,0:T(8,128)(2,1)S(1)} %pad_maximum_fusion.10), channel_id=1, source_target_pairs={{128,96},{129,97},{130,98},{131,99},{132,100},{133,101},{134,102},... | collective-permute-start | bytes 1966088 | tf_op jit(solution)/shard_map/ppermute | solution.py:33
  745.9 13.7 %collective-permute-start.117 = (bf16[4,128,640]{2,1,0:T(8,128)(2,1)S(1)}, bf16[4,128,640]{2,1,0:T(8,128)(2,1)}, u32[]{:S(2)}, u32[]{:S(2)}) collective-permute-start(bf16[4,128,640]{2,1,0:T(8,128)(2,1)S(1)} %pad_maximum_fusion.10), channel_id=1, source_target_pairs={{128,64},{129,65},{130,66},{131,67},{132,68},{133,69},{134,70},{13... | collective-permute-start | bytes 1966088 | tf_op jit(solution)/shard_map/ppermute | solution.py:33
  759.6 13.7 %collective-permute-start.116 = (bf16[4,128,640]{2,1,0:T(8,128)(2,1)S(1)}, bf16[4,128,640]{2,1,0:T(8,128)(2,1)}, u32[]{:S(2)}, u32[]{:S(2)}) collective-permute-start(bf16[4,128,640]{2,1,0:T(8,128)(2,1)S(1)} %pad_maximum_fusion.10), channel_id=1, source_target_pairs={{128,32},{129,33},{130,34},{131,35},{132,36},{133,37},{134,38},{13... | collective-permute-start | bytes 1966088 | tf_op jit(solution)/shard_map/ppermute | solution.py:33
  780.5 7.5 collective-permute-start.35
  797.1 7.5 collective-permute-done.34
  (529 shorter events, 371.7 us)
Async XLA Ops:
  7.2 293.6 %all-gather.3.cloned.1.call-start = ((), (), s32[]{:S(2)}) async-start(), calls=%async_computation | async-start | bytes 4177920 | tf_op jit(solution)/shard_map/all_gather | solution.py:329
  10.2 42.5 %collective-permute-start = (bf16[320,768]{1,0:T(8,128)(2,1)}, bf16[320,768]{1,0:T(8,128)(2,1)}, u32[]{:S(2)}, u32[]{:S(2)}) collective-permute-start(bf16[320,768]{1,0:T(8,128)(2,1)} %pad_maximum_fusion.11), channel_id=1, source_target_pairs={{0,8},{1,9},{2,10},{3,11},{4,12},{5,13},{6,14},{7,15},{8,16},{9,17... | collective-permute-start | bytes 1474568 | tf_op jit(solution)/shard_map/ppermute | solution.py:33
  15.4 41.4 %collective-permute-start.1 = (bf16[320,768]{1,0:T(8,128)(2,1)}, bf16[320,768]{1,0:T(8,128)(2,1)}, u32[]{:S(2)}, u32[]{:S(2)}) collective-permute-start(bf16[320,768]{1,0:T(8,128)(2,1)} %pad_maximum_fusion.11), channel_id=1, source_target_pairs={{0,24},{1,25},{2,26},{3,27},{4,28},{5,29},{6,30},{7,31},{8,0},{9,1... | collective-permute-start | bytes 1474568 | tf_op jit(solution)/shard_map/ppermute | solution.py:33
  44.7 75.6 %collective-permute-start.12 = (bf16[4,320,384]{2,1,0:T(8,128)(2,1)S(1)}, bf16[4,320,384]{2,1,0:T(8,128)(2,1)S(1)}, u32[]{:S(2)}, u32[]{:S(2)}) collective-permute-start(bf16[4,320,384]{2,1,0:T(8,128)(2,1)S(1)} %bitcast_dynamic-update-slice_fusion.38), channel_id=1, source_target_pairs={{0,8},{1,9},{2,10},{3,11},{4,12},{5,13},{6,14},{7,15},{8,16},{9,17... | collective-permute-start | bytes 2949128 | tf_op jit(solution)/shard_map/ppermute | solution.py:33
  47.3 76.5 %collective-permute-start.13 = (bf16[4,320,384]{2,1,0:T(8,128)(2,1)S(1)}, bf16[4,320,384]{2,1,0:T(8,128)(2,1)S(1)}, u32[]{:S(2)}, u32[]{:S(2)}) collective-permute-start(bf16[4,320,384]{2,1,0:T(8,128)(2,1)S(1)} %bitcast_dynamic-update-slice_fusion.38), channel_id=1, source_target_pairs={{0,24},{1,25},{2,26},{3,27},{4,28},{5,29},{6,30},{7,31},{8,0},{9,1... | collective-permute-start | bytes 2949128 | tf_op jit(solution)/shard_map/ppermute | solution.py:33
  53.6 56.9 %collective-permute-start.2 = (bf16[160,768]{1,0:T(8,128)(2,1)S(1)}, bf16[160,768]{1,0:T(8,128)(2,1)S(1)}, u32[]{:S(2)}, u32[]{:S(2)}) collective-permute-start(bf16[160,768]{1,0:T(8,128)(2,1)S(1)} %slice.401), channel_id=1, source_target_pairs={{0,8},{1,9},{2,10},{3,11},{4,12},{5,13},{6,14},{7,15},{8,16},{9,17... | collective-permute-start | bytes 737288 | tf_op jit(solution)/shard_map/ppermute | solution.py:33
  57.8 52.8 %collective-permute-start.3 = (bf16[160,768]{1,0:T(8,128)(2,1)S(1)}, bf16[160,768]{1,0:T(8,128)(2,1)S(1)}, u32[]{:S(2)}, u32[]{:S(2)}) collective-permute-start(bf16[160,768]{1,0:T(8,128)(2,1)S(1)} %slice.402), channel_id=1, source_target_pairs={{0,24},{1,25},{2,26},{3,27},{4,28},{5,29},{6,30},{7,31},{8,0},{9,1... | collective-permute-start | bytes 737288 | tf_op jit(solution)/shard_map/ppermute | solution.py:33
  208.3 38.2 %collective-permute-start.59 = (bf16[4,320,384]{2,1,0:T(8,128)(2,1)S(1)}, bf16[4,320,384]{2,1,0:T(8,128)(2,1)}, u32[]{:S(2)}, u32[]{:S(2)}) collective-permute-start(bf16[4,320,384]{2,1,0:T(8,128)(2,1)S(1)} %bitcast_dynamic-update-slice_fusion.36), channel_id=1, source_target_pairs={{128,152},{129,153},{130,154},{131,155},{132,156},{133,157},{134,1... | collective-permute-start | bytes 2949128 | tf_op jit(solution)/shard_map/ppermute | solution.py:33
  210.1 78.7 %collective-permute-start.50 = (bf16[4,320,768]{2,1,0:T(8,128)(2,1)S(1)}, bf16[4,320,768]{2,1,0:T(8,128)(2,1)}, u32[]{:S(2)}, u32[]{:S(2)}) collective-permute-start(bf16[4,320,768]{2,1,0:T(8,128)(2,1)S(1)} %bitcast_dynamic-update-slice_fusion.29), channel_id=1, source_target_pairs={{128,160},{129,161},{130,162},{131,163},{132,164},{133,165},{134,1... | collective-permute-start | bytes 5898248 | tf_op jit(solution)/shard_map/ppermute | solution.py:33
  225.3 67.4 %collective-permute-start.51 = (bf16[4,320,768]{2,1,0:T(8,128)(2,1)S(1)}, bf16[4,320,768]{2,1,0:T(8,128)(2,1)}, u32[]{:S(2)}, u32[]{:S(2)}) collective-permute-start(bf16[4,320,768]{2,1,0:T(8,128)(2,1)S(1)} %bitcast_dynamic-update-slice_fusion.29), channel_id=1, source_target_pairs={{128,224},{129,225},{130,226},{131,227},{132,228},{133,229},{134,2... | collective-permute-start | bytes 5898248 | tf_op jit(solution)/shard_map/ppermute | solution.py:33
  228.4 56.7 %collective-permute-start.60 = (bf16[2,320,384]{2,1,0:T(8,128)(2,1)}, bf16[2,320,384]{2,1,0:T(8,128)(2,1)}, u32[]{:S(2)}, u32[]{:S(2)}) collective-permute-start(bf16[2,320,384]{2,1,0:T(8,128)(2,1)} %slice.435), channel_id=1, source_target_pairs={{128,136},{129,137},{130,138},{131,139},{132,140},{133,141},{134,1... | collective-permute-start | bytes 1474568 | tf_op jit(solution)/shard_map/ppermute | solution.py:33
  291.0 38.5 %collective-permute-start.52 = (bf16[2,320,768]{2,1,0:T(8,128)(2,1)}, bf16[2,320,768]{2,1,0:T(8,128)(2,1)}, u32[]{:S(2)}, u32[]{:S(2)}) collective-permute-start(bf16[2,320,768]{2,1,0:T(8,128)(2,1)} %slice.428), channel_id=1, source_target_pairs={{128,160},{129,161},{130,162},{131,163},{132,164},{133,165},{134,1... | collective-permute-start | bytes 2949128 | tf_op jit(solution)/shard_map/ppermute | solution.py:33
  294.0 51.0 %collective-permute-start.53 = (bf16[2,320,768]{2,1,0:T(8,128)(2,1)S(1)}, bf16[2,320,768]{2,1,0:T(8,128)(2,1)S(1)}, u32[]{:S(2)}, u32[]{:S(2)}) collective-permute-start(bf16[2,320,768]{2,1,0:T(8,128)(2,1)S(1)} %slice.429), channel_id=1, source_target_pairs={{128,224},{129,225},{130,226},{131,227},{132,228},{133,229},{134,2... | collective-permute-start | bytes 2949128 | tf_op jit(solution)/shard_map/ppermute | solution.py:33
  304.6 55.6 %collective-permute-start.38 = (bf16[128,640]{1,0:T(8,128)(2,1)}, bf16[128,640]{1,0:T(8,128)(2,1)S(1)}, u32[]{:S(2)}, u32[]{:S(2)}) collective-permute-start(bf16[128,640]{1,0:T(8,128)(2,1)} %fusion.52), channel_id=1, source_target_pairs={{0,129},{1,128},{2,131},{3,130},{4,133},{5,132},{6,135},{7,134},{8... | collective-permute-start | bytes 491528 | tf_op jit(solution)/shard_map/ppermute | solution.py:33
  312.3 65.8 %collective-permute-start.37 = (bf16[128,640]{1,0:T(8,128)(2,1)}, bf16[128,640]{1,0:T(8,128)(2,1)S(1)}, u32[]{:S(2)}, u32[]{:S(2)}) collective-permute-start(bf16[128,640]{1,0:T(8,128)(2,1)} %fusion.52), channel_id=1, source_target_pairs={{0,128},{1,129},{2,130},{3,131},{4,132},{5,133},{6,134},{7,135},{8... | collective-permute-start | bytes 491528 | tf_op jit(solution)/shard_map/ppermute | solution.py:33
  313.7 77.6 %collective-permute-start.40 = (bf16[128,640]{1,0:T(8,128)(2,1)}, bf16[128,640]{1,0:T(8,128)(2,1)S(1)}, u32[]{:S(2)}, u32[]{:S(2)}) collective-permute-start(bf16[128,640]{1,0:T(8,128)(2,1)} %fusion.52), channel_id=1, source_target_pairs={{0,135},{1,134},{2,129},{3,128},{4,131},{5,130},{6,133},{7,132},{8... | collective-permute-start | bytes 491528 | tf_op jit(solution)/shard_map/ppermute | solution.py:33
  329.5 75.0 %collective-permute-start.39 = (bf16[128,640]{1,0:T(8,128)(2,1)}, bf16[128,640]{1,0:T(8,128)(2,1)S(1)}, u32[]{:S(2)}, u32[]{:S(2)}) collective-permute-start(bf16[128,640]{1,0:T(8,128)(2,1)} %fusion.52), channel_id=1, source_target_pairs={{0,134},{1,135},{2,128},{3,129},{4,130},{5,131},{6,132},{7,133},{8... | collective-permute-start | bytes 491528 | tf_op jit(solution)/shard_map/ppermute | solution.py:33
  345.0 60.2 %collective-permute-start.42 = (bf16[128,640]{1,0:T(8,128)(2,1)}, bf16[128,640]{1,0:T(8,128)(2,1)S(1)}, u32[]{:S(2)}, u32[]{:S(2)}) collective-permute-start(bf16[128,640]{1,0:T(8,128)(2,1)} %fusion.52), channel_id=1, source_target_pairs={{0,133},{1,132},{2,135},{3,134},{4,129},{5,128},{6,131},{7,130},{8... | collective-permute-start | bytes 491528 | tf_op jit(solution)/shard_map/ppermute | solution.py:33
  360.2 46.4 %collective-permute-start.41 = (bf16[128,640]{1,0:T(8,128)(2,1)}, bf16[128,640]{1,0:T(8,128)(2,1)S(1)}, u32[]{:S(2)}, u32[]{:S(2)}) collective-permute-start(bf16[128,640]{1,0:T(8,128)(2,1)} %fusion.52), channel_id=1, source_target_pairs={{0,132},{1,133},{2,134},{3,135},{4,128},{5,129},{6,130},{7,131},{8... | collective-permute-start | bytes 491528 | tf_op jit(solution)/shard_map/ppermute | solution.py:33
  490.6 117.5 %collective-permute-start.100 = (bf16[128,256]{1,0:T(8,128)(2,1)S(1)}, bf16[128,256]{1,0:T(8,128)(2,1)S(1)}, u32[]{:S(2)}, u32[]{:S(2)}) collective-permute-start(bf16[128,256]{1,0:T(8,128)(2,1)S(1)} %get-tuple-element.66), channel_id=1, source_target_pairs={{128,144},{129,145},{130,146},{131,147},{132,148},{133,149},{134,1... | collective-permute-start | bytes 196616 | tf_op jit(solution)/shard_map/ppermute | solution.py:33
  491.3 116.9 %collective-permute-start.99 = (bf16[128,256]{1,0:T(8,128)(2,1)S(1)}, bf16[128,256]{1,0:T(8,128)(2,1)S(1)}, u32[]{:S(2)}, u32[]{:S(2)}) collective-permute-start(bf16[128,256]{1,0:T(8,128)(2,1)S(1)} %get-tuple-element.66), channel_id=1, source_target_pairs={{128,136},{129,137},{130,138},{131,139},{132,140},{133,141},{134,1... | collective-permute-start | bytes 196616 | tf_op jit(solution)/shard_map/ppermute | solution.py:33
  492.2 113.2 %collective-permute-start.119 = (bf16[384,128]{1,0:T(8,128)(2,1)S(1)}, bf16[384,128]{1,0:T(8,128)(2,1)S(1)}, u32[]{:S(2)}, u32[]{:S(2)}) collective-permute-start(bf16[384,128]{1,0:T(8,128)(2,1)S(1)} %fusion.58), channel_id=1, source_target_pairs={{128,0},{129,1},{130,2},{131,3},{132,4},{133,5},{134,6},{135,7},{1... | collective-permute-start | bytes 294920 | tf_op jit(solution)/shard_map/ppermute | solution.py:33
  494.4 177.9 %collective-permute-start.33 = (bf16[4,128,192]{1,2,0:T(8,128)(2,1)}, bf16[4,128,192]{1,2,0:T(8,128)(2,1)}, u32[]{:S(2)}, u32[]{:S(2)}) collective-permute-start(bf16[4,128,192]{1,2,0:T(8,128)(2,1)} %get-tuple-element.109), channel_id=1, source_target_pairs={{0,96},{1,97},{2,98},{3,99},{4,100},{5,101},{6,102},{7,103},{8,104... | collective-permute-start | bytes 589832 | tf_op jit(solution)/shard_map/ppermute | solution.py:33
  500.7 174.5 %collective-permute-start.32 = (bf16[4,128,192]{1,2,0:T(8,128)(2,1)}, bf16[4,128,192]{1,2,0:T(8,128)(2,1)}, u32[]{:S(2)}, u32[]{:S(2)}) collective-permute-start(bf16[4,128,192]{1,2,0:T(8,128)(2,1)} %get-tuple-element.107), channel_id=1, source_target_pairs={{0,64},{1,65},{2,66},{3,67},{4,68},{5,69},{6,70},{7,71},{8,72},{9,... | collective-permute-start | bytes 589832 | tf_op jit(solution)/shard_map/ppermute | solution.py:33
  684.6 48.4 %collective-permute-start.36 = (bf16[4,128,192]{1,2,0:T(8,128)(2,1)S(1)}, bf16[4,128,192]{1,2,0:T(8,128)(2,1)}, u32[]{:S(2)}, u32[]{:S(2)}) collective-permute-start(bf16[4,128,192]{1,2,0:T(8,128)(2,1)S(1)} %get-tuple-element.103), channel_id=1, source_target_pairs={{0,24},{1,25},{2,26},{3,27},{4,28},{5,29},{6,30},{7,31},{8,0},{9,1... | collective-permute-start | bytes 589832 | tf_op jit(solution)/shard_map/ppermute | solution.py:33
  694.6 51.3 %collective-permute-start.132 = (bf16[4,192,128]{2,1,0:T(8,128)(2,1)}, bf16[4,192,128]{2,1,0:T(8,128)(2,1)S(1)}, u32[]{:S(2)}, u32[]{:S(2)}) collective-permute-start(bf16[4,192,128]{2,1,0:T(8,128)(2,1)} %get-tuple-element.112), channel_id=1, source_target_pairs={{0,24},{1,25},{2,26},{3,27},{4,28},{5,29},{6,30},{7,31},{8,0},{9,1... | collective-permute-start | bytes 589832 | tf_op jit(solution)/shard_map/ppermute | solution.py:33
  698.4 61.3 %collective-permute-start.131 = (bf16[4,192,128]{2,1,0:T(8,128)(2,1)S(1)}, bf16[4,192,128]{2,1,0:T(8,128)(2,1)S(1)}, u32[]{:S(2)}, u32[]{:S(2)}) collective-permute-start(bf16[4,192,128]{2,1,0:T(8,128)(2,1)S(1)} %get-tuple-element.113), channel_id=1, source_target_pairs={{0,16},{1,17},{2,18},{3,19},{4,20},{5,21},{6,22},{7,23},{8,24},{9,... | collective-permute-start | bytes 589832 | tf_op jit(solution)/shard_map/ppermute | solution.py:33
  700.7 72.7 %collective-permute-start.130 = (bf16[4,192,128]{2,1,0:T(8,128)(2,1)S(1)}, bf16[4,192,128]{2,1,0:T(8,128)(2,1)S(1)}, u32[]{:S(2)}, u32[]{:S(2)}) collective-permute-start(bf16[4,192,128]{2,1,0:T(8,128)(2,1)S(1)} %get-tuple-element.111), channel_id=1, source_target_pairs={{0,8},{1,9},{2,10},{3,11},{4,12},{5,13},{6,14},{7,15},{8,16},{9,17... | collective-permute-start | bytes 589832 | tf_op jit(solution)/shard_map/ppermute | solution.py:33
  707.1 67.6 %collective-permute-start.134 = (f32[8,128]{1,0:T(8,128)S(1)}, f32[8,128]{1,0:T(8,128)S(1)}, u32[]{:S(2)}, u32[]{:S(2)}) collective-permute-start(f32[8,128]{1,0:T(8,128)S(1)} %broadcast_in_dim.232), channel_id=1, source_target_pairs={{128,0},{129,1},{130,2},{131,3},{132,4},{133,5},{134,6},{135,7},{1... | collective-permute-start | bytes 12296 | tf_op jit(solution)/shard_map/ppermute | solution.py:33
  733.0 71.6 %collective-permute-start.118 = (bf16[4,128,640]{2,1,0:T(8,128)(2,1)S(1)}, bf16[4,128,640]{2,1,0:T(8,128)(2,1)}, u32[]{:S(2)}, u32[]{:S(2)}) collective-permute-start(bf16[4,128,640]{2,1,0:T(8,128)(2,1)S(1)} %pad_maximum_fusion.10), channel_id=1, source_target_pairs={{128,96},{129,97},{130,98},{131,99},{132,100},{133,101},{134,102},... | collective-permute-start | bytes 1966088 | tf_op jit(solution)/shard_map/ppermute | solution.py:33
  745.9 58.7 %collective-permute-start.117 = (bf16[4,128,640]{2,1,0:T(8,128)(2,1)S(1)}, bf16[4,128,640]{2,1,0:T(8,128)(2,1)}, u32[]{:S(2)}, u32[]{:S(2)}) collective-permute-start(bf16[4,128,640]{2,1,0:T(8,128)(2,1)S(1)} %pad_maximum_fusion.10), channel_id=1, source_target_pairs={{128,64},{129,65},{130,66},{131,67},{132,68},{133,69},{134,70},{13... | collective-permute-start | bytes 1966088 | tf_op jit(solution)/shard_map/ppermute | solution.py:33
  759.6 45.0 %collective-permute-start.116 = (bf16[4,128,640]{2,1,0:T(8,128)(2,1)S(1)}, bf16[4,128,640]{2,1,0:T(8,128)(2,1)}, u32[]{:S(2)}, u32[]{:S(2)}) collective-permute-start(bf16[4,128,640]{2,1,0:T(8,128)(2,1)S(1)} %pad_maximum_fusion.10), channel_id=1, source_target_pairs={{128,32},{129,33},{130,34},{131,35},{132,36},{133,37},{134,38},{13... | collective-permute-start | bytes 1966088 | tf_op jit(solution)/shard_map/ppermute | solution.py:33
  (143 other events, 1833.6 us)
Sparse Core Ops, SparseCore 0:
  26.6 84.2 all-gather.2

commit v3 on v1

--- a/solution.py
+++ b/solution.py
@@ -39,24 +39,12 @@
     return tuple(step)
 
 
-def ring4(value, axis, groups):
-    one = moved(value, along(axis, 1), groups)
-    three = moved(value, along(axis, -1), groups)
-    cut = value.ndim - 2
-    half = value.shape[cut] // 2
-    low = lax.slice_in_dim(one, 0, half, axis=cut)
-    high = lax.slice_in_dim(three, half, 2 * half, axis=cut)
-    low = moved(low, along(axis, 1), groups)
-    high = moved(high, along(axis, -1), groups)
-    return jnp.stack([value, one, jnp.concatenate([low, high], axis=cut), three])
-
-
 def direct4(value, axis, groups):
     return jnp.stack([value] + [moved(value, along(axis, k), groups) for k in (1, 2, 3)])
 
 
-def gather_seq(value, groups, step=ring4):
-    return step(step(value, 1, groups), 0, groups).reshape((4, 4) + value.shape)
+def gather_seq(value, groups):
+    return direct4(direct4(value, 1, groups), 0, groups).reshape((4, 4) + value.shape)
 
 
 def gather_fsdp(value, groups):
@@ -76,6 +64,15 @@
     for k in (2, 1, 3):
         total = total + moved(blocks[k], along(2, k), groups).astype(F32)
     return total[0] + moved(total[1], along(3, 1), groups)
+
+
+def across(value, groups):
+    return moved(value, (0, 0, 0, 0), groups, cross=True)
+
+
+def after(value, other):
+    first = other[(slice(0, 1),) * other.ndim].reshape(())
+    return value + (first.astype(F32) * 0.0).astype(value.dtype)
 
 
 def ordered(relative, x, w):
@@ -245,12 +242,14 @@
     return high.astype(BF16), (value - high).astype(BF16)
 
 
-def project(row_block, gain_vector, weight_set):
+def normalised(row_block, gain_vector):
     lifted = row_block.astype(F32)
     inverse = lax.rsqrt(jnp.mean(lifted * lifted, axis=-1, keepdims=True) + EPS)
-    normed = (lifted * inverse * gain_vector).astype(BF16)
-    parts = [jnp.dot(normed, weight_set[c], preferred_element_type=F32) for c in range(3)]
-    return [part.astype(BF16) for part in parts], inverse
+    return (lifted * inverse * gain_vector).astype(BF16), inverse
+
+
+def times(a, b):
+    return jnp.dot(a, b, preferred_element_type=F32).astype(BF16)
 
 
 def unit_terms(units, head_out):
@@ -283,14 +282,18 @@
     gains = norm_gains[0]
     start = fsdp_at * cols
 
-    weights = lax.all_gather(attn_weights[0], "seq", axis=1, tiled=True)
+    shard_q, shard_k, shard_v = (attn_weights[0, c] for c in range(3))
+    shard_kv = jnp.concatenate([shard_k, shard_v], axis=1)
+    weights_kv = lax.all_gather(shard_kv, "seq", axis=0, tiled=True)
+    weights_q = lax.all_gather(shard_q, "seq", axis=0, tiled=True)
     full_out = lax.all_gather(out_weights[0], "seq", axis=0, tiled=True)
 
     real_rows = pick_rows(real_bank, real_pick)
     first_rows = jnp.where(is_gen, new_rows, real_rows)
-    (first_q, first_k, first_v), _ = project(first_rows, gains, weights)
-    first_kv = gather_seq(jnp.concatenate([first_k, first_v], axis=1), (0, 1))
+    first_normed, _ = normalised(first_rows, gains)
+    first_kv = gather_seq(times(first_normed, weights_kv), (0, 1))
     first_kv = first_kv.reshape(tokens, 2 * width)
+    first_q = times(first_normed, weights_q)
     key_y = (y - jnp.arange(tokens) // (4 * rows)) % 4
     mask = jnp.broadcast_to((key_y // 2 <= y // 2).astype(F32)[None], (8, tokens))
     first_heads = lax.cond(
@@ -304,63 +307,62 @@
     first_all = gathered.transpose(1, 0, 2).reshape(rows, 8 * width)
     first_cols = lax.dynamic_slice_in_dim(first_rows, start, cols, 1).astype(F32)
     generated = (first_cols + jnp.dot(first_all, full_out, preferred_element_type=F32)).astype(BF16)
-    pair = jnp.stack([generated, moved(generated, along(3, 1), GEN)])
-    crossed = jnp.stack([moved(pair, along(2, k), GEN, cross=True) for k in range(4)])
-    crossed = ordered(crossed, x, w).reshape(8, rows, cols)
+    crossed = ordered(gather_fsdp(across(generated, GEN), CRIT), x, w).reshape(8, rows, cols)
     second_rows = crossed.transpose(1, 0, 2).reshape(rows, model)
 
     to_seq = first_all.reshape(rows, 4, 4, 192).transpose(1, 2, 0, 3)
     gen_heads = swap_seq(jnp.roll(to_seq, (-y, -z), (0, 1)), GEN).reshape(tokens, 192)
 
-    joint = jnp.dot(full_out, head_in, preferred_element_type=F32).reshape(4, 2, width, -1)
-    joint = scatter_fsdp(jnp.roll(joint, (-x, -w), (0, 1)), CRIT)
-    high, low = split(joint)
+    joint = jnp.dot(full_out, head_in, preferred_element_type=F32)
+    high, low = split(lax.psum_scatter(joint, "fsdp", scatter_dimension=0, tiled=True))
 
     def units_of(row_cols, heads):
         part = jnp.dot(row_cols, head_in, preferred_element_type=F32)
         part = part + jnp.dot(heads, high, preferred_element_type=F32)
-        part = part + jnp.dot(heads, low, preferred_element_type=F32)
-        return jnp.sum(gather_fsdp(part, CRIT), axis=(0, 1))
+        return part + jnp.dot(heads, low, preferred_element_type=F32)
 
     real_cols = lax.dynamic_slice_in_dim(first_rows, start, cols, 1)
-    real_score, real_unit = unit_terms(units_of(real_cols, first_heads), head_out)
-
-    (second_q, second_k, second_v), inverse = project(second_rows, gains, weights)
-    every = gather_seq(jnp.concatenate([second_k, second_v, second_q], axis=1), CRIT)
+
+    second_normed, inverse = normalised(second_rows, gains)
+    second_kv = times(second_normed, weights_kv)
+    second_k, second_v = second_kv[:, :width], second_kv[:, width:]
+    second_q = times(second_normed, weights_q)
+    every = gather_seq(jnp.concatenate([second_kv, second_q], axis=1), CRIT)
     every = every.reshape(tokens, 3 * width)
     second_heads, lse = critic_attention(second_q, every)
     second_cols = lax.dynamic_slice_in_dim(second_rows, start, cols, 1)
-    fake_score, fake_unit = unit_terms(units_of(second_cols, second_heads), head_out)
+    units = jnp.stack([units_of(real_cols, first_heads), units_of(second_cols, second_heads)])
+    units = jnp.sum(gather_fsdp(units, CRIT), axis=(0, 1))
+    real_score, real_unit = unit_terms(units[0], head_out)
+    fake_score, fake_unit = unit_terms(units[1], head_out)
     query_grad, sent = query_grads(
         second_q, every, lse, fake_unit, high, low, real_score - fake_score
     )
-    sent = gather_seq(sent, CRIT, direct4).reshape(tokens, 2 * HD)
+    sent = gather_seq(sent, CRIT).reshape(tokens, 2 * HD)
     key_grad, value_grad = key_grads(
         second_k, second_v, every[:, 2 * width :], sent, high, low
     )
-    row_terms = sum(
-        mm(grad, weights[c], 1, 1) for c, grad in enumerate((query_grad, key_grad, value_grad))
-    ).astype(BF16)
+    pair_grads = jnp.concatenate([key_grad, value_grad], axis=1)
+    row_terms = (mm(query_grad, weights_q, 1, 1) + mm(pair_grads, weights_kv, 1, 1)).astype(BF16)
     blocks = row_terms.reshape(rows, 4, 2, cols).transpose(1, 2, 0, 3)
     row_grad = scatter_fsdp(jnp.roll(blocks, (-x, -w), (0, 1)), CRIT)
     gain_cols = lax.dynamic_slice_in_dim(gains, start, cols, 0)
     direction = mm(fake_unit, head_in, 1, 1)
     input_grad = (inverse * row_grad * gain_cols + direction).astype(BF16)
 
-    four = ring4(input_grad, 1, CRIT)
-    back = jnp.stack([moved(four, along(0, k), CRIT, cross=True) for k in range(4)])
+    back = direct4(across(direct4(input_grad, 1, CRIT), CRIT), 0, GEN)
     back = back.reshape(tokens, cols)
     term_gen = mm(gen_heads, back, 0, 0)
 
     product = mm(second_heads, fake_unit, 0, 0) - mm(first_heads, real_unit, 0, 0)
-    product = ordered(gather_fsdp(product.astype(BF16), CRIT), x, w).reshape(4, 4, 192, -1)
-    product = swap_seq(jnp.roll(product, (-y, -z), (0, 1)), CRIT)
-    product_high, product_low = split(jnp.sum(product.astype(F32), axis=(0, 1)))
+    product = lax.all_gather(product, "fsdp", axis=0, tiled=True)
+    product = lax.psum_scatter(product, "seq", scatter_dimension=0, tiled=True)
+    product_high, product_low = split(product)
     term_crit = mm(product_high, head_in, 1, 1) + mm(product_low, head_in, 1, 1)
 
     stats = sent[:, HD:].astype(F32)
     margin = jnp.sum(stats[:, 18:21]) / tokens
-    margin_back = moved(jnp.broadcast_to(margin, (8, HD)), (0, 0, 0, 0), CRIT, cross=True)[0, 0]
+    margin_back = across(jnp.broadcast_to(margin, (8, HD)), CRIT)[0, 0]
     margin = jnp.where(is_gen, margin_back, margin)
     signed = jnp.where(is_gen, margin, -margin)
     factor = jnp.where(is_gen, -1.0, 1.0) * jax.nn.sigmoid(signed)

time: 585 us -> 609 us (1.041)
  the two profiles are of different devices: /device:TPU:6 before, /device:TPU:32 now
where the time goes in v3:
time: 609 us; the launch traced here: 600 us
  waiting for transfers between devices  407 us (67%)
  starting transfers between devices  84.6 us (14%)
  matrix products  33.2 us (5%)
  other arithmetic  22.3 us (4%)
  Pallas kernels  19.3 us (3%)
  between operations  18.6 us (3%)
  local copies, waits for them, and re-layouts  15 us (2%)
    all_gather x1, waiting for transfers between devices, local(): weights_kv = lax.all_gather(shard_kv, 'seq', axis=0, tiled=True)  109 us
    ppermute x49, starting transfers between devices, moved(): return lax.ppermute(value, AXES, pairs)  84.1 us
    ppermute x49, waiting for transfers between devices, moved(): return lax.ppermute(value, AXES, pairs)  79.3 us
    all_gather x1, waiting for transfers between devices, local(): weights_q = lax.all_gather(shard_q, 'seq', axis=0, tiled=True)  56.8 us
    reduce_scatter x1, waiting for transfers between devices, local(): lax.psum_scatter(joint, 'fsdp', scatter_dimension=0, tiled=True)  52.4 us
    all_gather x1, waiting for transfers between devices, local(): product = lax.all_gather(product, 'fsdp', axis=0, tiled=True)  49.1 us
    all_gather x1, waiting for transfers between devices, local(): full_out = lax.all_gather(out_weights[0], 'seq', axis=0, tiled=True)  38.5 us
    reduce_scatter x1, waiting for transfers between devices, local(): product = lax.psum_scatter(product, 'seq', scatter_dimension=0, tiled=True)  20.6 us
  transfers between devices with their start and end apart: 55, of which 17 were waited for; matrix products, arithmetic and copies ran while one was open for 9% of the time, Pallas kernels for 3%

profile of v3, /device:TPU:32, one launch (start us, length us, event | category | flops | bytes accessed | tf_op | source)
XLA Modules:
  0.0 600.4 jit_solution(11983633238026388503)
XLA Ops:
  11.8 3.4 fusion.10
  15.2 109.2 %all-gather.7.cloned.1.call-done = bf16[5120,768]{1,0:T(8,128)(2,1)} async-done(((bf16[320,768]{1,0:T(8,128)(2,1)}), bf16[5120,768]{1,0:T(8,128)(2,1)}) %all-gather.7.cloned.1.call-update) | async-done | bytes 7864336 | tf_op jit(solution)/shard_map/all_gather | solution.py:287
  124.5 4.9 convolution_convert_fusion.1
  131.2 3.2 collective-permute-start.1
  134.9 3.6 collective-permute-done.2
  138.5 19.1 %collective-permute-done.1 = bf16[128,768]{1,0:T(8,128)(2,1)S(1)} collective-permute-done((bf16[128,768]{1,0:T(8,128)(2,1)S(1)}, bf16[128,768]{1,0:T(8,128)(2,1)S(1)}, u32[]{:S(2)}, u32[]{:S(2)}) %collective-permute-start.1) | collective-permute-done | bytes 196640 | tf_op jit(solution)/shard_map/ppermute | solution.py:33
  165.1 56.8 %all-gather.11.cloned.1.call-done = bf16[1,1,5120,384]{3,2,1,0:T(8,128)(2,1)} async-done(((bf16[1,1,320,384]{3,2,1,0:T(8,128)(2,1)}), bf16[1,1,5120,384]{3,2,1,0:T(8,128)(2,1)}) %all-gather.11.cloned.1.call-update) | async-done | bytes 3932176 | tf_op jit(solution)/shard_map/all_gather | solution.py:288
  222.0 3.0 fusion.54
  228.3 7.1 %conditional.1 = (bf16[128,384]{1,0:T(8,128)(2,1)S(1)}) conditional(s32[]{:T(128)} %convert_element_type.89, (bf16[128,384]{1,0:T(8,128)(2,1)S(1)}, bf16[2048,768]{1,0:T(8,128)(2,1)S(1)}) %tuple.54, (s32[3]{0:T(128)S(1)}, f32[2048]{0:T(1024)S(1)}, bf16[128,384]{1,0:T(8,128)(2,1)S(1)}, bf16[4,1024,384]{2,1,0:T(8,128)(2,1)S(1)}, ...), branch_computations={%region_1.2_spmd, %region_2.3_spmd} | conditional | bytes 73736 | solution.py:299
  228.3 7.1 %branch_1_fun.1 = bf16[128,384]{1,0:T(8,128)(2,1)S(1)} custom-call(s32[3]{0:T(128)S(1)} %get-tuple-element.47.frames, f32[8,2048]{1,0:T(8,128)S(1)} %broadcast_in_dim.72.mask, bf16[128,384]{1,0:T(8,128)(2,1)S(1)} %get-tuple-element.25.q, bf16[4,1024,384]{2,1,0:T(8,128)(2,1)S(1)} %get-tuple-element.48.k0.k1.k2, ...), custom_call_target="tpu_custom_call" | custom-call | tf_op jit(solution)/shard_map/cond/branch_1_fun/pallas_call | solution.py:114
  237.4 5.4 collective-permute-done.6
  242.8 4.6 collective-permute-start.7
  253.3 3.3 collective-permute-done.8
  260.1 38.5 %all-gather.13.cloned.1.call-done = bf16[1,3072,640]{2,1,0:T(8,128)(2,1)} async-done(((bf16[1,192,640]{2,1,0:T(8,128)(2,1)}), bf16[1,3072,640]{2,1,0:T(8,128)(2,1)}) %all-gather.13.cloned.1.call-update) | async-done | bytes 3932176 | tf_op jit(solution)/shard_map/all_gather | solution.py:289
  298.6 3.1 fusion.48
  325.9 52.4 %reduce-scatter.3.cloned.1.call-done = f32[384,128]{1,0:T(8,128)} async-done(((f32[3072,128]{1,0:T(8,128)}), f32[384,128]{1,0:T(8,128)}) %reduce-scatter.3.cloned.1.call-update) | async-done | bytes 196624 | tf_op jit(solution)/shard_map/reduce_scatter | solution.py:317
  380.8 4.0 pad_maximum_fusion
  384.8 4.3 shard_map.125
  394.1 4.6 shard_map.126
  404.7 3.3 shard_map.127
  408.0 6.0 fusion.82
  416.5 4.2 reshape.123
  423.8 49.1 %all-gather.9.cloned.1.call-done = f32[3072,128]{1,0:T(8,128)} async-done(((f32[384,128]{1,0:T(8,128)}), f32[3072,128]{1,0:T(8,128)}) %all-gather.9.cloned.1.call-update) | async-done | bytes 1572880 | tf_op jit(solution)/shard_map/all_gather | solution.py:358
  483.3 5.5 collective-permute-start.11
  491.2 4.6 collective-permute-start.12
  502.2 32.8 %collective-permute-done.44 = bf16[4,128,640]{2,1,0:T(8,128)(2,1)} collective-permute-done((bf16[4,128,640]{2,1,0:T(8,128)(2,1)S(1)}, bf16[4,128,640]{2,1,0:T(8,128)(2,1)}, u32[]{:S(2)}, u32[]{:S(2)}) %collective-permute-start.44) | collective-permute-done | bytes 655392 | tf_op jit(solution)/shard_map/ppermute | solution.py:33
  534.9 5.5 collective-permute-start.47
  545.3 3.8 collective-permute-start.15
  549.0 5.2 collective-permute-start.14
  555.6 20.6 %reduce-scatter.5.cloned.1.call-done = f32[192,128]{1,0:T(8,128)} async-done(((f32[3072,128]{1,0:T(8,128)}), f32[192,128]{1,0:T(8,128)}) %reduce-scatter.5.cloned.1.call-update) | async-done | bytes 98320 | tf_op jit(solution)/shard_map/reduce_scatter | solution.py:359
  577.3 3.5 collective-permute-start.13
  581.9 7.2 %collective-permute-done.13 = bf16[4,128,192]{1,2,0:T(8,128)(2,1)S(1)} collective-permute-done((bf16[4,128,192]{1,2,0:T(8,128)(2,1)S(1)}, bf16[4,128,192]{1,2,0:T(8,128)(2,1)S(1)}, u32[]{:S(2)}, u32[]{:S(2)}) %collective-permute-start.13) | collective-permute-done | bytes 196640 | tf_op jit(solution)/shard_map/ppermute | solution.py:33
  (202 shorter events, 100.2 us)
Async XLA Ops:
  7.2 117.3 %all-gather.7.cloned.1.call-start = ((), (), s32[]{:S(2)}) async-start(), calls=%async_computation.2 | async-start | bytes 8355840 | tf_op jit(solution)/shard_map/all_gather | solution.py:287
  10.3 211.7 %all-gather.11.cloned.1.call-start = ((), (), s32[]{:S(2)}) async-start(), calls=%async_computation.6 | async-start | bytes 4177920 | tf_op jit(solution)/shard_map/all_gather | solution.py:288
  11.0 287.6 %all-gather.13.cloned.1.call-start = ((), (), s32[]{:S(2)}) async-start(), calls=%async_computation.7 | async-start | bytes 4177920 | tf_op jit(solution)/shard_map/all_gather | solution.py:289
  11.7 366.6 %reduce-scatter.3.cloned.1.call-start = ((), (), s32[]{:S(2)}) async-start(), calls=%async_computation.3 | async-start | bytes 1769472 | tf_op jit(solution)/shard_map/reduce_scatter | solution.py:317
  129.4 9.1 %collective-permute-start.2 = (bf16[128,768]{1,0:T(8,128)(2,1)S(1)}, bf16[128,768]{1,0:T(8,128)(2,1)S(1)}, u32[]{:S(2)}, u32[]{:S(2)}) collective-permute-start(bf16[128,768]{1,0:T(8,128)(2,1)S(1)} %convolution_convert_fusion.1), channel_id=1, source_target_pairs={{0,24},{1,25},{2,26},{3,27},{4,28},{5,29},{6,30},{7,31},{8,0},{9,1... | collective-permute-start | bytes 589832 | tf_op jit(solution)/shard_map/ppermute | solution.py:33
  131.2 26.5 %collective-permute-start.1 = (bf16[128,768]{1,0:T(8,128)(2,1)S(1)}, bf16[128,768]{1,0:T(8,128)(2,1)S(1)}, u32[]{:S(2)}, u32[]{:S(2)}) collective-permute-start(bf16[128,768]{1,0:T(8,128)(2,1)S(1)} %convolution_convert_fusion.1), channel_id=1, source_target_pairs={{0,16},{1,17},{2,18},{3,19},{4,20},{5,21},{6,22},{7,23},{8,24},{9,... | collective-permute-start | bytes 589832 | tf_op jit(solution)/shard_map/ppermute | solution.py:33
  134.3 24.3 %collective-permute-start = (bf16[128,768]{1,0:T(8,128)(2,1)S(1)}, bf16[128,768]{1,0:T(8,128)(2,1)S(1)}, u32[]{:S(2)}, u32[]{:S(2)}) collective-permute-start(bf16[128,768]{1,0:T(8,128)(2,1)S(1)} %convolution_convert_fusion.1), channel_id=1, source_target_pairs={{0,8},{1,9},{2,10},{3,11},{4,12},{5,13},{6,14},{7,15},{8,16},{9,17... | collective-permute-start | bytes 589832 | tf_op jit(solution)/shard_map/ppermute | solution.py:33
  159.8 65.2 %collective-permute-start.4 = (bf16[4,128,768]{2,1,0:T(8,128)(2,1)}, bf16[4,128,768]{2,1,0:T(8,128)(2,1)S(1)}, u32[]{:S(2)}, u32[]{:S(2)}) collective-permute-start(bf16[4,128,768]{2,1,0:T(8,128)(2,1)} %get-tuple-element.68), channel_id=1, source_target_pairs={{0,64},{1,65},{2,66},{3,67},{4,68},{5,69},{6,70},{7,71},{8,72},{9,... | collective-permute-start | bytes 2359304 | tf_op jit(solution)/shard_map/ppermute | solution.py:33
  161.9 63.1 %collective-permute-start.3 = (bf16[4,128,768]{2,1,0:T(8,128)(2,1)}, bf16[4,128,768]{2,1,0:T(8,128)(2,1)}, u32[]{:S(2)}, u32[]{:S(2)}) collective-permute-start(bf16[4,128,768]{2,1,0:T(8,128)(2,1)} %get-tuple-element.68), channel_id=1, source_target_pairs={{0,32},{1,33},{2,34},{3,35},{4,36},{5,37},{6,38},{7,39},{8,40},{9,... | collective-permute-start | bytes 2359304 | tf_op jit(solution)/shard_map/ppermute | solution.py:33
  164.9 60.1 %collective-permute-start.5 = (bf16[4,128,768]{2,1,0:T(8,128)(2,1)}, bf16[4,128,768]{2,1,0:T(8,128)(2,1)}, u32[]{:S(2)}, u32[]{:S(2)}) collective-permute-start(bf16[4,128,768]{2,1,0:T(8,128)(2,1)} %get-tuple-element.68), channel_id=1, source_target_pairs={{0,96},{1,97},{2,98},{3,99},{4,100},{5,101},{6,102},{7,103},{8,104... | collective-permute-start | bytes 2359304 | tf_op jit(solution)/shard_map/ppermute | solution.py:33
  235.5 7.3 %collective-permute-start.6 = (bf16[128,384]{1,0:T(8,128)(2,1)S(1)}, bf16[128,384]{1,0:T(8,128)(2,1)S(1)}, u32[]{:S(2)}, u32[]{:S(2)}) collective-permute-start(bf16[128,384]{1,0:T(8,128)(2,1)S(1)} %get-tuple-element.87), channel_id=1, source_target_pairs={{0,1},{1,0},{2,3},{3,2},{4,5},{5,4},{6,7},{7,6},{8,9},{9,8},{10,11... | collective-permute-start | bytes 294920 | tf_op jit(solution)/shard_map/ppermute | solution.py:33
  242.8 10.4 %collective-permute-start.7 = (bf16[2,128,384]{2,1,0:T(8,128)(2,1)S(1)}, bf16[2,128,384]{2,1,0:T(8,128)(2,1)S(1)}, u32[]{:S(2)}, u32[]{:S(2)}) collective-permute-start(bf16[2,128,384]{2,1,0:T(8,128)(2,1)S(1)} %pad_maximum_fusion.12), channel_id=1, source_target_pairs={{0,6},{1,7},{2,0},{3,1},{4,2},{5,3},{6,4},{7,5},{8,14},{9,15},{10,... | collective-permute-start | bytes 589832 | tf_op jit(solution)/shard_map/ppermute | solution.py:33
  247.5 9.1 %collective-permute-start.8 = (bf16[2,128,384]{2,1,0:T(8,128)(2,1)S(1)}, bf16[2,128,384]{2,1,0:T(8,128)(2,1)S(1)}, u32[]{:S(2)}, u32[]{:S(2)}) collective-permute-start(bf16[2,128,384]{2,1,0:T(8,128)(2,1)S(1)} %pad_maximum_fusion.12), channel_id=1, source_target_pairs={{0,4},{1,5},{2,6},{3,7},{4,0},{5,1},{6,2},{7,3},{8,12},{9,13},{10,... | collective-permute-start | bytes 589832 | tf_op jit(solution)/shard_map/ppermute | solution.py:33
  250.3 8.8 %collective-permute-start.9 = (bf16[2,128,384]{2,1,0:T(8,128)(2,1)S(1)}, bf16[2,128,384]{2,1,0:T(8,128)(2,1)S(1)}, u32[]{:S(2)}, u32[]{:S(2)}) collective-permute-start(bf16[2,128,384]{2,1,0:T(8,128)(2,1)S(1)} %pad_maximum_fusion.12), channel_id=1, source_target_pairs={{0,2},{1,3},{2,4},{3,5},{4,6},{5,7},{6,0},{7,1},{8,10},{9,11},{10,... | collective-permute-start | bytes 589832 | tf_op jit(solution)/shard_map/ppermute | solution.py:33
  305.2 4.5 collective-permute-start.19
  305.9 3.9 collective-permute-start.18
  309.6 163.3 %all-gather.9.cloned.1.call-start = ((), (), s32[]{:S(2)}) async-start(), calls=%async_computation.4 | async-start | bytes 1769472 | tf_op jit(solution)/shard_map/all_gather | solution.py:358
  319.7 61.0 %collective-permute-start.25 = (bf16[4,128,1152]{2,1,0:T(8,128)(2,1)}, bf16[4,128,1152]{2,1,0:T(8,128)(2,1)}, u32[]{:S(2)}, u32[]{:S(2)}) collective-permute-start(bf16[4,128,1152]{2,1,0:T(8,128)(2,1)} %get-tuple-element.58), channel_id=1, source_target_pairs={{128,192},{129,193},{130,194},{131,195},{132,196},{133,197},{134,1... | collective-permute-start | bytes 3538952 | tf_op jit(solution)/shard_map/ppermute | solution.py:33
  321.4 59.3 %collective-permute-start.24 = (bf16[4,128,1152]{2,1,0:T(8,128)(2,1)}, bf16[4,128,1152]{2,1,0:T(8,128)(2,1)}, u32[]{:S(2)}, u32[]{:S(2)}) collective-permute-start(bf16[4,128,1152]{2,1,0:T(8,128)(2,1)} %get-tuple-element.58), channel_id=1, source_target_pairs={{128,160},{129,161},{130,162},{131,163},{132,164},{133,165},{134,1... | collective-permute-start | bytes 3538952 | tf_op jit(solution)/shard_map/ppermute | solution.py:33
  323.2 57.6 %collective-permute-start.26 = (bf16[4,128,1152]{2,1,0:T(8,128)(2,1)}, bf16[4,128,1152]{2,1,0:T(8,128)(2,1)}, u32[]{:S(2)}, u32[]{:S(2)}) collective-permute-start(bf16[4,128,1152]{2,1,0:T(8,128)(2,1)} %get-tuple-element.58), channel_id=1, source_target_pairs={{128,224},{129,225},{130,226},{131,227},{132,228},{133,229},{134,2... | collective-permute-start | bytes 3538952 | tf_op jit(solution)/shard_map/ppermute | solution.py:33
  393.7 182.5 %reduce-scatter.5.cloned.1.call-start = ((), (), s32[]{:S(2)}) async-start(), calls=%async_computation.5 | async-start | bytes 1671168 | tf_op jit(solution)/shard_map/reduce_scatter | solution.py:359
  481.9 53.0 %collective-permute-start.44 = (bf16[4,128,640]{2,1,0:T(8,128)(2,1)S(1)}, bf16[4,128,640]{2,1,0:T(8,128)(2,1)}, u32[]{:S(2)}, u32[]{:S(2)}) collective-permute-start(bf16[4,128,640]{2,1,0:T(8,128)(2,1)S(1)} %pad_maximum_fusion.6), channel_id=1, source_target_pairs={{128,0},{129,1},{130,2},{131,3},{132,4},{133,5},{134,6},{135,7},{1... | collective-permute-start | bytes 1966088 | tf_op jit(solution)/shard_map/ppermute | solution.py:33
  483.3 12.5 %collective-permute-start.11 = (bf16[4,128,192]{1,2,0:T(8,128)(2,1)S(1)}, bf16[4,128,192]{1,2,0:T(8,128)(2,1)S(1)}, u32[]{:S(2)}, u32[]{:S(2)}) collective-permute-start(bf16[4,128,192]{1,2,0:T(8,128)(2,1)S(1)} %get-tuple-element.64), channel_id=1, source_target_pairs={{0,64},{1,65},{2,66},{3,67},{4,68},{5,69},{6,70},{7,71},{8,72},{9,... | collective-permute-start | bytes 589832 | tf_op jit(solution)/shard_map/ppermute | solution.py:33
  488.7 9.3 %collective-permute-start.10 = (bf16[4,128,192]{1,2,0:T(8,128)(2,1)S(1)}, bf16[4,128,192]{1,2,0:T(8,128)(2,1)S(1)}, u32[]{:S(2)}, u32[]{:S(2)}) collective-permute-start(bf16[4,128,192]{1,2,0:T(8,128)(2,1)S(1)} %get-tuple-element.65), channel_id=1, source_target_pairs={{0,32},{1,33},{2,34},{3,35},{4,36},{5,37},{6,38},{7,39},{8,40},{9,... | collective-permute-start | bytes 589832 | tf_op jit(solution)/shard_map/ppermute | solution.py:33
  491.2 7.9 %collective-permute-start.12 = (bf16[4,128,192]{1,2,0:T(8,128)(2,1)S(1)}, bf16[4,128,192]{1,2,0:T(8,128)(2,1)S(1)}, u32[]{:S(2)}, u32[]{:S(2)}) collective-permute-start(bf16[4,128,192]{1,2,0:T(8,128)(2,1)S(1)} %get-tuple-element.66), channel_id=1, source_target_pairs={{0,96},{1,97},{2,98},{3,99},{4,100},{5,101},{6,102},{7,103},{8,104... | collective-permute-start | bytes 589832 | tf_op jit(solution)/shard_map/ppermute | solution.py:33
  500.9 48.1 %collective-permute-start.48 = (f32[8,128]{1,0:T(8,128)S(1)}, f32[8,128]{1,0:T(8,128)S(1)}, u32[]{:S(2)}, u32[]{:S(2)}) collective-permute-start(f32[8,128]{1,0:T(8,128)S(1)} %broadcast_in_dim.69), channel_id=1, source_target_pairs={{128,0},{129,1},{130,2},{131,3},{132,4},{133,5},{134,6},{135,7},{1... | collective-permute-start | bytes 12296 | tf_op jit(solution)/shard_map/ppermute | solution.py:33
  534.9 54.2 %collective-permute-start.47 = (bf16[4,128,640]{2,1,0:T(8,128)(2,1)}, bf16[4,128,640]{2,1,0:T(8,128)(2,1)S(1)}, u32[]{:S(2)}, u32[]{:S(2)}) collective-permute-start(bf16[4,128,640]{2,1,0:T(8,128)(2,1)} %collective-permute-done.44), channel_id=1, source_target_pairs={{0,96},{1,97},{2,98},{3,99},{4,100},{5,101},{6,102},{7,103},{8,104... | collective-permute-start | bytes 1966088 | tf_op jit(solution)/shard_map/ppermute | solution.py:33
  540.5 48.6 %collective-permute-start.46 = (bf16[4,128,640]{2,1,0:T(8,128)(2,1)}, bf16[4,128,640]{2,1,0:T(8,128)(2,1)S(1)}, u32[]{:S(2)}, u32[]{:S(2)}) collective-permute-start(bf16[4,128,640]{2,1,0:T(8,128)(2,1)} %collective-permute-done.44), channel_id=1, source_target_pairs={{0,64},{1,65},{2,66},{3,67},{4,68},{5,69},{6,70},{7,71},{8,72},{9,... | collective-permute-start | bytes 1966088 | tf_op jit(solution)/shard_map/ppermute | solution.py:33
  542.4 46.7 %collective-permute-start.45 = (bf16[4,128,640]{2,1,0:T(8,128)(2,1)}, bf16[4,128,640]{2,1,0:T(8,128)(2,1)}, u32[]{:S(2)}, u32[]{:S(2)}) collective-permute-start(bf16[4,128,640]{2,1,0:T(8,128)(2,1)} %collective-permute-done.44), channel_id=1, source_target_pairs={{0,32},{1,33},{2,34},{3,35},{4,36},{5,37},{6,38},{7,39},{8,40},{9,... | collective-permute-start | bytes 1966088 | tf_op jit(solution)/shard_map/ppermute | solution.py:33
  545.3 32.1 %collective-permute-start.15 = (bf16[4,128,192]{1,2,0:T(8,128)(2,1)S(1)}, bf16[4,128,192]{1,2,0:T(8,128)(2,1)S(1)}, u32[]{:S(2)}, u32[]{:S(2)}) collective-permute-start(bf16[4,128,192]{1,2,0:T(8,128)(2,1)S(1)} %get-tuple-element.60), channel_id=1, source_target_pairs={{0,24},{1,25},{2,26},{3,27},{4,28},{5,29},{6,30},{7,31},{8,0},{9,1... | collective-permute-start | bytes 589832 | tf_op jit(solution)/shard_map/ppermute | solution.py:33
  549.0 32.9 %collective-permute-start.14 = (bf16[4,128,192]{1,2,0:T(8,128)(2,1)S(1)}, bf16[4,128,192]{1,2,0:T(8,128)(2,1)S(1)}, u32[]{:S(2)}, u32[]{:S(2)}) collective-permute-start(bf16[4,128,192]{1,2,0:T(8,128)(2,1)S(1)} %get-tuple-element.61), channel_id=1, source_target_pairs={{0,16},{1,17},{2,18},{3,19},{4,20},{5,21},{6,22},{7,23},{8,24},{9,... | collective-permute-start | bytes 589832 | tf_op jit(solution)/shard_map/ppermute | solution.py:33
  577.3 11.8 %collective-permute-start.13 = (bf16[4,128,192]{1,2,0:T(8,128)(2,1)S(1)}, bf16[4,128,192]{1,2,0:T(8,128)(2,1)S(1)}, u32[]{:S(2)}, u32[]{:S(2)}) collective-permute-start(bf16[4,128,192]{1,2,0:T(8,128)(2,1)S(1)} %get-tuple-element.62), channel_id=1, source_target_pairs={{0,8},{1,9},{2,10},{3,11},{4,12},{5,13},{6,14},{7,15},{8,16},{9,17... | collective-permute-start | bytes 589832 | tf_op jit(solution)/shard_map/ppermute | solution.py:33
  (38 other events, 595.0 us)
Sparse Core Ops, SparseCore 0:
  10.5 113.9 all-gather.6
  127.5 94.3 all-gather.10
  224.4 74.0 all-gather.12
  309.8 68.5 reduce-scatter.2
  393.8 79.0 all-gather.8
  476.3 99.8 reduce-scatter.4

commit v4 on v3

--- a/solution.py
+++ b/solution.py
@@ -43,8 +43,16 @@
     return jnp.stack([value] + [moved(value, along(axis, k), groups) for k in (1, 2, 3)])
 
 
-def gather_seq(value, groups):
-    return direct4(direct4(value, 1, groups), 0, groups).reshape((4, 4) + value.shape)
+def gather_seq(lead, tail, groups):
+    lead, tail = direct4(lead, 1, groups), direct4(tail, 0, groups)
+    lead = direct4(lead, 0, groups)
+    tail = jnp.stack([tail] + [moved(tail, along(1, k), groups) for k in (1, 2, 3)], axis=1)
+    return [part.reshape((-1, part.shape[-1])) for part in (lead, tail)]
+
+
+def spread(value, axis):
+    count = lax.axis_size(axis)
+    return lax.all_to_all(jnp.broadcast_to(value[None], (count,) + value.shape), axis, 0, 0)
 
 
 def gather_fsdp(value, groups):
@@ -57,13 +65,6 @@
     rows = jnp.stack(rows)
     cols = [rows[:, 0]] + [moved(rows[:, k], along(1, k), groups) for k in (1, 2, 3)]
     return jnp.stack(cols, axis=1)
-
-
-def scatter_fsdp(blocks, groups):
-    total = blocks[0].astype(F32)
-    for k in (2, 1, 3):
-        total = total + moved(blocks[k], along(2, k), groups).astype(F32)
-    return total[0] + moved(total[1], along(3, 1), groups)
 
 
 def across(value, groups):
@@ -103,10 +104,10 @@
     out[...] = result.astype(BF16)
 
 
-def generator_attention(frames, mask, query, cache_keys, cache_values, key_value):
+def generator_attention(frames, mask, query, cache_keys, cache_values, own_keys, own_values):
     rows, width = query.shape
     heads = width // HD
-    count, length = key_value.shape[0], cache_keys.shape[1]
+    count, length = own_keys.shape[0], cache_keys.shape[1]
 
     def picked(i):
         return pl.BlockSpec((1, length, HD), lambda h, f: (f[i], 0, h))
@@ -126,7 +127,7 @@
                 picked(1),
                 picked(2),
                 pl.BlockSpec((count, HD), lambda h, f: (0, h)),
-                pl.BlockSpec((count, HD), lambda h, f: (0, heads + h)),
+                pl.BlockSpec((count, HD), lambda h, f: (0, h)),
             ],
             out_specs=pl.BlockSpec((rows, HD), lambda h, f: (0, h)),
         ),
@@ -136,52 +137,52 @@
         frames, mask, query,
         cache_keys, cache_keys, cache_keys,
         cache_values, cache_values, cache_values,
-        key_value, key_value,
-    )
-
-
-def critic_kernel(q, k, v, out, lse):
-    scores = mm(q[...], k[...], 1, 1) * HD ** (-0.5)
-    top = scores.max(axis=-1, keepdims=True)
-    raised = jnp.exp(scores - top)
-    total = raised.sum(axis=-1, keepdims=True)
-    out[...] = mm((raised * (1.0 / total)).astype(BF16), v[...], 1, 0).astype(BF16)
-    lse[...] = jnp.broadcast_to(top + jnp.log(total), lse.shape)
-
-
-def critic_attention(query, key_value):
-    rows, width = query.shape
-    heads, count = width // HD, key_value.shape[0]
-    own = pl.BlockSpec((rows, HD), lambda h: (0, h))
+        own_keys, own_values,
+    )
+
+
+def column(lead, tail, index):
+    count = lead.shape[1] // HD
+    ref, index = (lead, index) if index < count else (tail, index - count)
+    return ref[:, index * HD : (index + 1) * HD]
+
+
+def critic_kernel(q, lead, tail, out, lse):
+    heads = q.shape[1] // HD
+    for head in range(heads):
+        here = slice(head * HD, (head + 1) * HD)
+        scores = mm(q[:, here], column(lead, tail, head), 1, 1) * HD ** (-0.5)
+        top = scores.max(axis=-1, keepdims=True)
+        raised = jnp.exp(scores - top)
+        total = raised.sum(axis=-1, keepdims=True)
+        weights = (raised * (1.0 / total)).astype(BF16)
+        out[:, here] = mm(weights, column(lead, tail, heads + head), 1, 0).astype(BF16)
+        lse[:, here] = jnp.broadcast_to(top + jnp.log(total), (q.shape[0], HD))
+
+
+def critic_attention(query, lead, tail):
     return pl.pallas_call(
         critic_kernel,
-        grid=(heads,),
-        in_specs=[
-            own,
-            pl.BlockSpec((count, HD), lambda h: (0, h)),
-            pl.BlockSpec((count, HD), lambda h: (0, heads + h)),
-        ],
-        out_specs=(own, own),
         out_shape=(
-            jax.ShapeDtypeStruct((rows, width), BF16),
-            jax.ShapeDtypeStruct((rows, width), F32),
+            jax.ShapeDtypeStruct(query.shape, BF16),
+            jax.ShapeDtypeStruct(query.shape, F32),
         ),
         compiler_params=VMEM,
-    )(query, key_value, key_value)
-
-
-def query_kernel(q, kv, lse, u, high, low, score, grad, sent):
+    )(query, lead, tail)
+
+
+def query_kernel(q, lead, tail, lse, u, high, low, score, grad, sent):
     scale = HD ** (-0.5)
     width = q.shape[1]
     unit = u[...]
     stats = []
-    for start in range(0, width, HD):
+    for head, start in enumerate(range(0, width, HD)):
         here = slice(start, start + HD)
-        keys = kv[:, here]
+        keys = column(lead, tail, head)
         head_grad = (mm(unit, high[here, :], 1, 1) + mm(unit, low[here, :], 1, 1)).astype(BF16)
         logs = lse[:, start : start + 1]
         weights = jnp.exp(mm(q[:, here], keys, 1, 1) * scale - logs)
-        slopes = mm(head_grad, kv[:, width + start : width + start + HD], 1, 1)
+        slopes = mm(head_grad, column(lead, tail, width // HD + head), 1, 1)
         centred = jnp.sum(slopes * weights, axis=-1, keepdims=True)
         score_grad = (weights * (slopes - centred)).astype(BF16)
         grad[:, here] = (mm(score_grad, keys, 1, 0) * scale).astype(BF16)
@@ -198,7 +199,7 @@
     sent[:, HD:] = table.astype(BF16)
 
 
-def query_grads(query, key_value, lse, unit, high, low, score):
+def query_grads(query, lead, tail, lse, unit, high, low, score):
     rows, width = query.shape
     return pl.pallas_call(
         query_kernel,
@@ -207,21 +208,28 @@
             jax.ShapeDtypeStruct((rows, 2 * HD), BF16),
         ),
         compiler_params=VMEM,
-    )(query, key_value, lse, unit, high, low, score)
-
-
-def key_kernel(k, v, q, sent, high, low, key_grad, value_grad):
+    )(query, lead, tail, lse, unit, high, low, score)
+
+
+def key_kernel(at, k, v, tail, sent, high, low, key_grad, value_grad, ordered_sent):
     scale = HD ** (-0.5)
-    width = k.shape[1]
-    unit = sent[:, :HD]
-    table = sent[:, HD:].astype(F32)
+    rows, width = k.shape
+    y, z = at[0] // 4, at[0] % 4
+    for dy in range(4):
+        for dz in range(4):
+            place = ((y + 4 - dy) % 4) * 4 + (z + 4 - dz) % 4
+            block = (4 * dy + dz) * rows
+            ordered_sent[block : block + rows, :] = sent[pl.ds(place, 1)][0]
+    unit = ordered_sent[:, :HD]
+    table = ordered_sent[:, HD:].astype(F32)
 
     def stat(i):
         return table[:, 3 * i : 3 * i + 1] + table[:, 3 * i + 1 : 3 * i + 2] + table[:, 3 * i + 2 : 3 * i + 3]
 
+    first = tail.shape[1] - width
     for head, start in enumerate(range(0, width, HD)):
         here = slice(start, start + HD)
-        queries = q[:, here]
+        queries = tail[:, first + start : first + start + HD]
         head_grad = (mm(unit, high[here, :], 1, 1) + mm(unit, low[here, :], 1, 1)).astype(BF16)
         weights = jnp.exp(mm(queries, k[:, here], 1, 1) * scale - stat(2 * head + 1))
         slopes = mm(head_grad, v[:, here], 1, 1)
@@ -230,11 +238,16 @@
         value_grad[:, here] = mm(weights.astype(BF16), head_grad, 0, 0).astype(BF16)
 
 
-def key_grads(keys, values, queries, sent, high, low):
+def key_grads(at, keys, values, tail, sent, high, low):
     shape = jax.ShapeDtypeStruct(keys.shape, BF16)
-    return pl.pallas_call(key_kernel, out_shape=(shape, shape), compiler_params=VMEM)(
-        keys, values, queries, sent, high, low
-    )
+    whole = pl.BlockSpec(memory_space=pltpu.VMEM)
+    return pl.pallas_call(
+        key_kernel,
+        in_specs=[pl.BlockSpec(memory_space=pltpu.SMEM)] + [whole] * 6,
+        out_shape=(shape, shape),
+        scratch_shapes=[pltpu.VMEM((tail.shape[0], sent.shape[-1]), BF16)],
+        compiler_params=VMEM,
+    )(at, keys, values, tail, sent, high, low)
 
 
 def split(value):
@@ -282,32 +295,29 @@
     gains = norm_gains[0]
     start = fsdp_at * cols
 
-    shard_q, shard_k, shard_v = (attn_weights[0, c] for c in range(3))
-    shard_kv = jnp.concatenate([shard_k, shard_v], axis=1)
-    weights_kv = lax.all_gather(shard_kv, "seq", axis=0, tiled=True)
-    weights_q = lax.all_gather(shard_q, "seq", axis=0, tiled=True)
+    shard = jnp.concatenate([attn_weights[0, c] for c in range(3)], axis=1)
+    weights = lax.all_gather(shard, "seq", axis=0, tiled=True)
     full_out = lax.all_gather(out_weights[0], "seq", axis=0, tiled=True)
 
     real_rows = pick_rows(real_bank, real_pick)
     first_rows = jnp.where(is_gen, new_rows, real_rows)
     first_normed, _ = normalised(first_rows, gains)
-    first_kv = gather_seq(times(first_normed, weights_kv), (0, 1))
-    first_kv = first_kv.reshape(tokens, 2 * width)
-    first_q = times(first_normed, weights_q)
+    first = times(first_normed, weights)
+    first_q = first[:, :width]
+    first_k, first_v = gather_seq(first[:, width : 2 * width], first[:, 2 * width :], (0, 1))
     key_y = (y - jnp.arange(tokens) // (4 * rows)) % 4
     mask = jnp.broadcast_to((key_y // 2 <= y // 2).astype(F32)[None], (8, tokens))
     first_heads = lax.cond(
         is_gen,
         lambda a: generator_attention(*a),
-        lambda a: critic_attention(a[2], a[5])[0],
-        (cache_frames, mask, first_q, cache_keys, cache_values, first_kv),
-    )
-
-    gathered = ordered(gather_fsdp(first_heads, GEN), x, w).reshape(8, rows, width)
-    first_all = gathered.transpose(1, 0, 2).reshape(rows, 8 * width)
+        lambda a: critic_attention(a[2], a[5], a[6])[0],
+        (cache_frames, mask, first_q, cache_keys, cache_values, first_k, first_v),
+    )
+
+    first_all = spread(first_heads, "fsdp").transpose(1, 0, 2).reshape(rows, 8 * width)
     first_cols = lax.dynamic_slice_in_dim(first_rows, start, cols, 1).astype(F32)
     generated = (first_cols + jnp.dot(first_all, full_out, preferred_element_type=F32)).astype(BF16)
-    crossed = ordered(gather_fsdp(across(generated, GEN), CRIT), x, w).reshape(8, rows, cols)
+    crossed = spread(across(generated, GEN), "fsdp")
     second_rows = crossed.transpose(1, 0, 2).reshape(rows, model)
 
     to_seq = first_all.reshape(rows, 4, 4, 192).transpose(1, 2, 0, 3)
@@ -324,44 +334,50 @@
     real_cols = lax.dynamic_slice_in_dim(first_rows, start, cols, 1)
 
     second_normed, inverse = normalised(second_rows, gains)
-    second_kv = times(second_normed, weights_kv)
-    second_k, second_v = second_kv[:, :width], second_kv[:, width:]
-    second_q = times(second_normed, weights_q)
-    every = gather_seq(jnp.concatenate([second_kv, second_q], axis=1), CRIT)
-    every = every.reshape(tokens, 3 * width)
-    second_heads, lse = critic_attention(second_q, every)
+    second = times(second_normed, weights)
+    second_q, second_k, second_v = (second[:, c * width : (c + 1) * width] for c in range(3))
+    cut = width - HD
+    every_lead, every_tail = gather_seq(
+        jnp.concatenate([second_k, second_v[:, :cut]], axis=1),
+        jnp.concatenate([second_v[:, cut:], second_q], axis=1),
+        CRIT,
+    )
+    second_heads, lse = critic_attention(second_q, every_lead, every_tail)
     second_cols = lax.dynamic_slice_in_dim(second_rows, start, cols, 1)
     units = jnp.stack([units_of(real_cols, first_heads), units_of(second_cols, second_heads)])
-    units = jnp.sum(gather_fsdp(units, CRIT), axis=(0, 1))
+    units = jnp.sum(spread(units, "fsdp"), axis=0)
     real_score, real_unit = unit_terms(units[0], head_out)
     fake_score, fake_unit = unit_terms(units[1], head_out)
     query_grad, sent = query_grads(
-        second_q, every, lse, fake_unit, high, low, real_score - fake_score
-    )
-    sent = gather_seq(sent, CRIT).reshape(tokens, 2 * HD)
-    key_grad, value_grad = key_grads(
-        second_k, second_v, every[:, 2 * width :], sent, high, low
-    )
-    pair_grads = jnp.concatenate([key_grad, value_grad], axis=1)
-    row_terms = (mm(query_grad, weights_q, 1, 1) + mm(pair_grads, weights_kv, 1, 1)).astype(BF16)
-    blocks = row_terms.reshape(rows, 4, 2, cols).transpose(1, 2, 0, 3)
-    row_grad = scatter_fsdp(jnp.roll(blocks, (-x, -w), (0, 1)), CRIT)
+        second_q, every_lead, every_tail, lse, fake_unit, high, low, real_score - fake_score
+    )
+    sent = spread(sent, "seq")
+    at = jnp.reshape(seq_at, (1,)).astype(jnp.int32)
+    key_grad, value_grad = key_grads(at, second_k, second_v, every_tail, sent, high, low)
+    grads = jnp.concatenate([query_grad, key_grad, value_grad], axis=1)
+    row_terms = jnp.einsum(
+        "tk,bnk->btn", grads, weights.reshape(8, cols, 3 * width), preferred_element_type=F32
+    )
+    row_terms = lax.all_to_all(row_terms.astype(BF16), "fsdp", 0, 0)
+    row_grad = jnp.sum(row_terms.astype(F32), axis=0)
     gain_cols = lax.dynamic_slice_in_dim(gains, start, cols, 0)
     direction = mm(fake_unit, head_in, 1, 1)
     input_grad = (inverse * row_grad * gain_cols + direction).astype(BF16)
 
-    back = direct4(across(direct4(input_grad, 1, CRIT), CRIT), 0, GEN)
+    product = mm(second_heads, fake_unit, 0, 0) - mm(first_heads, real_unit, 0, 0)
+    product = across(after(product.astype(BF16), gen_heads), CRIT)
+    product = ordered(gather_fsdp(product, GEN), x, w).reshape(4, 4, 192, -1)
+    product = swap_seq(jnp.roll(product, (-y, -z), (0, 1)), GEN)
+    product = across(jnp.sum(product.astype(F32), axis=(0, 1)), GEN)
+    product_high, product_low = split(product)
+    term_crit = mm(product_high, head_in, 1, 1) + mm(product_low, head_in, 1, 1)
+
+    back = direct4(across(direct4(after(input_grad, product), 1, CRIT), CRIT), 0, GEN)
     back = back.reshape(tokens, cols)
     term_gen = mm(gen_heads, back, 0, 0)
 
-    product = mm(second_heads, fake_unit, 0, 0) - mm(first_heads, real_unit, 0, 0)
-    product = lax.all_gather(product, "fsdp", axis=0, tiled=True)
-    product = lax.psum_scatter(product, "seq", scatter_dimension=0, tiled=True)
-    product_high, product_low = split(product)
-    term_crit = mm(product_high, head_in, 1, 1) + mm(product_low, head_in, 1, 1)
-
-    stats = sent[:, HD:].astype(F32)
-    margin = jnp.sum(stats[:, 18:21]) / tokens
+    stats = sent[:, :, HD:].astype(F32)
+    margin = jnp.sum(stats[:, :, 18:21]) / tokens
     margin_back = across(jnp.broadcast_to(margin, (8, HD)), CRIT)[0, 0]
     margin = jnp.where(is_gen, margin_back, margin)
     signed = jnp.where(is_gen, margin, -margin)

time: 609 us -> 605 us (level)
  waiting for transfers between devices: 407 us -> 324 us
  starting transfers between devices: 84.6 us -> 147 us
  local copies, waits for them, and re-layouts: 15 us -> 26.2 us
    all_gather x3 -> x1, waiting for transfers between devices: 215 us -> 150 us  [local(): weights = lax.all_gather(shard, 'seq', axis=0, tiled=True)]
    ppermute x49 -> x51, waiting for transfers between devices: 79.3 us -> 119 us  [moved(): return lax.ppermute(value, AXES, pairs)]
    reduce_scatter x1, waiting for transfers between devices: 52.4 us -> 15.6 us  [local(): lax.psum_scatter(joint, 'fsdp', scatter_dimension=0, tiled=True)]
    ppermute x49 -> x51, starting transfers between devices: 84.1 us -> 117 us  [moved(): return lax.ppermute(value, AXES, pairs)]
    all_to_all x0 -> x5, starting transfers between devices: none -> 30.1 us  [the longest x4 26.3 us: spread(): lax.all_to_all(jnp.broadcast_to(value[None], (count,) + value.shape), axi...]
    reduce_scatter x1 -> x0, waiting for transfers between devices: 20.6 us -> none  [local(): product = lax.psum_scatter(product, 'seq', scatter_dimension=0, tiled=True)]
    all_to_all x0 -> x5, waiting for transfers between devices: none -> 13.3 us  [the longest x4 13.3 us: spread(): lax.all_to_all(jnp.broadcast_to(value[None], (count,) + value.shape), axi...]
    all_gather x1, waiting for transfers between devices: 38.5 us -> 25.6 us  [local(): full_out = lax.all_gather(out_weights[0], 'seq', axis=0, tiled=True)]
  transfers between devices with their start and end apart: 55 -> 59, of which waited for: 17 -> 27; matrix products, arithmetic and copies ran while one was open for 9% -> 10% of each run, Pallas kernels for 3% -> 2%
where the time goes in v4:
time: 605 us; the launch traced here: 595 us
  waiting for transfers between devices  324 us (54%)
  starting transfers between devices  147 us (24%)
  matrix products  38.4 us (6%)
  local copies, waits for them, and re-layouts  26.2 us (4%)
  other arithmetic  21.7 us (4%)
  between operations  19.3 us (3%)
  Pallas kernels  18.5 us (3%)
    all_gather x1, waiting for transfers between devices, local(): weights = lax.all_gather(shard, 'seq', axis=0, tiled=True)  150 us
    ppermute x51, waiting for transfers between devices, moved(): return lax.ppermute(value, AXES, pairs)  119 us
    ppermute x51, starting transfers between devices, moved(): return lax.ppermute(value, AXES, pairs)  117 us
    all_to_all x4, starting transfers between devices, spread(): lax.all_to_all(jnp.broadcast_to(value[None], (count,) + value.shape), axi...  26.3 us
    all_gather x1, waiting for transfers between devices, local(): full_out = lax.all_gather(out_weights[0], 'seq', axis=0, tiled=True)  25.6 us
    reduce_scatter x1, waiting for transfers between devices, local(): lax.psum_scatter(joint, 'fsdp', scatter_dimension=0, tiled=True)  15.6 us
    all_to_all x4, waiting for transfers between devices, spread(): lax.all_to_all(jnp.broadcast_to(value[None], (count,) + value.shape), axi...  13.3 us
    dot_general x2, matrix products, times(): return jnp.dot(a, b, preferred_element_type=F32).astype(BF16)  13 us
  transfers between devices with their start and end apart: 59, of which 27 were waited for; matrix products, arithmetic and copies ran while one was open for 10% of the time, Pallas kernels for 2%

profile of v4, /device:TPU:32, one launch (start us, length us, event | category | flops | bytes accessed | tf_op | source)
XLA Modules:
  0.0 595.3 jit_solution(16836804468949223758)
XLA Ops:
  13.8 149.6 %all-gather.4.cloned.1.call-done = bf16[5120,1152]{1,0:T(8,128)(2,1)} async-done(((bf16[320,1152]{1,0:T(8,128)(2,1)}), bf16[5120,1152]{1,0:T(8,128)(2,1)}) %all-gather.4.cloned.1.call-update) | async-done | bytes 11796496 | tf_op jit(solution)/shard_map/all_gather | solution.py:299
  163.4 6.7 %convolution_convert_fusion.1 = bf16[128,1152]{1,0:T(8,128)(2,1)S(1)} fusion(bf16[5120,1152]{1,0:T(8,128)(2,1)} %all-gather.4.cloned.1.call-done, bf16[128,5120]{1,0:T(8,128)(2,1)} %get-tuple-element.58, f32[5120]{0:T(1024)S(1)} %bitcast.294, f32[128]{0:T(128)S(1)} %add_rsqrt_fusion.1), kind=kOutput, calls=%fused_computation.22 | convolution fusion | flops 1512718336 | bytes 13423104 | tf_op jit(solution)/shard_map/dot_general | solution.py:265
  190.4 20.4 %collective-permute-done.1 = bf16[128,384]{1,0:T(8,128)(2,1)S(1)} collective-permute-done((bf16[128,384]{1,0:T(8,128)(2,1)S(1)}, bf16[128,384]{1,0:T(8,128)(2,1)S(1)}, u32[]{:S(2)}, u32[]{:S(2)}) %collective-permute-start.1) | collective-permute-done | bytes 98336 | tf_op jit(solution)/shard_map/ppermute | solution.py:33
  210.8 13.6 %collective-permute-done = bf16[128,384]{1,0:T(8,128)(2,1)S(1)} collective-permute-done((bf16[128,384]{1,0:T(8,128)(2,1)S(1)}, bf16[128,384]{1,0:T(8,128)(2,1)S(1)}, u32[]{:S(2)}, u32[]{:S(2)}) %collective-permute-start) | collective-permute-done | bytes 98336 | tf_op jit(solution)/shard_map/ppermute | solution.py:33
  234.2 4.9 collective-permute-done.4
  239.1 7.0 %collective-permute-done.3 = bf16[4,128,384]{2,1,0:T(8,128)(2,1)S(1)} collective-permute-done((bf16[4,128,384]{2,1,0:T(8,128)(2,1)}, bf16[4,128,384]{2,1,0:T(8,128)(2,1)S(1)}, u32[]{:S(2)}, u32[]{:S(2)}) %collective-permute-start.3) | collective-permute-done | bytes 393248 | tf_op jit(solution)/shard_map/ppermute | solution.py:33
  249.2 7.1 %conditional.1 = (bf16[128,384]{1,0:T(8,128)(2,1)S(1)}) conditional(s32[]{:T(128)} %convert_element_type.96, (bf16[128,384]{1,0:T(8,128)(2,1)S(1)}, bf16[2048,384]{1,0:T(8,128)(2,1)S(1)}, bf16[2048,384]{1,0:T(8,128)(2,1)S(1)}) %tuple.60, (s32[3]{0:T(128)S(1)}, f32[2048]{0:T(1024)S(1)}, bf16[128,384]{1,0:T(8,128)(2,1)S(1)}, ...), branch_computations={%region_1.2_spmd, %region_2.3_spmd} | conditional | bytes 73736 | solution.py:310
  249.3 7.1 %branch_1_fun.1 = bf16[128,384]{1,0:T(8,128)(2,1)S(1)} custom-call(s32[3]{0:T(128)S(1)} %get-tuple-element.52.frames, f32[8,2048]{1,0:T(8,128)S(1)} %broadcast_in_dim.45.mask, bf16[128,384]{1,0:T(8,128)(2,1)S(1)} %get-tuple-element.29.q, bf16[4,1024,384]{2,1,0:T(8,128)(2,1)S(1)} %get-tuple-element.53.k0.k1.k2, ...), custom_call_target="tpu_custom_call" | custom-call | tf_op jit(solution)/shard_map/cond/branch_1_fun/pallas_call | solution.py:115
  257.5 4.9 all-to-all-start
  262.4 25.6 %all-gather.6.cloned.1.call-done = bf16[1,3072,640]{2,1,0:T(8,128)(2,1)} async-done(((bf16[1,192,640]{2,1,0:T(8,128)(2,1)}), bf16[1,3072,640]{2,1,0:T(8,128)(2,1)}) %all-gather.6.cloned.1.call-update) | async-done | bytes 3932176 | tf_op jit(solution)/shard_map/all_gather | solution.py:300
  294.9 6.2 %all-to-all-start.1 = ((bf16[8,128,640]{2,1,0:T(8,128)(2,1)}), bf16[8,128,640]{2,1,0:T(8,128)(2,1)S(1)}, u32[]{:S(2)}, u32[]{:S(2)}) async-start(bf16[8,128,640]{2,1,0:T(8,128)(2,1)} %broadcast_in_dim.38), calls=%async_computation.1 | async-start | bytes 2621440 | tf_op jit(solution)/shard_map/all_to_all | solution.py:55
  301.1 4.5 fusion
  305.7 13.3 %all-to-all-done.1 = bf16[8,128,640]{2,1,0:T(8,128)(2,1)S(1)} async-done(((bf16[8,128,640]{2,1,0:T(8,128)(2,1)}), bf16[8,128,640]{2,1,0:T(8,128)(2,1)S(1)}, u32[]{:S(2)}, u32[]{:S(2)}) %all-to-all-start.1) | async-done | bytes 1310752 | tf_op jit(solution)/shard_map/all_to_all | solution.py:55
  319.7 6.3 %convolution_convert_fusion = bf16[128,1152]{1,0:T(8,128)(2,1)S(1)} fusion(bf16[5120,1152]{1,0:T(8,128)(2,1)} %all-gather.4.cloned.1.call-done, bf16[128,5120]{1,0:T(8,128)(2,1)S(1)} %bitcast.250, f32[128]{0:T(128)S(1)} %add_rsqrt_fusion, f32[5120]{0:T(1024)S(1)} %bitcast.295), kind=kOutput, calls=%fused_computation.21 | convolution fusion | flops 1512718336 | bytes 13423104 | tf_op jit(solution)/shard_map/dot_general | solution.py:265
  335.0 15.6 %reduce-scatter.2.cloned.1.call-done = f32[384,128]{1,0:T(8,128)} async-done(((f32[3072,128]{1,0:T(8,128)}), f32[384,128]{1,0:T(8,128)}) %reduce-scatter.2.cloned.1.call-update) | async-done | bytes 196624 | tf_op jit(solution)/shard_map/reduce_scatter | solution.py:327
  366.2 7.6 %all-to-all-start.2 = ((f32[8,2,128,128]{3,2,1,0:T(8,128)}), f32[8,2,128,128]{3,2,1,0:T(8,128)}, u32[]{:S(2)}, u32[]{:S(2)}) async-start(f32[8,2,128,128]{3,2,1,0:T(8,128)} %broadcast_in_dim.39), calls=%async_computation.3 | async-start | bytes 2097152 | tf_op jit(solution)/shard_map/all_to_all | solution.py:55
  374.5 5.4 collective-permute-start.13
  381.8 5.1 collective-permute-start.14
  387.0 6.0 %collective-permute-done.12 = bf16[4,128,192]{1,2,0:T(8,128)(2,1)S(1)} collective-permute-done((bf16[4,128,192]{1,2,0:T(8,128)(2,1)S(1)}, bf16[4,128,192]{1,2,0:T(8,128)(2,1)S(1)}, u32[]{:S(2)}, u32[]{:S(2)}) %collective-permute-start.12) | collective-permute-done | bytes 196640 | tf_op jit(solution)/shard_map/ppermute | solution.py:33
  394.0 6.3 %collective-permute-start.17 = (bf16[4,128,192]{1,2,0:T(8,128)(2,1)}, bf16[4,128,192]{1,2,0:T(8,128)(2,1)}, u32[]{:S(2)}, u32[]{:S(2)}) collective-permute-start(bf16[4,128,192]{1,2,0:T(8,128)(2,1)} %get-tuple-element.68), channel_id=1, source_target_pairs={{0,24},{1,25},{2,26},{3,27},{4,28},{5,29},{6,30},{7,31},{8,0},{9,1... | collective-permute-start | bytes 589832 | tf_op jit(solution)/shard_map/ppermute | solution.py:33
  400.4 7.5 %collective-permute-start.16 = (bf16[4,128,192]{1,2,0:T(8,128)(2,1)}, bf16[4,128,192]{1,2,0:T(8,128)(2,1)}, u32[]{:S(2)}, u32[]{:S(2)}) collective-permute-start(bf16[4,128,192]{1,2,0:T(8,128)(2,1)} %get-tuple-element.69), channel_id=1, source_target_pairs={{0,16},{1,17},{2,18},{3,19},{4,20},{5,21},{6,22},{7,23},{8,24},{9,... | collective-permute-start | bytes 589832 | tf_op jit(solution)/shard_map/ppermute | solution.py:33
  417.0 7.6 %all-to-all-start.3 = ((bf16[16,128,256]{2,1,0:T(8,128)(2,1)}), bf16[16,128,256]{2,1,0:T(8,128)(2,1)S(1)}, u32[]{:S(2)}, u32[]{:S(2)}) async-start(bf16[16,128,256]{2,1,0:T(8,128)(2,1)} %broadcast_in_dim.41), calls=%async_computation.4 | async-start | bytes 2097152 | tf_op jit(solution)/shard_map/all_to_all | solution.py:55
  434.5 12.5 %collective-permute-done.31 = bf16[384,128]{1,0:T(8,128)(2,1)S(1)} collective-permute-done((bf16[384,128]{1,0:T(8,128)(2,1)S(1)}, bf16[384,128]{1,0:T(8,128)(2,1)S(1)}, u32[]{:S(2)}, u32[]{:S(2)}) %collective-permute-start.31) | collective-permute-done | bytes 98336 | tf_op jit(solution)/shard_map/ppermute | solution.py:33
  448.9 4.6 collective-permute-done.32
  477.3 8.7 %fusion.15 = bf16[8,128,640]{1,2,0:T(8,128)(2,1)} fusion(bf16[8,640,1152]{2,1,0:T(8,128)(2,1)} %bitcast.296, bf16[128,384]{1,0:T(8,128)(2,1)S(1)} %get-tuple-element.47, bf16[128,384]{1,0:T(8,128)(2,1)S(1)} %get-tuple-element.46, bf16[128,384]{1,0:T(8,128)(2,1)S(1)} %copy-done.5), kind=kOutput, calls=%fused_computation.38 | convolution fusion | flops 1511489536 | bytes 13402112 | tf_op jit(solution)/shard_map/tk,bnk->btn/dot_general | solution.py:358
  494.9 5.0 collective-permute-start.37
  510.3 4.8 collective-permute-start.39
  518.3 6.6 %collective-permute-start.40 = (bf16[4,192,128]{2,1,0:T(8,128)(2,1)S(1)}, bf16[4,192,128]{2,1,0:T(8,128)(2,1)S(1)}, u32[]{:S(2)}, u32[]{:S(2)}) collective-permute-start(bf16[4,192,128]{2,1,0:T(8,128)(2,1)S(1)} %get-tuple-element.62), channel_id=1, source_target_pairs={{0,16},{1,17},{2,18},{3,19},{4,20},{5,21},{6,22},{7,23},{8,24},{9,... | collective-permute-start | bytes 589832 | tf_op jit(solution)/shard_map/ppermute | solution.py:33
  525.2 6.7 %collective-permute-done.40 = bf16[4,192,128]{2,1,0:T(8,128)(2,1)S(1)} collective-permute-done((bf16[4,192,128]{2,1,0:T(8,128)(2,1)S(1)}, bf16[4,192,128]{2,1,0:T(8,128)(2,1)S(1)}, u32[]{:S(2)}, u32[]{:S(2)}) %collective-permute-start.40) | collective-permute-done | bytes 196640 | tf_op jit(solution)/shard_map/ppermute | solution.py:33
  539.6 17.2 %collective-permute-done.46 = bf16[4,128,640]{2,1,0:T(8,128)(2,1)} collective-permute-done((bf16[4,128,640]{2,1,0:T(8,128)(2,1)S(1)}, bf16[4,128,640]{2,1,0:T(8,128)(2,1)}, u32[]{:S(2)}, u32[]{:S(2)}) %collective-permute-start.46) | collective-permute-done | bytes 655392 | tf_op jit(solution)/shard_map/ppermute | solution.py:33
  556.7 5.6 collective-permute-start.49
  577.8 5.9 collective-permute-done.47
  (243 shorter events, 167.4 us)
Async XLA Ops:
  7.2 156.2 %all-gather.4.cloned.1.call-start = ((), (), s32[]{:S(2)}) async-start(), calls=%async_computation.6 | async-start | bytes 12533760 | tf_op jit(solution)/shard_map/all_gather | solution.py:299
  9.6 278.3 %all-gather.6.cloned.1.call-start = ((), (), s32[]{:S(2)}) async-start(), calls=%async_computation.8 | async-start | bytes 4177920 | tf_op jit(solution)/shard_map/all_gather | solution.py:300
  179.3 48.9 %collective-permute-start.10 = (bf16[4,128,384]{2,1,0:T(8,128)(2,1)S(1)}, bf16[4,128,384]{2,1,0:T(8,128)(2,1)S(1)}, u32[]{:S(2)}, u32[]{:S(2)}) collective-permute-start(bf16[4,128,384]{2,1,0:T(8,128)(2,1)S(1)} %get-tuple-element.83), channel_id=1, source_target_pairs={{0,16},{1,17},{2,18},{3,19},{4,20},{5,21},{6,22},{7,23},{8,24},{9,... | collective-permute-start | bytes 1179656 | tf_op jit(solution)/shard_map/ppermute | solution.py:33
  182.1 28.6 %collective-permute-start.1 = (bf16[128,384]{1,0:T(8,128)(2,1)S(1)}, bf16[128,384]{1,0:T(8,128)(2,1)S(1)}, u32[]{:S(2)}, u32[]{:S(2)}) collective-permute-start(bf16[128,384]{1,0:T(8,128)(2,1)S(1)} %get-tuple-element.94), channel_id=1, source_target_pairs={{0,16},{1,17},{2,18},{3,19},{4,20},{5,21},{6,22},{7,23},{8,24},{9,... | collective-permute-start | bytes 294920 | tf_op jit(solution)/shard_map/ppermute | solution.py:33
  185.3 39.1 %collective-permute-start = (bf16[128,384]{1,0:T(8,128)(2,1)S(1)}, bf16[128,384]{1,0:T(8,128)(2,1)S(1)}, u32[]{:S(2)}, u32[]{:S(2)}) collective-permute-start(bf16[128,384]{1,0:T(8,128)(2,1)S(1)} %get-tuple-element.94), channel_id=1, source_target_pairs={{0,8},{1,9},{2,10},{3,11},{4,12},{5,13},{6,14},{7,15},{8,16},{9,17... | collective-permute-start | bytes 294920 | tf_op jit(solution)/shard_map/ppermute | solution.py:33
  187.5 36.9 %collective-permute-start.2 = (bf16[128,384]{1,0:T(8,128)(2,1)S(1)}, bf16[128,384]{1,0:T(8,128)(2,1)S(1)}, u32[]{:S(2)}, u32[]{:S(2)}) collective-permute-start(bf16[128,384]{1,0:T(8,128)(2,1)S(1)} %get-tuple-element.94), channel_id=1, source_target_pairs={{0,24},{1,25},{2,26},{3,27},{4,28},{5,29},{6,30},{7,31},{8,0},{9,1... | collective-permute-start | bytes 294920 | tf_op jit(solution)/shard_map/ppermute | solution.py:33
  189.4 43.6 %collective-permute-start.9 = (bf16[4,128,384]{2,1,0:T(8,128)(2,1)S(1)}, bf16[4,128,384]{2,1,0:T(8,128)(2,1)S(1)}, u32[]{:S(2)}, u32[]{:S(2)}) collective-permute-start(bf16[4,128,384]{2,1,0:T(8,128)(2,1)S(1)} %get-tuple-element.83), channel_id=1, source_target_pairs={{0,8},{1,9},{2,10},{3,11},{4,12},{5,13},{6,14},{7,15},{8,16},{9,17... | collective-permute-start | bytes 1179656 | tf_op jit(solution)/shard_map/ppermute | solution.py:33
  210.8 23.0 %collective-permute-start.11 = (bf16[4,128,384]{2,1,0:T(8,128)(2,1)S(1)}, bf16[4,128,384]{2,1,0:T(8,128)(2,1)S(1)}, u32[]{:S(2)}, u32[]{:S(2)}) collective-permute-start(bf16[4,128,384]{2,1,0:T(8,128)(2,1)S(1)} %get-tuple-element.83), channel_id=1, source_target_pairs={{0,24},{1,25},{2,26},{3,27},{4,28},{5,29},{6,30},{7,31},{8,0},{9,1... | collective-permute-start | bytes 1179656 | tf_op jit(solution)/shard_map/ppermute | solution.py:33
  225.4 13.7 %collective-permute-start.4 = (bf16[4,128,384]{2,1,0:T(8,128)(2,1)}, bf16[4,128,384]{2,1,0:T(8,128)(2,1)S(1)}, u32[]{:S(2)}, u32[]{:S(2)}) collective-permute-start(bf16[4,128,384]{2,1,0:T(8,128)(2,1)} %get-tuple-element.85), channel_id=1, source_target_pairs={{0,64},{1,65},{2,66},{3,67},{4,68},{5,69},{6,70},{7,71},{8,72},{9,... | collective-permute-start | bytes 1179656 | tf_op jit(solution)/shard_map/ppermute | solution.py:33
  225.4 20.7 %collective-permute-start.3 = (bf16[4,128,384]{2,1,0:T(8,128)(2,1)}, bf16[4,128,384]{2,1,0:T(8,128)(2,1)S(1)}, u32[]{:S(2)}, u32[]{:S(2)}) collective-permute-start(bf16[4,128,384]{2,1,0:T(8,128)(2,1)} %get-tuple-element.85), channel_id=1, source_target_pairs={{0,32},{1,33},{2,34},{3,35},{4,36},{5,37},{6,38},{7,39},{8,40},{9,... | collective-permute-start | bytes 1179656 | tf_op jit(solution)/shard_map/ppermute | solution.py:33
  228.1 18.0 %collective-permute-start.5 = (bf16[4,128,384]{2,1,0:T(8,128)(2,1)}, bf16[4,128,384]{2,1,0:T(8,128)(2,1)S(1)}, u32[]{:S(2)}, u32[]{:S(2)}) collective-permute-start(bf16[4,128,384]{2,1,0:T(8,128)(2,1)} %get-tuple-element.85), channel_id=1, source_target_pairs={{0,96},{1,97},{2,98},{3,99},{4,100},{5,101},{6,102},{7,103},{8,104... | collective-permute-start | bytes 1179656 | tf_op jit(solution)/shard_map/ppermute | solution.py:33
  257.5 30.5 %all-to-all-start = ((bf16[8,128,384]{1,2,0:T(8,128)(2,1)}), bf16[8,128,384]{1,2,0:T(8,128)(2,1)S(1)}, u32[]{:S(2)}, u32[]{:S(2)}) async-start(bf16[8,128,384]{1,2,0:T(8,128)(2,1)} %broadcast_in_dim.37), calls=%async_computation | async-start | bytes 1572864 | tf_op jit(solution)/shard_map/all_to_all | solution.py:55
  294.9 24.1 %all-to-all-start.1 = ((bf16[8,128,640]{2,1,0:T(8,128)(2,1)}), bf16[8,128,640]{2,1,0:T(8,128)(2,1)S(1)}, u32[]{:S(2)}, u32[]{:S(2)}) async-start(bf16[8,128,640]{2,1,0:T(8,128)(2,1)} %broadcast_in_dim.38), calls=%async_computation.1 | async-start | bytes 2621440 | tf_op jit(solution)/shard_map/all_to_all | solution.py:55
  301.1 49.4 %reduce-scatter.2.cloned.1.call-start = ((), (), s32[]{:S(2)}) async-start(), calls=%async_computation.7 | async-start | bytes 1769472 | tf_op jit(solution)/shard_map/reduce_scatter | solution.py:327
  330.1 25.4 %collective-permute-start.29 = (bf16[4,128,512]{2,1,0:T(8,128)(2,1)S(1)}, bf16[4,128,512]{2,1,0:T(8,128)(2,1)S(1)}, u32[]{:S(2)}, u32[]{:S(2)}) collective-permute-start(bf16[4,128,512]{2,1,0:T(8,128)(2,1)S(1)} %get-tuple-element.81), channel_id=1, source_target_pairs={{128,144},{129,145},{130,146},{131,147},{132,148},{133,149},{134,1... | collective-permute-start | bytes 1572872 | tf_op jit(solution)/shard_map/ppermute | solution.py:33
  331.6 20.6 %collective-permute-start.20 = (bf16[128,640]{1,0:T(8,128)(2,1)}, bf16[128,640]{1,0:T(8,128)(2,1)S(1)}, u32[]{:S(2)}, u32[]{:S(2)}) collective-permute-start(bf16[128,640]{1,0:T(8,128)(2,1)} %get-tuple-element.90), channel_id=1, source_target_pairs={{128,144},{129,145},{130,146},{131,147},{132,148},{133,149},{134,1... | collective-permute-start | bytes 491528 | tf_op jit(solution)/shard_map/ppermute | solution.py:33
  332.3 20.6 %collective-permute-start.19 = (bf16[128,640]{1,0:T(8,128)(2,1)}, bf16[128,640]{1,0:T(8,128)(2,1)}, u32[]{:S(2)}, u32[]{:S(2)}) collective-permute-start(bf16[128,640]{1,0:T(8,128)(2,1)} %get-tuple-element.90), channel_id=1, source_target_pairs={{128,136},{129,137},{130,138},{131,139},{132,140},{133,141},{134,1... | collective-permute-start | bytes 491528 | tf_op jit(solution)/shard_map/ppermute | solution.py:33
  333.6 19.3 %collective-permute-start.21 = (bf16[128,640]{1,0:T(8,128)(2,1)}, bf16[128,640]{1,0:T(8,128)(2,1)}, u32[]{:S(2)}, u32[]{:S(2)}) collective-permute-start(bf16[128,640]{1,0:T(8,128)(2,1)} %get-tuple-element.90), channel_id=1, source_target_pairs={{128,152},{129,153},{130,154},{131,155},{132,156},{133,157},{134,1... | collective-permute-start | bytes 491528 | tf_op jit(solution)/shard_map/ppermute | solution.py:33
  366.2 43.6 %all-to-all-start.2 = ((f32[8,2,128,128]{3,2,1,0:T(8,128)}), f32[8,2,128,128]{3,2,1,0:T(8,128)}, u32[]{:S(2)}, u32[]{:S(2)}) async-start(f32[8,2,128,128]{3,2,1,0:T(8,128)} %broadcast_in_dim.39), calls=%async_computation.3 | async-start | bytes 2097152 | tf_op jit(solution)/shard_map/all_to_all | solution.py:55
  379.9 13.1 %collective-permute-start.12 = (bf16[4,128,192]{1,2,0:T(8,128)(2,1)S(1)}, bf16[4,128,192]{1,2,0:T(8,128)(2,1)S(1)}, u32[]{:S(2)}, u32[]{:S(2)}) collective-permute-start(bf16[4,128,192]{1,2,0:T(8,128)(2,1)S(1)} %get-tuple-element.73), channel_id=1, source_target_pairs={{0,32},{1,33},{2,34},{3,35},{4,36},{5,37},{6,38},{7,39},{8,40},{9,... | collective-permute-start | bytes 589832 | tf_op jit(solution)/shard_map/ppermute | solution.py:33
  394.0 30.6 %collective-permute-start.17 = (bf16[4,128,192]{1,2,0:T(8,128)(2,1)}, bf16[4,128,192]{1,2,0:T(8,128)(2,1)}, u32[]{:S(2)}, u32[]{:S(2)}) collective-permute-start(bf16[4,128,192]{1,2,0:T(8,128)(2,1)} %get-tuple-element.68), channel_id=1, source_target_pairs={{0,24},{1,25},{2,26},{3,27},{4,28},{5,29},{6,30},{7,31},{8,0},{9,1... | collective-permute-start | bytes 589832 | tf_op jit(solution)/shard_map/ppermute | solution.py:33
  400.4 24.2 %collective-permute-start.16 = (bf16[4,128,192]{1,2,0:T(8,128)(2,1)}, bf16[4,128,192]{1,2,0:T(8,128)(2,1)}, u32[]{:S(2)}, u32[]{:S(2)}) collective-permute-start(bf16[4,128,192]{1,2,0:T(8,128)(2,1)} %get-tuple-element.69), channel_id=1, source_target_pairs={{0,16},{1,17},{2,18},{3,19},{4,20},{5,21},{6,22},{7,23},{8,24},{9,... | collective-permute-start | bytes 589832 | tf_op jit(solution)/shard_map/ppermute | solution.py:33
  407.8 16.7 %collective-permute-start.15 = (bf16[4,128,192]{1,2,0:T(8,128)(2,1)}, bf16[4,128,192]{1,2,0:T(8,128)(2,1)}, u32[]{:S(2)}, u32[]{:S(2)}) collective-permute-start(bf16[4,128,192]{1,2,0:T(8,128)(2,1)} %get-tuple-element.70), channel_id=1, source_target_pairs={{0,8},{1,9},{2,10},{3,11},{4,12},{5,13},{6,14},{7,15},{8,16},{9,17... | collective-permute-start | bytes 589832 | tf_op jit(solution)/shard_map/ppermute | solution.py:33
  417.0 55.1 %all-to-all-start.3 = ((bf16[16,128,256]{2,1,0:T(8,128)(2,1)}), bf16[16,128,256]{2,1,0:T(8,128)(2,1)S(1)}, u32[]{:S(2)}, u32[]{:S(2)}) async-start(bf16[16,128,256]{2,1,0:T(8,128)(2,1)} %broadcast_in_dim.41), calls=%async_computation.4 | async-start | bytes 2097152 | tf_op jit(solution)/shard_map/all_to_all | solution.py:55
  433.2 13.8 %collective-permute-start.31 = (bf16[384,128]{1,0:T(8,128)(2,1)S(1)}, bf16[384,128]{1,0:T(8,128)(2,1)S(1)}, u32[]{:S(2)}, u32[]{:S(2)}) collective-permute-start(bf16[384,128]{1,0:T(8,128)(2,1)S(1)} %fusion.46), channel_id=1, source_target_pairs={{128,0},{129,1},{130,2},{131,3},{132,4},{133,5},{134,6},{135,7},{1... | collective-permute-start | bytes 294920 | tf_op jit(solution)/shard_map/ppermute | solution.py:33
  485.9 49.4 %all-to-all-start.4 = ((bf16[8,128,640]{1,2,0:T(8,128)(2,1)}), bf16[8,128,640]{1,2,0:T(8,128)(2,1)S(1)}, u32[]{:S(2)}, u32[]{:S(2)}) async-start(bf16[8,128,640]{1,2,0:T(8,128)(2,1)} %fusion.15), calls=%async_computation.5 | async-start | bytes 2621440 | tf_op jit(solution)/shard_map/all_to_all | solution.py:361
  510.3 14.6 %collective-permute-start.39 = (bf16[4,192,128]{2,1,0:T(8,128)(2,1)S(1)}, bf16[4,192,128]{2,1,0:T(8,128)(2,1)S(1)}, u32[]{:S(2)}, u32[]{:S(2)}) collective-permute-start(bf16[4,192,128]{2,1,0:T(8,128)(2,1)S(1)} %get-tuple-element.60), channel_id=1, source_target_pairs={{0,8},{1,9},{2,10},{3,11},{4,12},{5,13},{6,14},{7,15},{8,16},{9,17... | collective-permute-start | bytes 589832 | tf_op jit(solution)/shard_map/ppermute | solution.py:33
  518.3 13.6 %collective-permute-start.40 = (bf16[4,192,128]{2,1,0:T(8,128)(2,1)S(1)}, bf16[4,192,128]{2,1,0:T(8,128)(2,1)S(1)}, u32[]{:S(2)}, u32[]{:S(2)}) collective-permute-start(bf16[4,192,128]{2,1,0:T(8,128)(2,1)S(1)} %get-tuple-element.62), channel_id=1, source_target_pairs={{0,16},{1,17},{2,18},{3,19},{4,20},{5,21},{6,22},{7,23},{8,24},{9,... | collective-permute-start | bytes 589832 | tf_op jit(solution)/shard_map/ppermute | solution.py:33
  538.1 18.6 %collective-permute-start.46 = (bf16[4,128,640]{2,1,0:T(8,128)(2,1)S(1)}, bf16[4,128,640]{2,1,0:T(8,128)(2,1)}, u32[]{:S(2)}, u32[]{:S(2)}) collective-permute-start(bf16[4,128,640]{2,1,0:T(8,128)(2,1)S(1)} %pad_maximum_fusion.9), channel_id=1, source_target_pairs={{128,0},{129,1},{130,2},{131,3},{132,4},{133,5},{134,6},{135,7},{1... | collective-permute-start | bytes 1966088 | tf_op jit(solution)/shard_map/ppermute | solution.py:33
  556.7 21.0 %collective-permute-start.49 = (bf16[4,128,640]{2,1,0:T(8,128)(2,1)}, bf16[4,128,640]{2,1,0:T(8,128)(2,1)}, u32[]{:S(2)}, u32[]{:S(2)}) collective-permute-start(bf16[4,128,640]{2,1,0:T(8,128)(2,1)} %collective-permute-done.46), channel_id=1, source_target_pairs={{0,96},{1,97},{2,98},{3,99},{4,100},{5,101},{6,102},{7,103},{8,104... | collective-permute-start | bytes 1966088 | tf_op jit(solution)/shard_map/ppermute | solution.py:33
  562.3 15.4 %collective-permute-start.48 = (bf16[4,128,640]{2,1,0:T(8,128)(2,1)}, bf16[4,128,640]{2,1,0:T(8,128)(2,1)}, u32[]{:S(2)}, u32[]{:S(2)}) collective-permute-start(bf16[4,128,640]{2,1,0:T(8,128)(2,1)} %collective-permute-done.46), channel_id=1, source_target_pairs={{0,64},{1,65},{2,66},{3,67},{4,68},{5,69},{6,70},{7,71},{8,72},{9,... | collective-permute-start | bytes 1966088 | tf_op jit(solution)/shard_map/ppermute | solution.py:33
  564.3 19.4 %collective-permute-start.47 = (bf16[4,128,640]{2,1,0:T(8,128)(2,1)}, bf16[4,128,640]{2,1,0:T(8,128)(2,1)}, u32[]{:S(2)}, u32[]{:S(2)}) collective-permute-start(bf16[4,128,640]{2,1,0:T(8,128)(2,1)} %collective-permute-done.46), channel_id=1, source_target_pairs={{0,32},{1,33},{2,34},{3,35},{4,36},{5,37},{6,38},{7,39},{8,40},{9,... | collective-permute-start | bytes 1966088 | tf_op jit(solution)/shard_map/ppermute | solution.py:33
  (58 other events, 802.3 us)
Sparse Core Ops, SparseCore 0:
  10.5 152.8 all-gather.3
  165.9 122.0 all-gather.5
  305.8 44.7 reduce-scatter.1

commit v5 on v4

--- a/solution.py
+++ b/solution.py
@@ -11,6 +11,7 @@
 AXES = ("grp", "seq", "fsdp")
 VMEM = pltpu.CompilerParams(vmem_limit_bytes=50 * 2**20)
 F32, BF16 = jnp.float32, jnp.bfloat16
+GEN, CRIT = (0,), (1,)
 
 
 def moved(value, step, groups=(0, 1), cross=False):
@@ -55,16 +56,23 @@
     return lax.all_to_all(jnp.broadcast_to(value[None], (count,) + value.shape), axis, 0, 0)
 
 
-def gather_fsdp(value, groups):
-    pair = jnp.stack([value, moved(value, along(3, 1), groups)])
-    return direct4(pair, 2, groups)
-
-
-def swap_seq(blocks, groups):
-    rows = [blocks[0]] + [moved(blocks[k], along(0, k), groups) for k in (1, 2, 3)]
-    rows = jnp.stack(rows)
-    cols = [rows[:, 0]] + [moved(rows[:, k], along(1, k), groups) for k in (1, 2, 3)]
-    return jnp.stack(cols, axis=1)
+def gather_out(shard, y, z):
+    depth, width = shard.shape
+    cut = 3 * HD
+
+    def placed(value, axis, whole, at, new_axis):
+        for k in range(4):
+            piece = moved(value, along(axis, k), GEN) if k else value
+            start = [0] * whole.ndim
+            start[new_axis] = (at - k) % 4
+            whole = lax.dynamic_update_slice(whole, jnp.expand_dims(piece, new_axis), start)
+        return whole
+
+    lead = placed(shard[:, :cut], 1, jnp.zeros((4, depth, cut), BF16), z, 0)
+    tail = placed(shard[:, cut:], 0, jnp.zeros((4, depth, width - cut), BF16), y, 0)
+    lead = placed(lead, 0, jnp.zeros((4, 4, depth, cut), BF16), y, 0)
+    tail = placed(tail, 1, jnp.zeros((4, 4, depth, width - cut), BF16), z, 1)
+    return [part.reshape(16 * depth, -1) for part in (lead, tail)]
 
 
 def across(value, groups):
@@ -74,11 +82,6 @@
 def after(value, other):
     first = other[(slice(0, 1),) * other.ndim].reshape(())
     return value + (first.astype(F32) * 0.0).astype(value.dtype)
-
-
-def ordered(relative, x, w):
-    backward = jnp.stack([relative[k] for k in (0, 3, 2, 1)])
-    return jnp.roll(backward, (x, w), (0, 1))
 
 
 def mm(a, b, ca, cb):
@@ -250,6 +253,29 @@
     )(at, keys, values, tail, sent, high, low)
 
 
+def product_kernel(at, heads, back, out, ordered_heads):
+    rows = heads.shape[1]
+    y, z = at[0] // 4, at[0] % 4
+    for dy in range(4):
+        for dz in range(4):
+            place = ((y + 4 - dy) % 4) * 4 + (z + 4 - dz) % 4
+            block = (4 * dy + dz) * rows
+            ordered_heads[block : block + rows, :] = heads[pl.ds(place, 1)][0]
+    out[...] = mm(ordered_heads[...], back[...], 0, 0)
+
+
+def summed_product(at, heads, back):
+    width = heads.shape[2]
+    whole = pl.BlockSpec(memory_space=pltpu.VMEM)
+    return pl.pallas_call(
+        product_kernel,
+        in_specs=[pl.BlockSpec(memory_space=pltpu.SMEM), whole, whole],
+        out_shape=jax.ShapeDtypeStruct((width, back.shape[1]), F32),
+        scratch_shapes=[pltpu.VMEM((back.shape[0], width), BF16)],
+        compiler_params=VMEM,
+    )(at, heads, back)
+
+
 def split(value):
     high = lax.reduce_precision(value, 8, 7)
     return high.astype(BF16), (value - high).astype(BF16)
@@ -276,9 +302,6 @@
     for entry in range(real_bank.shape[0]):
         chosen = jnp.where((real_pick == entry)[:, None], real_bank[entry], chosen)
     return chosen
-
-
-GEN, CRIT = (0,), (1,)
 
 
 def local(
@@ -297,11 +320,16 @@
 
     shard = jnp.concatenate([attn_weights[0, c] for c in range(3)], axis=1)
     weights = lax.all_gather(shard, "seq", axis=0, tiled=True)
-    full_out = lax.all_gather(out_weights[0], "seq", axis=0, tiled=True)
+    out_lead, out_tail = gather_out(out_weights[0], y, z)
+
+    joint = jnp.dot(out_weights[0], head_in, preferred_element_type=F32)
+    joint = spread(jnp.sum(spread(joint, "fsdp"), axis=0), "seq").reshape(8 * width, -1)
+    high, low = split(lax.dynamic_slice_in_dim(joint, fsdp_at * width, width, 0))
 
     real_rows = pick_rows(real_bank, real_pick)
     first_rows = jnp.where(is_gen, new_rows, real_rows)
     first_normed, _ = normalised(first_rows, gains)
+    first_normed = after(after(after(first_normed, high), out_lead), out_tail)
     first = times(first_normed, weights)
     first_q = first[:, :width]
     first_k, first_v = gather_seq(first[:, width : 2 * width], first[:, 2 * width :], (0, 1))
@@ -316,15 +344,15 @@
 
     first_all = spread(first_heads, "fsdp").transpose(1, 0, 2).reshape(rows, 8 * width)
     first_cols = lax.dynamic_slice_in_dim(first_rows, start, cols, 1).astype(F32)
-    generated = (first_cols + jnp.dot(first_all, full_out, preferred_element_type=F32)).astype(BF16)
+    projected = [
+        jnp.dot(first_all, part, preferred_element_type=F32) for part in (out_lead, out_tail)
+    ]
+    generated = (first_cols + jnp.concatenate(projected, axis=1)).astype(BF16)
     crossed = spread(across(generated, GEN), "fsdp")
     second_rows = crossed.transpose(1, 0, 2).reshape(rows, model)
 
-    to_seq = first_all.reshape(rows, 4, 4, 192).transpose(1, 2, 0, 3)
-    gen_heads = swap_seq(jnp.roll(to_seq, (-y, -z), (0, 1)), GEN).reshape(tokens, 192)
-
-    joint = jnp.dot(full_out, head_in, preferred_element_type=F32)
-    high, low = split(lax.psum_scatter(joint, "fsdp", scatter_dimension=0, tiled=True))
+    to_seq = after(first_all, generated).reshape(rows, 16, 192).transpose(1, 0, 2)
+    gen_heads = lax.all_to_all(to_seq, "seq", 0, 0)
 
     def units_of(row_cols, heads):
         part = jnp.dot(row_cols, head_in, preferred_element_type=F32)
@@ -342,7 +370,7 @@
         jnp.concatenate([second_v[:, cut:], second_q], axis=1),
         CRIT,
     )
-    second_heads, lse = critic_attention(second_q, every_lead, every_tail)
+    second_heads, lse = critic_attention(after(second_q, gen_heads), every_lead, every_tail)
     second_cols = lax.dynamic_slice_in_dim(second_rows, start, cols, 1)
     units = jnp.stack([units_of(real_cols, first_heads), units_of(second_cols, second_heads)])
     units = jnp.sum(spread(units, "fsdp"), axis=0)
@@ -365,16 +393,14 @@
     input_grad = (inverse * row_grad * gain_cols + direction).astype(BF16)
 
     product = mm(second_heads, fake_unit, 0, 0) - mm(first_heads, real_unit, 0, 0)
-    product = across(after(product.astype(BF16), gen_heads), CRIT)
-    product = ordered(gather_fsdp(product, GEN), x, w).reshape(4, 4, 192, -1)
-    product = swap_seq(jnp.roll(product, (-y, -z), (0, 1)), GEN)
-    product = across(jnp.sum(product.astype(F32), axis=(0, 1)), GEN)
-    product_high, product_low = split(product)
+    product = spread(product.astype(BF16), "fsdp").reshape(16, 192, -1)
+    product = lax.all_to_all(product, "seq", 0, 0)
+    product_high, product_low = split(jnp.sum(product.astype(F32), axis=0))
     term_crit = mm(product_high, head_in, 1, 1) + mm(product_low, head_in, 1, 1)
 
-    back = direct4(across(direct4(after(input_grad, product), 1, CRIT), CRIT), 0, GEN)
+    back = direct4(across(direct4(input_grad, 1, CRIT), CRIT), 0, GEN)
     back = back.reshape(tokens, cols)
-    term_gen = mm(gen_heads, back, 0, 0)
+    term_gen = summed_product(at, gen_heads, back)
 
     stats = sent[:, :, HD:].astype(F32)
     margin = jnp.sum(stats[:, :, 18:21]) / tokens

time: 605 us -> 612 us (1.012)
  the two profiles are of different devices: /device:TPU:32 before, /device:TPU:8 now
where the time goes in v5:
time: 612 us; the launch traced here: 601 us
  waiting for transfers between devices  307 us (50%)
  starting transfers between devices  168 us (27%)
  local copies, waits for them, and re-layouts  30.7 us (5%)
  matrix products  29.7 us (5%)
  other arithmetic  22.4 us (4%)
  Pallas kernels  21.8 us (4%)
  between operations  21.7 us (4%)
    ppermute x45, waiting for transfers between devices, moved(): return lax.ppermute(value, AXES, pairs)  147 us
    ppermute x45, starting transfers between devices, moved(): return lax.ppermute(value, AXES, pairs)  109 us
    all_to_all x7, waiting for transfers between devices, spread(): lax.all_to_all(jnp.broadcast_to(value[None], (count,) + value.shape), axi...  83.9 us
    all_gather x1, waiting for transfers between devices, local(): weights = lax.all_gather(shard, 'seq', axis=0, tiled=True)  49.3 us
    all_to_all x7, starting transfers between devices, spread(): lax.all_to_all(jnp.broadcast_to(value[None], (count,) + value.shape), axi...  34.8 us
    all_to_all x1, waiting for transfers between devices, local(): gen_heads = lax.all_to_all(to_seq, 'seq', 0, 0)  14.1 us
    dot_general x2, matrix products, times(): return jnp.dot(a, b, preferred_element_type=F32).astype(BF16)  12.5 us
    all_to_all x1, waiting for transfers between devices, local(): row_terms = lax.all_to_all(row_terms.astype(BF16), 'fsdp', 0, 0)  12.2 us
  transfers between devices with their start and end apart: 56, of which 21 were waited for; matrix products, arithmetic and copies ran while one was open for 7% of the time, Pallas kernels for 1%

profile of v5, /device:TPU:8, one launch (start us, length us, event | category | flops | bytes accessed | tf_op | source)
XLA Modules:
  0.0 601.2 jit_solution(1190699681554374924)
XLA Ops:
  9.6 5.2 collective-permute-start
  14.8 7.3 %collective-permute-start.1 = (bf16[192,384]{1,0:T(8,128)(2,1)S(1)}, bf16[192,384]{1,0:T(8,128)(2,1)}, u32[]{:S(2)}, u32[]{:S(2)}) collective-permute-start(bf16[192,384]{1,0:T(8,128)(2,1)S(1)} %slice.103), channel_id=1, source_target_pairs={{0,16},{1,17},{2,18},{3,19},{4,20},{5,21},{6,22},{7,23},{8,24},{9,... | collective-permute-start | bytes 442376 | tf_op jit(solution)/shard_map/ppermute | solution.py:34
  47.6 16.9 %all-to-all-done = f32[8,192,128]{2,1,0:T(8,128)S(1)} async-done(((f32[8,192,128]{2,1,0:T(8,128)}), f32[8,192,128]{2,1,0:T(8,128)S(1)}, u32[]{:S(2)}, u32[]{:S(2)}) %all-to-all-start) | async-done | bytes 786464 | tf_op jit(solution)/shard_map/all_to_all | solution.py:56
  65.8 7.9 %all-to-all-start.1 = ((f32[16,192,128]{2,1,0:T(8,128)}), f32[16,192,128]{2,1,0:T(8,128)}, u32[]{:S(2)}, u32[]{:S(2)}) async-start(f32[16,192,128]{2,1,0:T(8,128)} %broadcast_in_dim.150), calls=%async_computation.1 | async-start | bytes 3145728 | tf_op jit(solution)/shard_map/all_to_all | solution.py:56
  79.9 5.5 collective-permute-start.10
  85.6 5.5 collective-permute-start.11
  100.8 22.8 %collective-permute-done.9 = bf16[4,192,256]{2,1,0:T(8,128)(2,1)S(1)} collective-permute-done((bf16[4,192,256]{2,1,0:T(8,128)(2,1)S(1)}, bf16[4,192,256]{2,1,0:T(8,128)(2,1)S(1)}, u32[]{:S(2)}, u32[]{:S(2)}) %collective-permute-start.9) | collective-permute-done | bytes 393248 | tf_op jit(solution)/shard_map/ppermute | solution.py:34
  125.6 12.0 %collective-permute-done.10 = bf16[4,192,256]{2,1,0:T(8,128)(2,1)S(1)} collective-permute-done((bf16[4,192,256]{2,1,0:T(8,128)(2,1)S(1)}, bf16[4,192,256]{2,1,0:T(8,128)(2,1)S(1)}, u32[]{:S(2)}, u32[]{:S(2)}) %collective-permute-start.10) | collective-permute-done | bytes 393248 | tf_op jit(solution)/shard_map/ppermute | solution.py:34
  137.6 12.8 %collective-permute-done.11 = bf16[4,192,256]{2,1,0:T(8,128)(2,1)S(1)} collective-permute-done((bf16[4,192,256]{2,1,0:T(8,128)(2,1)S(1)}, bf16[4,192,256]{2,1,0:T(8,128)(2,1)S(1)}, u32[]{:S(2)}, u32[]{:S(2)}) %collective-permute-start.11) | collective-permute-done | bytes 393248 | tf_op jit(solution)/shard_map/ppermute | solution.py:34
  156.8 49.3 %all-gather.2.cloned.1.call-done = bf16[5120,1152]{1,0:T(8,128)(2,1)} async-done(((bf16[320,1152]{1,0:T(8,128)(2,1)}), bf16[5120,1152]{1,0:T(8,128)(2,1)}) %all-gather.2.cloned.1.call-update) | async-done | bytes 11796496 | tf_op jit(solution)/shard_map/all_gather | solution.py:322
  206.1 6.3 %convolution_convert_fusion.1 = bf16[128,1152]{1,0:T(8,128)(2,1)S(1)} fusion(bf16[5120,1152]{1,0:T(8,128)(2,1)} %all-gather.2.cloned.1.call-done, bf16[128,5120]{1,0:T(8,128)(2,1)S(1)} %get-tuple-element.58, f32[5120]{0:T(1024)S(1)} %bitcast.249, f32[128]{0:T(128)S(1)} %add_rsqrt_fusion.1, bf16[]{:T(256)} %bitcast.29, bf16[]{:T(256)} %bitcast.16, bf16[]{:T(256)} %bitcast.6), kind=kOutput, calls=%fused_computation.11 | convolution fusion | flops 1514684416 | bytes 13423110 | tf_op jit(solution)/shard_map/dot_general | solution.py:291
  213.0 11.5 %collective-permute-start.18 = (bf16[128,384]{1,0:T(8,128)(2,1)S(1)}, bf16[128,384]{1,0:T(8,128)(2,1)S(1)}, u32[]{:S(2)}, u32[]{:S(2)}) collective-permute-start(bf16[128,384]{1,0:T(8,128)(2,1)S(1)} %get-tuple-element.80), channel_id=1, source_target_pairs={{0,32},{1,33},{2,34},{3,35},{4,36},{5,37},{6,38},{7,39},{8,40},{9,... | collective-permute-start | bytes 294920 | tf_op jit(solution)/shard_map/ppermute | solution.py:34
  242.4 24.2 %collective-permute-done.12 = bf16[128,384]{1,0:T(8,128)(2,1)S(1)} collective-permute-done((bf16[128,384]{1,0:T(8,128)(2,1)S(1)}, bf16[128,384]{1,0:T(8,128)(2,1)S(1)}, u32[]{:S(2)}, u32[]{:S(2)}) %collective-permute-start.12) | collective-permute-done | bytes 98336 | tf_op jit(solution)/shard_map/ppermute | solution.py:34
  267.6 4.8 collective-permute-start.15
  277.9 5.9 collective-permute-done.15
  286.2 7.0 %collective-permute-done.17 = bf16[4,128,384]{2,1,0:T(8,128)(2,1)S(1)} collective-permute-done((bf16[4,128,384]{2,1,0:T(8,128)(2,1)}, bf16[4,128,384]{2,1,0:T(8,128)(2,1)S(1)}, u32[]{:S(2)}, u32[]{:S(2)}) %collective-permute-start.17) | collective-permute-done | bytes 393248 | tf_op jit(solution)/shard_map/ppermute | solution.py:34
  296.2 7.8 %conditional.1 = (bf16[128,384]{1,0:T(8,128)(2,1)}) conditional(s32[]{:T(128)} %convert_element_type.130, (bf16[128,384]{1,0:T(8,128)(2,1)S(1)}, bf16[2048,384]{1,0:T(8,128)(2,1)S(1)}, bf16[2048,384]{1,0:T(8,128)(2,1)S(1)}) %tuple.46, (s32[3]{0:T(128)S(1)}, f32[2048]{0:T(1024)S(1)}, bf16[128,384]{1,0:T(8,128)(2,1)S(1)}, ...), branch_computations={%region_2.3_spmd, %region_3.4_spmd} | conditional | bytes 73736 | solution.py:338
  296.3 7.8 %branch_1_fun.1 = bf16[128,384]{1,0:T(8,128)(2,1)} custom-call(s32[3]{0:T(128)S(1)} %get-tuple-element.52.frames, f32[8,2048]{1,0:T(8,128)S(1)} %broadcast_in_dim.181.mask, bf16[128,384]{1,0:T(8,128)(2,1)S(1)} %get-tuple-element.29.q, bf16[4,1024,384]{2,1,0:T(8,128)(2,1)S(1)} %get-tuple-element.53.k0.k1.k2, ...), custom_call_target="tpu_custom_call" | custom-call | tf_op jit(solution)/shard_map/cond/branch_1_fun/pallas_call | solution.py:118
  310.2 10.1 %all-to-all-done.2 = bf16[8,128,384]{1,2,0:T(8,128)(2,1)S(1)} async-done(((bf16[8,128,384]{1,2,0:T(8,128)(2,1)}), bf16[8,128,384]{1,2,0:T(8,128)(2,1)S(1)}, u32[]{:S(2)}, u32[]{:S(2)}) %all-to-all-start.2) | async-done | bytes 786464 | tf_op jit(solution)/shard_map/all_to_all | solution.py:56
  325.2 8.7 %all-to-all-start.3 = ((bf16[16,128,192]{1,2,0:T(8,128)(2,1)}), bf16[16,128,192]{1,2,0:T(8,128)(2,1)S(1)}, u32[]{:S(2)}, u32[]{:S(2)}) async-start(bf16[16,128,192]{1,2,0:T(8,128)(2,1)} %bitcast.56), calls=%async_computation.3 | async-start | bytes 1572864 | tf_op jit(solution)/shard_map/all_to_all | solution.py:355
  336.3 14.1 %all-to-all-done.3 = bf16[16,128,192]{1,2,0:T(8,128)(2,1)S(1)} async-done(((bf16[16,128,192]{1,2,0:T(8,128)(2,1)}), bf16[16,128,192]{1,2,0:T(8,128)(2,1)S(1)}, u32[]{:S(2)}, u32[]{:S(2)}) %all-to-all-start.3) | async-done | bytes 786464 | tf_op jit(solution)/shard_map/all_to_all | solution.py:355
  356.7 11.7 %all-to-all-done.4 = bf16[8,128,640]{2,1,0:T(8,128)(2,1)S(1)} async-done(((bf16[8,128,640]{2,1,0:T(8,128)(2,1)}), bf16[8,128,640]{2,1,0:T(8,128)(2,1)S(1)}, u32[]{:S(2)}, u32[]{:S(2)}) %all-to-all-start.4) | async-done | bytes 1310752 | tf_op jit(solution)/shard_map/all_to_all | solution.py:56
  368.9 6.3 %convolution_convert_fusion = bf16[128,1152]{1,0:T(8,128)(2,1)S(1)} fusion(bf16[5120,1152]{1,0:T(8,128)(2,1)} %all-gather.2.cloned.1.call-done, bf16[128,5120]{1,0:T(8,128)(2,1)S(1)} %bitcast.219, f32[128]{0:T(128)S(1)} %add_rsqrt_fusion, f32[5120]{0:T(1024)S(1)} %bitcast.250), kind=kOutput, calls=%fused_computation.10 | convolution fusion | flops 1512718336 | bytes 13423104 | tf_op jit(solution)/shard_map/dot_general | solution.py:291
  400.6 27.7 %all-to-all-done.5 = f32[8,2,128,128]{3,2,1,0:T(8,128)} async-done(((f32[8,2,128,128]{3,2,1,0:T(8,128)}), f32[8,2,128,128]{3,2,1,0:T(8,128)}, u32[]{:S(2)}, u32[]{:S(2)}) %all-to-all-start.5) | async-done | bytes 1048608 | tf_op jit(solution)/shard_map/all_to_all | solution.py:56
  435.4 5.8 all-to-all-start.6
  444.1 17.5 %all-to-all-done.6.sent = bf16[16,128,256]{2,1,0:T(8,128)(2,1)S(1)} async-done(((bf16[16,128,256]{2,1,0:T(8,128)(2,1)}), bf16[16,128,256]{2,1,0:T(8,128)(2,1)S(1)}, u32[]{:S(2)}, u32[]{:S(2)}) %all-to-all-start.6) | async-done | bytes 1048608 | tf_op jit(solution)/shard_map/all_to_all | solution.py:56
  473.1 8.7 %fusion.3 = bf16[8,128,640]{1,2,0:T(8,128)(2,1)} fusion(bf16[8,640,1152]{2,1,0:T(8,128)(2,1)} %bitcast.251, bf16[128,384]{1,0:T(8,128)(2,1)S(1)} %get-tuple-element.47, bf16[128,384]{1,0:T(8,128)(2,1)S(1)} %get-tuple-element.46, bf16[128,384]{1,0:T(8,128)(2,1)S(1)} %copy-done.5), kind=kOutput, calls=%fused_computation.17 | convolution fusion | flops 1511489536 | bytes 13402112 | tf_op jit(solution)/shard_map/tk,bnk->btn/dot_general | solution.py:386
  481.8 5.7 all-to-all-start.7
  488.1 12.2 %all-to-all-done.7 = bf16[8,128,640]{1,2,0:T(8,128)(2,1)S(1)} async-done(((bf16[8,128,640]{1,2,0:T(8,128)(2,1)}), bf16[8,128,640]{1,2,0:T(8,128)(2,1)S(1)}, u32[]{:S(2)}, u32[]{:S(2)}) %all-to-all-start.7) | async-done | bytes 1310752 | tf_op jit(solution)/shard_map/all_to_all | solution.py:389
  500.4 9.6 %all-to-all-start.9 = ((bf16[16,192,128]{2,1,0:T(8,128)(2,1)}), bf16[16,192,128]{2,1,0:T(8,128)(2,1)}, u32[]{:S(2)}, u32[]{:S(2)}) async-start(bf16[16,192,128]{2,1,0:T(8,128)(2,1)} %bitcast.94), calls=%async_computation.9 | async-start | bytes 1572864 | tf_op jit(solution)/shard_map/all_to_all | solution.py:397
  515.7 45.4 %collective-permute-done.40 = bf16[4,128,640]{2,1,0:T(8,128)(2,1)} collective-permute-done((bf16[4,128,640]{2,1,0:T(8,128)(2,1)S(1)}, bf16[4,128,640]{2,1,0:T(8,128)(2,1)}, u32[]{:S(2)}, u32[]{:S(2)}) %collective-permute-start.40) | collective-permute-done | bytes 655392 | tf_op jit(solution)/shard_map/ppermute | solution.py:34
  579.4 6.5 %collective-permute-done.43 = bf16[4,128,640]{2,1,0:T(8,128)(2,1)} collective-permute-done((bf16[4,128,640]{2,1,0:T(8,128)(2,1)}, bf16[4,128,640]{2,1,0:T(8,128)(2,1)}, u32[]{:S(2)}, u32[]{:S(2)}) %collective-permute-start.43) | collective-permute-done | bytes 655392 | tf_op jit(solution)/shard_map/ppermute | solution.py:34
  (235 shorter events, 176.8 us)
Async XLA Ops:
  7.2 198.9 %all-gather.2.cloned.1.call-start = ((), (), s32[]{:S(2)}) async-start(), calls=%async_computation.10 | async-start | bytes 12533760 | tf_op jit(solution)/shard_map/all_gather | solution.py:322
  9.6 75.9 %collective-permute-start = (bf16[192,384]{1,0:T(8,128)(2,1)S(1)}, bf16[192,384]{1,0:T(8,128)(2,1)}, u32[]{:S(2)}, u32[]{:S(2)}) collective-permute-start(bf16[192,384]{1,0:T(8,128)(2,1)S(1)} %slice.103), channel_id=1, source_target_pairs={{0,8},{1,9},{2,10},{3,11},{4,12},{5,13},{6,14},{7,15},{8,16},{9,17... | collective-permute-start | bytes 442376 | tf_op jit(solution)/shard_map/ppermute | solution.py:34
  14.8 77.2 %collective-permute-start.1 = (bf16[192,384]{1,0:T(8,128)(2,1)S(1)}, bf16[192,384]{1,0:T(8,128)(2,1)}, u32[]{:S(2)}, u32[]{:S(2)}) collective-permute-start(bf16[192,384]{1,0:T(8,128)(2,1)S(1)} %slice.103), channel_id=1, source_target_pairs={{0,16},{1,17},{2,18},{3,19},{4,20},{5,21},{6,22},{7,23},{8,24},{9,... | collective-permute-start | bytes 442376 | tf_op jit(solution)/shard_map/ppermute | solution.py:34
  22.1 70.8 %collective-permute-start.2 = (bf16[192,384]{1,0:T(8,128)(2,1)S(1)}, bf16[192,384]{1,0:T(8,128)(2,1)}, u32[]{:S(2)}, u32[]{:S(2)}) collective-permute-start(bf16[192,384]{1,0:T(8,128)(2,1)S(1)} %slice.103), channel_id=1, source_target_pairs={{0,24},{1,25},{2,26},{3,27},{4,28},{5,29},{6,30},{7,31},{8,0},{9,1... | collective-permute-start | bytes 442376 | tf_op jit(solution)/shard_map/ppermute | solution.py:34
  27.3 15.9 %collective-permute-start.6 = (bf16[192,256]{1,0:T(8,128)(2,1)}, bf16[192,256]{1,0:T(8,128)(2,1)S(1)}, u32[]{:S(2)}, u32[]{:S(2)}) collective-permute-start(bf16[192,256]{1,0:T(8,128)(2,1)} %slice.105), channel_id=1, source_target_pairs={{0,32},{1,33},{2,34},{3,35},{4,36},{5,37},{6,38},{7,39},{8,40},{9,... | collective-permute-start | bytes 294920 | tf_op jit(solution)/shard_map/ppermute | solution.py:34
  30.8 42.9 %collective-permute-start.7 = (bf16[192,256]{1,0:T(8,128)(2,1)}, bf16[192,256]{1,0:T(8,128)(2,1)}, u32[]{:S(2)}, u32[]{:S(2)}) collective-permute-start(bf16[192,256]{1,0:T(8,128)(2,1)} %slice.105), channel_id=1, source_target_pairs={{0,64},{1,65},{2,66},{3,67},{4,68},{5,69},{6,70},{7,71},{8,72},{9,... | collective-permute-start | bytes 294920 | tf_op jit(solution)/shard_map/ppermute | solution.py:34
  34.9 29.6 %all-to-all-start = ((f32[8,192,128]{2,1,0:T(8,128)}), f32[8,192,128]{2,1,0:T(8,128)S(1)}, u32[]{:S(2)}, u32[]{:S(2)}) async-start(f32[8,192,128]{2,1,0:T(8,128)} %broadcast_in_dim.149), calls=%async_computation | async-start | bytes 1572864 | tf_op jit(solution)/shard_map/all_to_all | solution.py:56
  43.2 31.4 %collective-permute-start.8 = (bf16[192,256]{1,0:T(8,128)(2,1)}, bf16[192,256]{1,0:T(8,128)(2,1)}, u32[]{:S(2)}, u32[]{:S(2)}) collective-permute-start(bf16[192,256]{1,0:T(8,128)(2,1)} %slice.105), channel_id=1, source_target_pairs={{0,96},{1,97},{2,98},{3,99},{4,100},{5,101},{6,102},{7,103},{8,104... | collective-permute-start | bytes 294920 | tf_op jit(solution)/shard_map/ppermute | solution.py:34
  65.8 88.9 %all-to-all-start.1 = ((f32[16,192,128]{2,1,0:T(8,128)}), f32[16,192,128]{2,1,0:T(8,128)}, u32[]{:S(2)}, u32[]{:S(2)}) async-start(f32[16,192,128]{2,1,0:T(8,128)} %broadcast_in_dim.150), calls=%async_computation.1 | async-start | bytes 3145728 | tf_op jit(solution)/shard_map/all_to_all | solution.py:56
  75.6 48.0 %collective-permute-start.9 = (bf16[4,192,256]{2,1,0:T(8,128)(2,1)S(1)}, bf16[4,192,256]{2,1,0:T(8,128)(2,1)S(1)}, u32[]{:S(2)}, u32[]{:S(2)}) collective-permute-start(bf16[4,192,256]{2,1,0:T(8,128)(2,1)S(1)} %bitcast_dynamic-update-slice_fusion.12), channel_id=1, source_target_pairs={{0,8},{1,9},{2,10},{3,11},{4,12},{5,13},{6,14},{7,15},{8,16},{9,17... | collective-permute-start | bytes 1179656 | tf_op jit(solution)/shard_map/ppermute | solution.py:34
  79.9 57.7 %collective-permute-start.10 = (bf16[4,192,256]{2,1,0:T(8,128)(2,1)S(1)}, bf16[4,192,256]{2,1,0:T(8,128)(2,1)S(1)}, u32[]{:S(2)}, u32[]{:S(2)}) collective-permute-start(bf16[4,192,256]{2,1,0:T(8,128)(2,1)S(1)} %bitcast_dynamic-update-slice_fusion.12), channel_id=1, source_target_pairs={{0,16},{1,17},{2,18},{3,19},{4,20},{5,21},{6,22},{7,23},{8,24},{9,... | collective-permute-start | bytes 1179656 | tf_op jit(solution)/shard_map/ppermute | solution.py:34
  85.6 64.9 %collective-permute-start.11 = (bf16[4,192,256]{2,1,0:T(8,128)(2,1)S(1)}, bf16[4,192,256]{2,1,0:T(8,128)(2,1)S(1)}, u32[]{:S(2)}, u32[]{:S(2)}) collective-permute-start(bf16[4,192,256]{2,1,0:T(8,128)(2,1)S(1)} %bitcast_dynamic-update-slice_fusion.12), channel_id=1, source_target_pairs={{0,24},{1,25},{2,26},{3,27},{4,28},{5,29},{6,30},{7,31},{8,0},{9,1... | collective-permute-start | bytes 1179656 | tf_op jit(solution)/shard_map/ppermute | solution.py:34
  93.9 57.9 %collective-permute-start.3 = (bf16[4,192,384]{2,1,0:T(8,128)(2,1)S(1)}, bf16[4,192,384]{2,1,0:T(8,128)(2,1)S(1)}, u32[]{:S(2)}, u32[]{:S(2)}) collective-permute-start(bf16[4,192,384]{2,1,0:T(8,128)(2,1)S(1)} %bitcast_dynamic-update-slice_fusion.8), channel_id=1, source_target_pairs={{0,32},{1,33},{2,34},{3,35},{4,36},{5,37},{6,38},{7,39},{8,40},{9,... | collective-permute-start | bytes 1769480 | tf_op jit(solution)/shard_map/ppermute | solution.py:34
  97.3 54.6 %collective-permute-start.4 = (bf16[4,192,384]{2,1,0:T(8,128)(2,1)S(1)}, bf16[4,192,384]{2,1,0:T(8,128)(2,1)S(1)}, u32[]{:S(2)}, u32[]{:S(2)}) collective-permute-start(bf16[4,192,384]{2,1,0:T(8,128)(2,1)S(1)} %bitcast_dynamic-update-slice_fusion.8), channel_id=1, source_target_pairs={{0,64},{1,65},{2,66},{3,67},{4,68},{5,69},{6,70},{7,71},{8,72},{9,... | collective-permute-start | bytes 1769480 | tf_op jit(solution)/shard_map/ppermute | solution.py:34
  123.6 28.4 %collective-permute-start.5 = (bf16[4,192,384]{2,1,0:T(8,128)(2,1)S(1)}, bf16[4,192,384]{2,1,0:T(8,128)(2,1)S(1)}, u32[]{:S(2)}, u32[]{:S(2)}) collective-permute-start(bf16[4,192,384]{2,1,0:T(8,128)(2,1)S(1)} %bitcast_dynamic-update-slice_fusion.8), channel_id=1, source_target_pairs={{0,96},{1,97},{2,98},{3,99},{4,100},{5,101},{6,102},{7,103},{8,104... | collective-permute-start | bytes 1769480 | tf_op jit(solution)/shard_map/ppermute | solution.py:34
  231.8 43.8 %collective-permute-start.21 = (bf16[4,128,384]{2,1,0:T(8,128)(2,1)S(1)}, bf16[4,128,384]{2,1,0:T(8,128)(2,1)S(1)}, u32[]{:S(2)}, u32[]{:S(2)}) collective-permute-start(bf16[4,128,384]{2,1,0:T(8,128)(2,1)S(1)} %get-tuple-element.69), channel_id=1, source_target_pairs={{0,8},{1,9},{2,10},{3,11},{4,12},{5,13},{6,14},{7,15},{8,16},{9,17... | collective-permute-start | bytes 1179656 | tf_op jit(solution)/shard_map/ppermute | solution.py:34
  232.1 34.5 %collective-permute-start.12 = (bf16[128,384]{1,0:T(8,128)(2,1)S(1)}, bf16[128,384]{1,0:T(8,128)(2,1)S(1)}, u32[]{:S(2)}, u32[]{:S(2)}) collective-permute-start(bf16[128,384]{1,0:T(8,128)(2,1)S(1)} %get-tuple-element.81), channel_id=1, source_target_pairs={{0,8},{1,9},{2,10},{3,11},{4,12},{5,13},{6,14},{7,15},{8,16},{9,17... | collective-permute-start | bytes 294920 | tf_op jit(solution)/shard_map/ppermute | solution.py:34
  235.6 31.1 %collective-permute-start.13 = (bf16[128,384]{1,0:T(8,128)(2,1)S(1)}, bf16[128,384]{1,0:T(8,128)(2,1)S(1)}, u32[]{:S(2)}, u32[]{:S(2)}) collective-permute-start(bf16[128,384]{1,0:T(8,128)(2,1)S(1)} %get-tuple-element.81), channel_id=1, source_target_pairs={{0,16},{1,17},{2,18},{3,19},{4,20},{5,21},{6,22},{7,23},{8,24},{9,... | collective-permute-start | bytes 294920 | tf_op jit(solution)/shard_map/ppermute | solution.py:34
  238.4 28.2 %collective-permute-start.14 = (bf16[128,384]{1,0:T(8,128)(2,1)S(1)}, bf16[128,384]{1,0:T(8,128)(2,1)S(1)}, u32[]{:S(2)}, u32[]{:S(2)}) collective-permute-start(bf16[128,384]{1,0:T(8,128)(2,1)S(1)} %get-tuple-element.81), channel_id=1, source_target_pairs={{0,24},{1,25},{2,26},{3,27},{4,28},{5,29},{6,30},{7,31},{8,0},{9,1... | collective-permute-start | bytes 294920 | tf_op jit(solution)/shard_map/ppermute | solution.py:34
  239.2 36.5 %collective-permute-start.22 = (bf16[4,128,384]{2,1,0:T(8,128)(2,1)S(1)}, bf16[4,128,384]{2,1,0:T(8,128)(2,1)S(1)}, u32[]{:S(2)}, u32[]{:S(2)}) collective-permute-start(bf16[4,128,384]{2,1,0:T(8,128)(2,1)S(1)} %get-tuple-element.69), channel_id=1, source_target_pairs={{0,16},{1,17},{2,18},{3,19},{4,20},{5,21},{6,22},{7,23},{8,24},{9,... | collective-permute-start | bytes 1179656 | tf_op jit(solution)/shard_map/ppermute | solution.py:34
  267.6 16.1 %collective-permute-start.15 = (bf16[4,128,384]{2,1,0:T(8,128)(2,1)}, bf16[4,128,384]{2,1,0:T(8,128)(2,1)S(1)}, u32[]{:S(2)}, u32[]{:S(2)}) collective-permute-start(bf16[4,128,384]{2,1,0:T(8,128)(2,1)} %get-tuple-element.71), channel_id=1, source_target_pairs={{0,32},{1,33},{2,34},{3,35},{4,36},{5,37},{6,38},{7,39},{8,40},{9,... | collective-permute-start | bytes 1179656 | tf_op jit(solution)/shard_map/ppermute | solution.py:34
  275.7 17.6 %collective-permute-start.17 = (bf16[4,128,384]{2,1,0:T(8,128)(2,1)}, bf16[4,128,384]{2,1,0:T(8,128)(2,1)S(1)}, u32[]{:S(2)}, u32[]{:S(2)}) collective-permute-start(bf16[4,128,384]{2,1,0:T(8,128)(2,1)} %get-tuple-element.71), channel_id=1, source_target_pairs={{0,96},{1,97},{2,98},{3,99},{4,100},{5,101},{6,102},{7,103},{8,104... | collective-permute-start | bytes 1179656 | tf_op jit(solution)/shard_map/ppermute | solution.py:34
  325.2 25.2 %all-to-all-start.3 = ((bf16[16,128,192]{1,2,0:T(8,128)(2,1)}), bf16[16,128,192]{1,2,0:T(8,128)(2,1)S(1)}, u32[]{:S(2)}, u32[]{:S(2)}) async-start(bf16[16,128,192]{1,2,0:T(8,128)(2,1)} %bitcast.56), calls=%async_computation.3 | async-start | bytes 1572864 | tf_op jit(solution)/shard_map/all_to_all | solution.py:355
  351.7 16.7 %all-to-all-start.4 = ((bf16[8,128,640]{2,1,0:T(8,128)(2,1)}), bf16[8,128,640]{2,1,0:T(8,128)(2,1)S(1)}, u32[]{:S(2)}, u32[]{:S(2)}) async-start(bf16[8,128,640]{2,1,0:T(8,128)(2,1)} %broadcast_in_dim.173), calls=%async_computation.4 | async-start | bytes 2621440 | tf_op jit(solution)/shard_map/all_to_all | solution.py:56
  396.3 32.0 %all-to-all-start.5 = ((f32[8,2,128,128]{3,2,1,0:T(8,128)}), f32[8,2,128,128]{3,2,1,0:T(8,128)}, u32[]{:S(2)}, u32[]{:S(2)}) async-start(f32[8,2,128,128]{3,2,1,0:T(8,128)} %broadcast_in_dim.174), calls=%async_computation.5 | async-start | bytes 2097152 | tf_op jit(solution)/shard_map/all_to_all | solution.py:56
  435.4 26.1 %all-to-all-start.6 = ((bf16[16,128,256]{2,1,0:T(8,128)(2,1)}), bf16[16,128,256]{2,1,0:T(8,128)(2,1)S(1)}, u32[]{:S(2)}, u32[]{:S(2)}) async-start(bf16[16,128,256]{2,1,0:T(8,128)(2,1)} %broadcast_in_dim.176), calls=%async_computation.6 | async-start | bytes 2097152 | tf_op jit(solution)/shard_map/all_to_all | solution.py:56
  463.4 18.3 %all-to-all-start.8 = ((bf16[8,384,128]{2,1,0:T(8,128)(2,1)}), bf16[8,384,128]{2,1,0:T(8,128)(2,1)}, u32[]{:S(2)}, u32[]{:S(2)}) async-start(bf16[8,384,128]{2,1,0:T(8,128)(2,1)} %broadcast_in_dim.177), calls=%async_computation.8 | async-start | bytes 1572864 | tf_op jit(solution)/shard_map/all_to_all | solution.py:56
  481.8 18.6 %all-to-all-start.7 = ((bf16[8,128,640]{1,2,0:T(8,128)(2,1)}), bf16[8,128,640]{1,2,0:T(8,128)(2,1)S(1)}, u32[]{:S(2)}, u32[]{:S(2)}) async-start(bf16[8,128,640]{1,2,0:T(8,128)(2,1)} %fusion.3), calls=%async_computation.7 | async-start | bytes 2621440 | tf_op jit(solution)/shard_map/all_to_all | solution.py:389
  500.4 77.3 %all-to-all-start.9 = ((bf16[16,192,128]{2,1,0:T(8,128)(2,1)}), bf16[16,192,128]{2,1,0:T(8,128)(2,1)}, u32[]{:S(2)}, u32[]{:S(2)}) async-start(bf16[16,192,128]{2,1,0:T(8,128)(2,1)} %bitcast.94), calls=%async_computation.9 | async-start | bytes 1572864 | tf_op jit(solution)/shard_map/all_to_all | solution.py:397
  514.4 46.7 %collective-permute-start.40 = (bf16[4,128,640]{2,1,0:T(8,128)(2,1)S(1)}, bf16[4,128,640]{2,1,0:T(8,128)(2,1)}, u32[]{:S(2)}, u32[]{:S(2)}) collective-permute-start(bf16[4,128,640]{2,1,0:T(8,128)(2,1)S(1)} %pad_maximum_fusion.7), channel_id=1, source_target_pairs={{128,0},{129,1},{130,2},{131,3},{132,4},{133,5},{134,6},{135,7},{1... | collective-permute-start | bytes 1966088 | tf_op jit(solution)/shard_map/ppermute | solution.py:34
  561.2 18.2 %collective-permute-start.41 = (bf16[4,128,640]{2,1,0:T(8,128)(2,1)}, bf16[4,128,640]{2,1,0:T(8,128)(2,1)}, u32[]{:S(2)}, u32[]{:S(2)}) collective-permute-start(bf16[4,128,640]{2,1,0:T(8,128)(2,1)} %collective-permute-done.40), channel_id=1, source_target_pairs={{0,32},{1,33},{2,34},{3,35},{4,36},{5,37},{6,38},{7,39},{8,40},{9,... | collective-permute-start | bytes 1966088 | tf_op jit(solution)/shard_map/ppermute | solution.py:34
  567.6 18.2 %collective-permute-start.43 = (bf16[4,128,640]{2,1,0:T(8,128)(2,1)}, bf16[4,128,640]{2,1,0:T(8,128)(2,1)}, u32[]{:S(2)}, u32[]{:S(2)}) collective-permute-start(bf16[4,128,640]{2,1,0:T(8,128)(2,1)} %collective-permute-done.40), channel_id=1, source_target_pairs={{0,96},{1,97},{2,98},{3,99},{4,100},{5,101},{6,102},{7,103},{8,104... | collective-permute-start | bytes 1966088 | tf_op jit(solution)/shard_map/ppermute | solution.py:34
  (49 other events, 571.7 us)
Sparse Core Ops, SparseCore 0:
  10.5 195.5 all-gather.1

commit v6 on v4

--- a/solution.py
+++ b/solution.py
@@ -39,6 +39,18 @@
     return tuple(step)
 
 
+def ring4(value, axis, groups):
+    one = moved(value, along(axis, 1), groups)
+    three = moved(value, along(axis, -1), groups)
+    cut = value.ndim - 2
+    half = value.shape[cut] // 2
+    low = lax.slice_in_dim(one, 0, half, axis=cut)
+    high = lax.slice_in_dim(three, half, 2 * half, axis=cut)
+    low = moved(low, along(axis, 1), groups)
+    high = moved(high, along(axis, -1), groups)
+    return jnp.stack([value, one, jnp.concatenate([low, high], axis=cut), three])
+
+
 def direct4(value, axis, groups):
     return jnp.stack([value] + [moved(value, along(axis, k), groups) for k in (1, 2, 3)])
 
@@ -55,11 +67,6 @@
     return lax.all_to_all(jnp.broadcast_to(value[None], (count,) + value.shape), axis, 0, 0)
 
 
-def gather_fsdp(value, groups):
-    pair = jnp.stack([value, moved(value, along(3, 1), groups)])
-    return direct4(pair, 2, groups)
-
-
 def swap_seq(blocks, groups):
     rows = [blocks[0]] + [moved(blocks[k], along(0, k), groups) for k in (1, 2, 3)]
     rows = jnp.stack(rows)
@@ -74,11 +81,6 @@
 def after(value, other):
     first = other[(slice(0, 1),) * other.ndim].reshape(())
     return value + (first.astype(F32) * 0.0).astype(value.dtype)
-
-
-def ordered(relative, x, w):
-    backward = jnp.stack([relative[k] for k in (0, 3, 2, 1)])
-    return jnp.roll(backward, (x, w), (0, 1))
 
 
 def mm(a, b, ca, cb):
@@ -304,7 +306,8 @@
     first_normed, _ = normalised(first_rows, gains)
     first = times(first_normed, weights)
     first_q = first[:, :width]
-    first_k, first_v = gather_seq(first[:, width : 2 * width], first[:, 2 * width :], (0, 1))
+    first_kv = ring4(ring4(first[:, width:], 1, (0, 1)), 0, (0, 1)).reshape(tokens, 2 * width)
+    first_k, first_v = first_kv[:, :width], first_kv[:, width:]
     key_y = (y - jnp.arange(tokens) // (4 * rows)) % 4
     mask = jnp.broadcast_to((key_y // 2 <= y // 2).astype(F32)[None], (8, tokens))
     first_heads = lax.cond(
@@ -314,7 +317,9 @@
         (cache_frames, mask, first_q, cache_keys, cache_values, first_k, first_v),
     )
 
+    joint = jnp.dot(full_out, head_in, preferred_element_type=F32)
     first_all = spread(first_heads, "fsdp").transpose(1, 0, 2).reshape(rows, 8 * width)
+    first_all = after(first_all, joint)
     first_cols = lax.dynamic_slice_in_dim(first_rows, start, cols, 1).astype(F32)
     generated = (first_cols + jnp.dot(first_all, full_out, preferred_element_type=F32)).astype(BF16)
     crossed = spread(across(generated, GEN), "fsdp")
@@ -323,7 +328,6 @@
     to_seq = first_all.reshape(rows, 4, 4, 192).transpose(1, 2, 0, 3)
     gen_heads = swap_seq(jnp.roll(to_seq, (-y, -z), (0, 1)), GEN).reshape(tokens, 192)
 
-    joint = jnp.dot(full_out, head_in, preferred_element_type=F32)
     high, low = split(lax.psum_scatter(joint, "fsdp", scatter_dimension=0, tiled=True))
 
     def units_of(row_cols, heads):
@@ -344,8 +348,8 @@
     )
     second_heads, lse = critic_attention(second_q, every_lead, every_tail)
     second_cols = lax.dynamic_slice_in_dim(second_rows, start, cols, 1)
-    units = jnp.stack([units_of(real_cols, first_heads), units_of(second_cols, second_heads)])
-    units = jnp.sum(spread(units, "fsdp"), axis=0)
+    units = jnp.stack([units_of(real_cols, after(first_heads, second_heads)), units_of(second_cols, second_heads)])
+    units = after(jnp.sum(spread(units, "fsdp"), axis=0), gen_heads)
     real_score, real_unit = unit_terms(units[0], head_out)
     fake_score, fake_unit = unit_terms(units[1], head_out)
     query_grad, sent = query_grads(
@@ -365,14 +369,12 @@
     input_grad = (inverse * row_grad * gain_cols + direction).astype(BF16)
 
     product = mm(second_heads, fake_unit, 0, 0) - mm(first_heads, real_unit, 0, 0)
-    product = across(after(product.astype(BF16), gen_heads), CRIT)
-    product = ordered(gather_fsdp(product, GEN), x, w).reshape(4, 4, 192, -1)
-    product = swap_seq(jnp.roll(product, (-y, -z), (0, 1)), GEN)
-    product = across(jnp.sum(product.astype(F32), axis=(0, 1)), GEN)
-    product_high, product_low = split(product)
+    product = spread(product.astype(BF16), "fsdp").reshape(16, 192, -1)
+    product = lax.all_to_all(product, "seq", 0, 0)
+    product_high, product_low = split(jnp.sum(product.astype(F32), axis=0))
     term_crit = mm(product_high, head_in, 1, 1) + mm(product_low, head_in, 1, 1)
 
-    back = direct4(across(direct4(after(input_grad, product), 1, CRIT), CRIT), 0, GEN)
+    back = direct4(across(direct4(input_grad, 1, CRIT), CRIT), 0, GEN)
     back = back.reshape(tokens, cols)
     term_gen = mm(gen_heads, back, 0, 0)
 

time: 605 us -> 572 us (0.945)
  starting transfers between devices: 147 us -> 118 us
    ppermute x51 -> x35, starting transfers between devices: 117 us -> 75.3 us  [moved(): return lax.ppermute(value, AXES, pairs)]
    all_to_all x4 -> x5, waiting for transfers between devices: 13.3 us -> 46.8 us  [spread(): lax.all_to_all(jnp.broadcast_to(value[None], (count,) + value.shape), axi...]
    all_gather x1, waiting for transfers between devices: 25.6 us -> 0.01 us  [local(): full_out = lax.all_gather(out_weights[0], 'seq', axis=0, tiled=True)]
    ppermute x51 -> x35, waiting for transfers between devices: 119 us -> 101 us  [moved(): return lax.ppermute(value, AXES, pairs)]
    all_to_all x1, waiting for transfers between devices: 0.01 us -> 16.4 us  [local(): row_terms = lax.all_to_all(row_terms.astype(BF16), 'fsdp', 0, 0)]
    all_to_all x4 -> x5, starting transfers between devices: 26.3 us -> 33.7 us  [spread(): lax.all_to_all(jnp.broadcast_to(value[None], (count,) + value.shape), axi...]
    reduce_scatter x1, waiting for transfers between devices: 15.6 us -> 8.31 us  [local(): lax.psum_scatter(joint, 'fsdp', scatter_dimension=0, tiled=True)]
  transfers between devices with their start and end apart: 59 -> 45, of which waited for: 27 -> 22; matrix products, arithmetic and copies ran while one was open for 10% -> 10% of each run, Pallas kernels for 2% -> 2%
where the time goes in v6:
time: 572 us; the launch traced here: 562 us
  waiting for transfers between devices  324 us (57%)
  starting transfers between devices  118 us (21%)
  matrix products  38.1 us (7%)
  local copies, waits for them, and re-layouts  22.5 us (4%)
  other arithmetic  20.9 us (4%)
  between operations  19.7 us (3%)
  Pallas kernels  18.7 us (3%)
    all_gather x1, waiting for transfers between devices, local(): weights = lax.all_gather(shard, 'seq', axis=0, tiled=True)  150 us
    ppermute x35, waiting for transfers between devices, moved(): return lax.ppermute(value, AXES, pairs)  101 us
    ppermute x35, starting transfers between devices, moved(): return lax.ppermute(value, AXES, pairs)  75.3 us
    all_to_all x5, waiting for transfers between devices, spread(): lax.all_to_all(jnp.broadcast_to(value[None], (count,) + value.shape), axi...  46.8 us
    all_to_all x5, starting transfers between devices, spread(): lax.all_to_all(jnp.broadcast_to(value[None], (count,) + value.shape), axi...  33.7 us
    all_to_all x1, waiting for transfers between devices, local(): row_terms = lax.all_to_all(row_terms.astype(BF16), 'fsdp', 0, 0)  16.4 us
    dot_general x2, matrix products, times(): return jnp.dot(a, b, preferred_element_type=F32).astype(BF16)  13.1 us
  transfers between devices with their start and end apart: 45, of which 22 were waited for; matrix products, arithmetic and copies ran while one was open for 10% of the time, Pallas kernels for 2%

profile of v6, /device:TPU:32, one launch (start us, length us, event | category | flops | bytes accessed | tf_op | source)
XLA Modules:
  0.0 562.3 jit_solution(5752282272265088516)
XLA Ops:
  13.8 149.6 %all-gather.4.cloned.1.call-done = bf16[5120,1152]{1,0:T(8,128)(2,1)} async-done(((bf16[320,1152]{1,0:T(8,128)(2,1)}), bf16[5120,1152]{1,0:T(8,128)(2,1)}) %all-gather.4.cloned.1.call-update) | async-done | bytes 11796496 | tf_op jit(solution)/shard_map/all_gather | solution.py:301
  163.4 6.7 %convolution_convert_fusion.1 = bf16[128,1152]{1,0:T(8,128)(2,1)S(1)} fusion(bf16[5120,1152]{1,0:T(8,128)(2,1)} %all-gather.4.cloned.1.call-done, bf16[128,5120]{1,0:T(8,128)(2,1)} %get-tuple-element.58, f32[5120]{0:T(1024)S(1)} %bitcast.225, f32[128]{0:T(128)S(1)} %add_rsqrt_fusion.1), kind=kOutput, calls=%fused_computation.23 | convolution fusion | flops 1512718336 | bytes 13423104 | tf_op jit(solution)/shard_map/dot_general | solution.py:267
  170.2 4.1 collective-permute-start.2
  174.4 6.2 %collective-permute-done = bf16[128,768]{1,0:T(8,128)(2,1)S(1)} collective-permute-done((bf16[128,768]{1,0:T(8,128)(2,1)S(1)}, bf16[128,768]{1,0:T(8,128)(2,1)S(1)}, u32[]{:S(2)}, u32[]{:S(2)}) %collective-permute-start) | collective-permute-done | bytes 196640 | tf_op jit(solution)/shard_map/ppermute | solution.py:33
  180.6 4.6 collective-permute-start.1
  185.7 4.8 collective-permute-start.3
  192.8 4.7 collective-permute-done.3
  201.1 22.5 %collective-permute-done.4 = bf16[4,128,768]{2,1,0:T(8,128)(2,1)S(1)} collective-permute-done((bf16[4,128,768]{2,1,0:T(8,128)(2,1)S(1)}, bf16[4,128,768]{2,1,0:T(8,128)(2,1)S(1)}, u32[]{:S(2)}, u32[]{:S(2)}) %collective-permute-start.4) | collective-permute-done | bytes 786464 | tf_op jit(solution)/shard_map/ppermute | solution.py:33
  229.0 7.9 %collective-permute-done.5 = bf16[4,64,768]{2,1,0:T(8,128)(2,1)} collective-permute-done((bf16[4,64,768]{2,1,0:T(8,128)(2,1)S(1)}, bf16[4,64,768]{2,1,0:T(8,128)(2,1)}, u32[]{:S(2)}, u32[]{:S(2)}) %collective-permute-start.5) | collective-permute-done | bytes 393248 | tf_op jit(solution)/shard_map/ppermute | solution.py:33
  243.0 7.4 %conditional.1 = (bf16[128,384]{1,0:T(8,128)(2,1)S(1)}) conditional(s32[]{:T(128)} %convert_element_type.100, (bf16[128,384]{1,0:T(8,128)(2,1)S(1)}, bf16[2048,384]{1,0:T(8,128)(2,1)S(1)}, bf16[2048,384]{1,0:T(8,128)(2,1)S(1)}) %tuple.48, (s32[3]{0:T(128)S(1)}, f32[2048]{0:T(1024)S(1)}, bf16[128,384]{1,0:T(8,128)(2,1)S(1)}, ...), branch_computations={%region_1.2_spmd, %region_2.3_spmd} | conditional | bytes 73736 | solution.py:313
  243.2 7.2 %branch_1_fun.1 = bf16[128,384]{1,0:T(8,128)(2,1)S(1)} custom-call(s32[3]{0:T(128)S(1)} %get-tuple-element.52.frames, f32[8,2048]{1,0:T(8,128)S(1)} %broadcast_in_dim.89.mask, bf16[128,384]{1,0:T(8,128)(2,1)S(1)} %get-tuple-element.29.q, bf16[4,1024,384]{2,1,0:T(8,128)(2,1)S(1)} %get-tuple-element.53.k0.k1.k2, ...), custom_call_target="tpu_custom_call" | custom-call | tf_op jit(solution)/shard_map/cond/branch_1_fun/pallas_call | solution.py:117
  251.6 7.3 %all-to-all-start = ((bf16[8,128,384]{1,2,0:T(8,128)(2,1)}), bf16[8,128,384]{1,2,0:T(8,128)(2,1)S(1)}, u32[]{:S(2)}, u32[]{:S(2)}) async-start(bf16[8,128,384]{1,2,0:T(8,128)(2,1)} %broadcast_in_dim.39), calls=%async_computation | async-start | bytes 1572864 | tf_op jit(solution)/shard_map/all_to_all | solution.py:67
  263.5 4.4 all-to-all-done
  276.7 4.7 all-to-all-start.1
  282.1 17.4 %all-to-all-done.1 = bf16[8,128,640]{2,1,0:T(8,128)(2,1)S(1)} async-done(((bf16[8,128,640]{2,1,0:T(8,128)(2,1)}), bf16[8,128,640]{2,1,0:T(8,128)(2,1)S(1)}, u32[]{:S(2)}, u32[]{:S(2)}) %all-to-all-start.1) | async-done | bytes 1310752 | tf_op jit(solution)/shard_map/all_to_all | solution.py:67
  300.1 6.5 %convolution_convert_fusion = bf16[128,1152]{1,0:T(8,128)(2,1)S(1)} fusion(bf16[5120,1152]{1,0:T(8,128)(2,1)} %all-gather.4.cloned.1.call-done, bf16[128,5120]{1,0:T(8,128)(2,1)S(1)} %bitcast.200, f32[128]{0:T(128)S(1)} %add_rsqrt_fusion, f32[5120]{0:T(1024)S(1)} %bitcast.226), kind=kOutput, calls=%fused_computation.22 | convolution fusion | flops 1512718336 | bytes 13423104 | tf_op jit(solution)/shard_map/dot_general | solution.py:267
  322.0 8.3 %reduce-scatter.2.cloned.1.call-done = f32[384,128]{1,0:T(8,128)} async-done(((f32[3072,128]{1,0:T(8,128)}), f32[384,128]{1,0:T(8,128)}) %reduce-scatter.2.cloned.1.call-update) | async-done | bytes 196624 | tf_op jit(solution)/shard_map/reduce_scatter | solution.py:331
  344.6 6.2 %all-to-all-start.2 = ((f32[8,2,128,128]{3,2,1,0:T(8,128)}), f32[8,2,128,128]{3,2,1,0:T(8,128)}, u32[]{:S(2)}, u32[]{:S(2)}) async-start(f32[8,2,128,128]{3,2,1,0:T(8,128)} %broadcast_in_dim.41), calls=%async_computation.3 | async-start | bytes 2097152 | tf_op jit(solution)/shard_map/all_to_all | solution.py:67
  352.6 5.8 %collective-permute-start.9 = (bf16[4,128,192]{1,2,0:T(8,128)(2,1)S(1)}, bf16[4,128,192]{1,2,0:T(8,128)(2,1)S(1)}, u32[]{:S(2)}, u32[]{:S(2)}) collective-permute-start(bf16[4,128,192]{1,2,0:T(8,128)(2,1)S(1)} %get-tuple-element.66), channel_id=1, source_target_pairs={{0,64},{1,65},{2,66},{3,67},{4,68},{5,69},{6,70},{7,71},{8,72},{9,... | collective-permute-start | bytes 589832 | tf_op jit(solution)/shard_map/ppermute | solution.py:33
  361.2 4.3 collective-permute-start.10
  365.5 8.0 %collective-permute-done.8 = bf16[4,128,192]{1,2,0:T(8,128)(2,1)S(1)} collective-permute-done((bf16[4,128,192]{1,2,0:T(8,128)(2,1)S(1)}, bf16[4,128,192]{1,2,0:T(8,128)(2,1)S(1)}, u32[]{:S(2)}, u32[]{:S(2)}) %collective-permute-start.8) | collective-permute-done | bytes 196640 | tf_op jit(solution)/shard_map/ppermute | solution.py:33
  373.8 5.9 %collective-permute-start.13 = (bf16[4,128,192]{1,2,0:T(8,128)(2,1)S(1)}, bf16[4,128,192]{1,2,0:T(8,128)(2,1)S(1)}, u32[]{:S(2)}, u32[]{:S(2)}) collective-permute-start(bf16[4,128,192]{1,2,0:T(8,128)(2,1)S(1)} %get-tuple-element.62), channel_id=1, source_target_pairs={{0,24},{1,25},{2,26},{3,27},{4,28},{5,29},{6,30},{7,31},{8,0},{9,1... | collective-permute-start | bytes 589832 | tf_op jit(solution)/shard_map/ppermute | solution.py:33
  379.6 5.3 collective-permute-start.12
  386.9 5.6 collective-permute-done.12
  408.9 6.8 %all-to-all-start.3 = ((bf16[16,128,256]{2,1,0:T(8,128)(2,1)}), bf16[16,128,256]{2,1,0:T(8,128)(2,1)S(1)}, u32[]{:S(2)}, u32[]{:S(2)}) async-start(bf16[16,128,256]{2,1,0:T(8,128)(2,1)} %broadcast_in_dim.43), calls=%async_computation.4 | async-start | bytes 2097152 | tf_op jit(solution)/shard_map/all_to_all | solution.py:67
  418.6 24.9 %all-to-all-done.3.sent = bf16[16,128,256]{2,1,0:T(8,128)(2,1)S(1)} async-done(((bf16[16,128,256]{2,1,0:T(8,128)(2,1)}), bf16[16,128,256]{2,1,0:T(8,128)(2,1)S(1)}, u32[]{:S(2)}, u32[]{:S(2)}) %all-to-all-start.3) | async-done | bytes 1048608 | tf_op jit(solution)/shard_map/all_to_all | solution.py:67
  445.4 8.6 %all-to-all-start.5 = ((bf16[8,384,128]{2,1,0:T(8,128)(2,1)}), bf16[8,384,128]{2,1,0:T(8,128)(2,1)}, u32[]{:S(2)}, u32[]{:S(2)}) async-start(bf16[8,384,128]{2,1,0:T(8,128)(2,1)} %broadcast_in_dim.44), calls=%async_computation.6 | async-start | bytes 1572864 | tf_op jit(solution)/shard_map/all_to_all | solution.py:67
  459.2 8.7 %fusion.15 = bf16[8,128,640]{1,2,0:T(8,128)(2,1)} fusion(bf16[8,640,1152]{2,1,0:T(8,128)(2,1)} %bitcast.227, bf16[128,384]{1,0:T(8,128)(2,1)S(1)} %get-tuple-element.47, bf16[128,384]{1,0:T(8,128)(2,1)S(1)} %get-tuple-element.46, bf16[128,384]{1,0:T(8,128)(2,1)S(1)} %copy-done.5), kind=kOutput, calls=%fused_computation.31 | convolution fusion | flops 1511489536 | bytes 13402112 | tf_op jit(solution)/shard_map/tk,bnk->btn/dot_general | solution.py:362
  467.8 5.7 %all-to-all-start.4 = ((bf16[8,128,640]{1,2,0:T(8,128)(2,1)}), bf16[8,128,640]{1,2,0:T(8,128)(2,1)S(1)}, u32[]{:S(2)}, u32[]{:S(2)}) async-start(bf16[8,128,640]{1,2,0:T(8,128)(2,1)} %fusion.15), calls=%async_computation.5 | async-start | bytes 2621440 | tf_op jit(solution)/shard_map/all_to_all | solution.py:365
  474.2 16.4 %all-to-all-done.4 = bf16[8,128,640]{1,2,0:T(8,128)(2,1)S(1)} async-done(((bf16[8,128,640]{1,2,0:T(8,128)(2,1)}), bf16[8,128,640]{1,2,0:T(8,128)(2,1)S(1)}, u32[]{:S(2)}, u32[]{:S(2)}) %all-to-all-start.4) | async-done | bytes 1310752 | tf_op jit(solution)/shard_map/all_to_all | solution.py:365
  500.2 25.6 %collective-permute-done.30 = bf16[4,128,640]{2,1,0:T(8,128)(2,1)} collective-permute-done((bf16[4,128,640]{2,1,0:T(8,128)(2,1)S(1)}, bf16[4,128,640]{2,1,0:T(8,128)(2,1)}, u32[]{:S(2)}, u32[]{:S(2)}) %collective-permute-start.30) | collective-permute-done | bytes 655392 | tf_op jit(solution)/shard_map/ppermute | solution.py:33
  544.9 5.9 %collective-permute-done.31 = bf16[4,128,640]{2,1,0:T(8,128)(2,1)} collective-permute-done((bf16[4,128,640]{2,1,0:T(8,128)(2,1)}, bf16[4,128,640]{2,1,0:T(8,128)(2,1)}, u32[]{:S(2)}, u32[]{:S(2)}) %collective-permute-start.31) | collective-permute-done | bytes 655392 | tf_op jit(solution)/shard_map/ppermute | solution.py:33
  (201 shorter events, 131.5 us)
Async XLA Ops:
  7.2 156.2 %all-gather.4.cloned.1.call-start = ((), (), s32[]{:S(2)}) async-start(), calls=%async_computation.8 | async-start | bytes 12533760 | tf_op jit(solution)/shard_map/all_gather | solution.py:301
  9.6 249.3 %all-gather.6.cloned.1.call-start = ((), (), s32[]{:S(2)}) async-start(), calls=%async_computation.10 | async-start | bytes 4177920 | tf_op jit(solution)/shard_map/all_gather | solution.py:302
  170.2 15.4 %collective-permute-start.2 = (bf16[128,768]{1,0:T(8,128)(2,1)S(1)}, bf16[128,768]{1,0:T(8,128)(2,1)S(1)}, u32[]{:S(2)}, u32[]{:S(2)}) collective-permute-start(bf16[128,768]{1,0:T(8,128)(2,1)S(1)} %get-tuple-element.84), channel_id=1, source_target_pairs={{0,24},{1,25},{2,26},{3,27},{4,28},{5,29},{6,30},{7,31},{8,0},{9,1... | collective-permute-start | bytes 589832 | tf_op jit(solution)/shard_map/ppermute | solution.py:33
  180.6 12.2 %collective-permute-start.1 = (bf16[64,768]{1,0:T(8,128)(2,1)S(1)}, bf16[64,768]{1,0:T(8,128)(2,1)S(1)}, u32[]{:S(2)}, u32[]{:S(2)}) collective-permute-start(bf16[64,768]{1,0:T(8,128)(2,1)S(1)} %slice.140), channel_id=1, source_target_pairs={{0,8},{1,9},{2,10},{3,11},{4,12},{5,13},{6,14},{7,15},{8,16},{9,17... | collective-permute-start | bytes 294920 | tf_op jit(solution)/shard_map/ppermute | solution.py:33
  185.7 11.9 %collective-permute-start.3 = (bf16[64,768]{1,0:T(8,128)(2,1)S(1)}, bf16[64,768]{1,0:T(8,128)(2,1)S(1)}, u32[]{:S(2)}, u32[]{:S(2)}) collective-permute-start(bf16[64,768]{1,0:T(8,128)(2,1)S(1)} %slice.141), channel_id=1, source_target_pairs={{0,24},{1,25},{2,26},{3,27},{4,28},{5,29},{6,30},{7,31},{8,0},{9,1... | collective-permute-start | bytes 294920 | tf_op jit(solution)/shard_map/ppermute | solution.py:33
  197.7 25.8 %collective-permute-start.4 = (bf16[4,128,768]{2,1,0:T(8,128)(2,1)S(1)}, bf16[4,128,768]{2,1,0:T(8,128)(2,1)S(1)}, u32[]{:S(2)}, u32[]{:S(2)}) collective-permute-start(bf16[4,128,768]{2,1,0:T(8,128)(2,1)S(1)} %get-tuple-element.70), channel_id=1, source_target_pairs={{0,32},{1,33},{2,34},{3,35},{4,36},{5,37},{6,38},{7,39},{8,40},{9,... | collective-permute-start | bytes 2359304 | tf_op jit(solution)/shard_map/ppermute | solution.py:33
  198.2 28.0 %collective-permute-start.6 = (bf16[4,128,768]{2,1,0:T(8,128)(2,1)S(1)}, bf16[4,128,768]{2,1,0:T(8,128)(2,1)S(1)}, u32[]{:S(2)}, u32[]{:S(2)}) collective-permute-start(bf16[4,128,768]{2,1,0:T(8,128)(2,1)S(1)} %get-tuple-element.70), channel_id=1, source_target_pairs={{0,96},{1,97},{2,98},{3,99},{4,100},{5,101},{6,102},{7,103},{8,104... | collective-permute-start | bytes 2359304 | tf_op jit(solution)/shard_map/ppermute | solution.py:33
  223.6 13.3 %collective-permute-start.5 = (bf16[4,64,768]{2,1,0:T(8,128)(2,1)S(1)}, bf16[4,64,768]{2,1,0:T(8,128)(2,1)}, u32[]{:S(2)}, u32[]{:S(2)}) collective-permute-start(bf16[4,64,768]{2,1,0:T(8,128)(2,1)S(1)} %slice.142), channel_id=1, source_target_pairs={{0,32},{1,33},{2,34},{3,35},{4,36},{5,37},{6,38},{7,39},{8,40},{9,... | collective-permute-start | bytes 1179656 | tf_op jit(solution)/shard_map/ppermute | solution.py:33
  226.9 12.5 %collective-permute-start.7 = (bf16[4,64,768]{2,1,0:T(8,128)(2,1)}, bf16[4,64,768]{2,1,0:T(8,128)(2,1)}, u32[]{:S(2)}, u32[]{:S(2)}) collective-permute-start(bf16[4,64,768]{2,1,0:T(8,128)(2,1)} %slice.143), channel_id=1, source_target_pairs={{0,96},{1,97},{2,98},{3,99},{4,100},{5,101},{6,102},{7,103},{8,104... | collective-permute-start | bytes 1179656 | tf_op jit(solution)/shard_map/ppermute | solution.py:33
  251.6 16.3 %all-to-all-start = ((bf16[8,128,384]{1,2,0:T(8,128)(2,1)}), bf16[8,128,384]{1,2,0:T(8,128)(2,1)S(1)}, u32[]{:S(2)}, u32[]{:S(2)}) async-start(bf16[8,128,384]{1,2,0:T(8,128)(2,1)} %broadcast_in_dim.39), calls=%async_computation | async-start | bytes 1572864 | tf_op jit(solution)/shard_map/all_to_all | solution.py:67
  276.7 22.9 %all-to-all-start.1 = ((bf16[8,128,640]{2,1,0:T(8,128)(2,1)}), bf16[8,128,640]{2,1,0:T(8,128)(2,1)S(1)}, u32[]{:S(2)}, u32[]{:S(2)}) async-start(bf16[8,128,640]{2,1,0:T(8,128)(2,1)} %broadcast_in_dim.40), calls=%async_computation.1 | async-start | bytes 2621440 | tf_op jit(solution)/shard_map/all_to_all | solution.py:67
  281.4 48.9 %reduce-scatter.2.cloned.1.call-start = ((), (), s32[]{:S(2)}) async-start(), calls=%async_computation.9 | async-start | bytes 1769472 | tf_op jit(solution)/shard_map/reduce_scatter | solution.py:331
  312.3 20.1 %collective-permute-start.24 = (bf16[4,128,512]{2,1,0:T(8,128)(2,1)S(1)}, bf16[4,128,512]{2,1,0:T(8,128)(2,1)}, u32[]{:S(2)}, u32[]{:S(2)}) collective-permute-start(bf16[4,128,512]{2,1,0:T(8,128)(2,1)S(1)} %get-tuple-element.77), channel_id=1, source_target_pairs={{128,136},{129,137},{130,138},{131,139},{132,140},{133,141},{134,1... | collective-permute-start | bytes 1572872 | tf_op jit(solution)/shard_map/ppermute | solution.py:33
  313.7 18.7 %collective-permute-start.26 = (bf16[4,128,512]{2,1,0:T(8,128)(2,1)S(1)}, bf16[4,128,512]{2,1,0:T(8,128)(2,1)}, u32[]{:S(2)}, u32[]{:S(2)}) collective-permute-start(bf16[4,128,512]{2,1,0:T(8,128)(2,1)S(1)} %get-tuple-element.77), channel_id=1, source_target_pairs={{128,152},{129,153},{130,154},{131,155},{132,156},{133,157},{134,1... | collective-permute-start | bytes 1572872 | tf_op jit(solution)/shard_map/ppermute | solution.py:33
  316.2 17.9 %collective-permute-start.19 = (bf16[4,128,640]{2,1,0:T(8,128)(2,1)}, bf16[4,128,640]{2,1,0:T(8,128)(2,1)}, u32[]{:S(2)}, u32[]{:S(2)}) collective-permute-start(bf16[4,128,640]{2,1,0:T(8,128)(2,1)} %get-tuple-element.75), channel_id=1, source_target_pairs={{128,192},{129,193},{130,194},{131,195},{132,196},{133,197},{134,1... | collective-permute-start | bytes 1966088 | tf_op jit(solution)/shard_map/ppermute | solution.py:33
  317.7 16.4 %collective-permute-start.18 = (bf16[4,128,640]{2,1,0:T(8,128)(2,1)}, bf16[4,128,640]{2,1,0:T(8,128)(2,1)}, u32[]{:S(2)}, u32[]{:S(2)}) collective-permute-start(bf16[4,128,640]{2,1,0:T(8,128)(2,1)} %get-tuple-element.75), channel_id=1, source_target_pairs={{128,160},{129,161},{130,162},{131,163},{132,164},{133,165},{134,1... | collective-permute-start | bytes 1966088 | tf_op jit(solution)/shard_map/ppermute | solution.py:33
  319.2 14.9 %collective-permute-start.20 = (bf16[4,128,640]{2,1,0:T(8,128)(2,1)}, bf16[4,128,640]{2,1,0:T(8,128)(2,1)}, u32[]{:S(2)}, u32[]{:S(2)}) collective-permute-start(bf16[4,128,640]{2,1,0:T(8,128)(2,1)} %get-tuple-element.75), channel_id=1, source_target_pairs={{128,224},{129,225},{130,226},{131,227},{132,228},{133,229},{134,2... | collective-permute-start | bytes 1966088 | tf_op jit(solution)/shard_map/ppermute | solution.py:33
  344.6 57.2 %all-to-all-start.2 = ((f32[8,2,128,128]{3,2,1,0:T(8,128)}), f32[8,2,128,128]{3,2,1,0:T(8,128)}, u32[]{:S(2)}, u32[]{:S(2)}) async-start(f32[8,2,128,128]{3,2,1,0:T(8,128)} %broadcast_in_dim.41), calls=%async_computation.3 | async-start | bytes 2097152 | tf_op jit(solution)/shard_map/all_to_all | solution.py:67
  352.6 12.9 %collective-permute-start.9 = (bf16[4,128,192]{1,2,0:T(8,128)(2,1)S(1)}, bf16[4,128,192]{1,2,0:T(8,128)(2,1)S(1)}, u32[]{:S(2)}, u32[]{:S(2)}) collective-permute-start(bf16[4,128,192]{1,2,0:T(8,128)(2,1)S(1)} %get-tuple-element.66), channel_id=1, source_target_pairs={{0,64},{1,65},{2,66},{3,67},{4,68},{5,69},{6,70},{7,71},{8,72},{9,... | collective-permute-start | bytes 589832 | tf_op jit(solution)/shard_map/ppermute | solution.py:33
  358.4 15.1 %collective-permute-start.8 = (bf16[4,128,192]{1,2,0:T(8,128)(2,1)S(1)}, bf16[4,128,192]{1,2,0:T(8,128)(2,1)S(1)}, u32[]{:S(2)}, u32[]{:S(2)}) collective-permute-start(bf16[4,128,192]{1,2,0:T(8,128)(2,1)S(1)} %get-tuple-element.67), channel_id=1, source_target_pairs={{0,32},{1,33},{2,34},{3,35},{4,36},{5,37},{6,38},{7,39},{8,40},{9,... | collective-permute-start | bytes 589832 | tf_op jit(solution)/shard_map/ppermute | solution.py:33
  361.2 12.4 %collective-permute-start.10 = (bf16[4,128,192]{1,2,0:T(8,128)(2,1)S(1)}, bf16[4,128,192]{1,2,0:T(8,128)(2,1)S(1)}, u32[]{:S(2)}, u32[]{:S(2)}) collective-permute-start(bf16[4,128,192]{1,2,0:T(8,128)(2,1)S(1)} %get-tuple-element.68), channel_id=1, source_target_pairs={{0,96},{1,97},{2,98},{3,99},{4,100},{5,101},{6,102},{7,103},{8,104... | collective-permute-start | bytes 589832 | tf_op jit(solution)/shard_map/ppermute | solution.py:33
  373.8 13.2 %collective-permute-start.13 = (bf16[4,128,192]{1,2,0:T(8,128)(2,1)S(1)}, bf16[4,128,192]{1,2,0:T(8,128)(2,1)S(1)}, u32[]{:S(2)}, u32[]{:S(2)}) collective-permute-start(bf16[4,128,192]{1,2,0:T(8,128)(2,1)S(1)} %get-tuple-element.62), channel_id=1, source_target_pairs={{0,24},{1,25},{2,26},{3,27},{4,28},{5,29},{6,30},{7,31},{8,0},{9,1... | collective-permute-start | bytes 589832 | tf_op jit(solution)/shard_map/ppermute | solution.py:33
  379.6 12.9 %collective-permute-start.12 = (bf16[4,128,192]{1,2,0:T(8,128)(2,1)S(1)}, bf16[4,128,192]{1,2,0:T(8,128)(2,1)S(1)}, u32[]{:S(2)}, u32[]{:S(2)}) collective-permute-start(bf16[4,128,192]{1,2,0:T(8,128)(2,1)S(1)} %get-tuple-element.63), channel_id=1, source_target_pairs={{0,16},{1,17},{2,18},{3,19},{4,20},{5,21},{6,22},{7,23},{8,24},{9,... | collective-permute-start | bytes 589832 | tf_op jit(solution)/shard_map/ppermute | solution.py:33
  385.0 11.0 %collective-permute-start.11 = (bf16[4,128,192]{1,2,0:T(8,128)(2,1)S(1)}, bf16[4,128,192]{1,2,0:T(8,128)(2,1)S(1)}, u32[]{:S(2)}, u32[]{:S(2)}) collective-permute-start(bf16[4,128,192]{1,2,0:T(8,128)(2,1)S(1)} %get-tuple-element.64), channel_id=1, source_target_pairs={{0,8},{1,9},{2,10},{3,11},{4,12},{5,13},{6,14},{7,15},{8,16},{9,17... | collective-permute-start | bytes 589832 | tf_op jit(solution)/shard_map/ppermute | solution.py:33
  408.9 34.6 %all-to-all-start.3 = ((bf16[16,128,256]{2,1,0:T(8,128)(2,1)}), bf16[16,128,256]{2,1,0:T(8,128)(2,1)S(1)}, u32[]{:S(2)}, u32[]{:S(2)}) async-start(bf16[16,128,256]{2,1,0:T(8,128)(2,1)} %broadcast_in_dim.43), calls=%async_computation.4 | async-start | bytes 2097152 | tf_op jit(solution)/shard_map/all_to_all | solution.py:67
  445.4 22.5 %all-to-all-start.5 = ((bf16[8,384,128]{2,1,0:T(8,128)(2,1)}), bf16[8,384,128]{2,1,0:T(8,128)(2,1)}, u32[]{:S(2)}, u32[]{:S(2)}) async-start(bf16[8,384,128]{2,1,0:T(8,128)(2,1)} %broadcast_in_dim.44), calls=%async_computation.6 | async-start | bytes 1572864 | tf_op jit(solution)/shard_map/all_to_all | solution.py:67
  467.8 22.8 %all-to-all-start.4 = ((bf16[8,128,640]{1,2,0:T(8,128)(2,1)}), bf16[8,128,640]{1,2,0:T(8,128)(2,1)S(1)}, u32[]{:S(2)}, u32[]{:S(2)}) async-start(bf16[8,128,640]{1,2,0:T(8,128)(2,1)} %fusion.15), calls=%async_computation.5 | async-start | bytes 2621440 | tf_op jit(solution)/shard_map/all_to_all | solution.py:365
  490.6 50.4 %all-to-all-start.6 = ((bf16[16,192,128]{2,1,0:T(8,128)(2,1)}), bf16[16,192,128]{2,1,0:T(8,128)(2,1)S(1)}, u32[]{:S(2)}, u32[]{:S(2)}) async-start(bf16[16,192,128]{2,1,0:T(8,128)(2,1)} %bitcast.80), calls=%async_computation.7 | async-start | bytes 1572864 | tf_op jit(solution)/shard_map/all_to_all | solution.py:373
  498.9 26.9 %collective-permute-start.30 = (bf16[4,128,640]{2,1,0:T(8,128)(2,1)S(1)}, bf16[4,128,640]{2,1,0:T(8,128)(2,1)}, u32[]{:S(2)}, u32[]{:S(2)}) collective-permute-start(bf16[4,128,640]{2,1,0:T(8,128)(2,1)S(1)} %pad_maximum_fusion.8), channel_id=1, source_target_pairs={{128,0},{129,1},{130,2},{131,3},{132,4},{133,5},{134,6},{135,7},{1... | collective-permute-start | bytes 1966088 | tf_op jit(solution)/shard_map/ppermute | solution.py:33
  525.7 19.2 %collective-permute-start.33 = (bf16[4,128,640]{2,1,0:T(8,128)(2,1)}, bf16[4,128,640]{2,1,0:T(8,128)(2,1)}, u32[]{:S(2)}, u32[]{:S(2)}) collective-permute-start(bf16[4,128,640]{2,1,0:T(8,128)(2,1)} %collective-permute-done.30), channel_id=1, source_target_pairs={{0,96},{1,97},{2,98},{3,99},{4,100},{5,101},{6,102},{7,103},{8,104... | collective-permute-start | bytes 1966088 | tf_op jit(solution)/shard_map/ppermute | solution.py:33
  529.5 15.5 %collective-permute-start.32 = (bf16[4,128,640]{2,1,0:T(8,128)(2,1)}, bf16[4,128,640]{2,1,0:T(8,128)(2,1)}, u32[]{:S(2)}, u32[]{:S(2)}) collective-permute-start(bf16[4,128,640]{2,1,0:T(8,128)(2,1)} %collective-permute-done.30), channel_id=1, source_target_pairs={{0,64},{1,65},{2,66},{3,67},{4,68},{5,69},{6,70},{7,71},{8,72},{9,... | collective-permute-start | bytes 1966088 | tf_op jit(solution)/shard_map/ppermute | solution.py:33
  532.2 18.6 %collective-permute-start.31 = (bf16[4,128,640]{2,1,0:T(8,128)(2,1)}, bf16[4,128,640]{2,1,0:T(8,128)(2,1)}, u32[]{:S(2)}, u32[]{:S(2)}) collective-permute-start(bf16[4,128,640]{2,1,0:T(8,128)(2,1)} %collective-permute-done.30), channel_id=1, source_target_pairs={{0,32},{1,33},{2,34},{3,35},{4,36},{5,37},{6,38},{7,39},{8,40},{9,... | collective-permute-start | bytes 1966088 | tf_op jit(solution)/shard_map/ppermute | solution.py:33
  (41 other events, 887.0 us)
Sparse Core Ops, SparseCore 0:
  10.5 152.8 all-gather.3
  165.9 77.5 all-gather.5
  284.8 45.4 reduce-scatter.1

commit v7 on v6

--- a/solution.py
+++ b/solution.py
@@ -362,15 +362,19 @@
     row_terms = jnp.einsum(
         "tk,bnk->btn", grads, weights.reshape(8, cols, 3 * width), preferred_element_type=F32
     )
-    row_terms = lax.all_to_all(row_terms.astype(BF16), "fsdp", 0, 0)
-    row_grad = jnp.sum(row_terms.astype(F32), axis=0)
+    product = mm(second_heads, fake_unit, 0, 0) - mm(first_heads, real_unit, 0, 0)
+    product = [product[i * HD : (i + 1) * HD] for i in range(width // HD)]
+    product = jnp.concatenate(product, axis=1).astype(BF16)
+    product = jnp.broadcast_to(product[None], (8,) + product.shape)
+    joined = jnp.concatenate([row_terms.astype(BF16), product], axis=2)
+    joined = lax.all_to_all(joined, "fsdp", 0, 0)
+    row_grad = jnp.sum(joined[:, :, :cols].astype(F32), axis=0)
     gain_cols = lax.dynamic_slice_in_dim(gains, start, cols, 0)
     direction = mm(fake_unit, head_in, 1, 1)
     input_grad = (inverse * row_grad * gain_cols + direction).astype(BF16)
 
-    product = mm(second_heads, fake_unit, 0, 0) - mm(first_heads, real_unit, 0, 0)
-    product = spread(product.astype(BF16), "fsdp").reshape(16, 192, -1)
-    product = lax.all_to_all(product, "seq", 0, 0)
+    product = [joined[:, :, i : i + HD] for i in range(cols, cols + width, HD)]
+    product = lax.all_to_all(jnp.stack(product, axis=1).reshape(16, 192, HD), "seq", 0, 0)
     product_high, product_low = split(jnp.sum(product.astype(F32), axis=0))
     term_crit = mm(product_high, head_in, 1, 1) + mm(product_low, head_in, 1, 1)
 

time: 572 us -> 577 us (level)
    all_to_all x2, waiting for transfers between devices: 16.4 us -> 25.4 us  [the longest x1 25.4 us: local(): joined = lax.all_to_all(joined, 'fsdp', 0, 0)]
    all_to_all x5 -> x4, starting transfers between devices: 33.7 us -> 26 us  [spread(): lax.all_to_all(jnp.broadcast_to(value[None], (count,) + value.shape), axi...]
    ppermute x35, waiting for transfers between devices: 101 us -> 95.5 us  [moved(): return lax.ppermute(value, AXES, pairs)]
    all_to_all x5 -> x4, waiting for transfers between devices: 46.8 us -> 47.6 us  [spread(): lax.all_to_all(jnp.broadcast_to(value[None], (count,) + value.shape), axi...]
  transfers between devices with their start and end apart: 45 -> 44, of which waited for: 22 -> 21; matrix products, arithmetic and copies ran while one was open for 10% -> 8% of each run, Pallas kernels for 2% -> 1%
where the time goes in v7:
time: 577 us; the launch traced here: 568 us
  waiting for transfers between devices  328 us (57%)
  starting transfers between devices  117 us (20%)
  matrix products  36.1 us (6%)
  other arithmetic  25.1 us (4%)
  local copies, waits for them, and re-layouts  23.1 us (4%)
  between operations  19.8 us (3%)
  Pallas kernels  18.7 us (3%)
    all_gather x1, waiting for transfers between devices, local(): weights = lax.all_gather(shard, 'seq', axis=0, tiled=True)  150 us
    ppermute x35, waiting for transfers between devices, moved(): return lax.ppermute(value, AXES, pairs)  95.5 us
    ppermute x35, starting transfers between devices, moved(): return lax.ppermute(value, AXES, pairs)  79.4 us
    all_to_all x4, waiting for transfers between devices, spread(): lax.all_to_all(jnp.broadcast_to(value[None], (count,) + value.shape), axi...  47.6 us
    all_to_all x4, starting transfers between devices, spread(): lax.all_to_all(jnp.broadcast_to(value[None], (count,) + value.shape), axi...  26 us
    all_to_all x1, waiting for transfers between devices, local(): joined = lax.all_to_all(joined, 'fsdp', 0, 0)  25.4 us
    dot_general x2, matrix products, times(): return jnp.dot(a, b, preferred_element_type=F32).astype(BF16)  13.1 us
  transfers between devices with their start and end apart: 44, of which 21 were waited for; matrix products, arithmetic and copies ran while one was open for 8% of the time, Pallas kernels for 1%

profile of v7, /device:TPU:32, one launch (start us, length us, event | category | flops | bytes accessed | tf_op | source)
XLA Modules:
  0.0 568.0 jit_solution(7813462984530862281)
XLA Ops:
  13.8 149.6 %all-gather.4.cloned.1.call-done = bf16[5120,1152]{1,0:T(8,128)(2,1)} async-done(((bf16[320,1152]{1,0:T(8,128)(2,1)}), bf16[5120,1152]{1,0:T(8,128)(2,1)}) %all-gather.4.cloned.1.call-update) | async-done | bytes 11796496 | tf_op jit(solution)/shard_map/all_gather | solution.py:301
  163.4 6.7 %convolution_convert_fusion.1 = bf16[128,1152]{1,0:T(8,128)(2,1)S(1)} fusion(bf16[5120,1152]{1,0:T(8,128)(2,1)} %all-gather.4.cloned.1.call-done, bf16[128,5120]{1,0:T(8,128)(2,1)} %get-tuple-element.58, f32[5120]{0:T(1024)S(1)} %bitcast.232, f32[128]{0:T(128)S(1)} %add_rsqrt_fusion.1), kind=kOutput, calls=%fused_computation.23 | convolution fusion | flops 1512718336 | bytes 13423104 | tf_op jit(solution)/shard_map/dot_general | solution.py:267
  170.2 4.1 collective-permute-start.2
  174.4 6.0 %collective-permute-done = bf16[128,768]{1,0:T(8,128)(2,1)S(1)} collective-permute-done((bf16[128,768]{1,0:T(8,128)(2,1)S(1)}, bf16[128,768]{1,0:T(8,128)(2,1)S(1)}, u32[]{:S(2)}, u32[]{:S(2)}) %collective-permute-start) | collective-permute-done | bytes 196640 | tf_op jit(solution)/shard_map/ppermute | solution.py:33
  180.4 4.8 collective-permute-start.1
  185.7 4.8 collective-permute-start.3
  192.8 4.7 collective-permute-done.3
  201.0 22.5 %collective-permute-done.4 = bf16[4,128,768]{2,1,0:T(8,128)(2,1)S(1)} collective-permute-done((bf16[4,128,768]{2,1,0:T(8,128)(2,1)S(1)}, bf16[4,128,768]{2,1,0:T(8,128)(2,1)S(1)}, u32[]{:S(2)}, u32[]{:S(2)}) %collective-permute-start.4) | collective-permute-done | bytes 786464 | tf_op jit(solution)/shard_map/ppermute | solution.py:33
  229.0 7.8 %collective-permute-done.5 = bf16[4,64,768]{2,1,0:T(8,128)(2,1)} collective-permute-done((bf16[4,64,768]{2,1,0:T(8,128)(2,1)S(1)}, bf16[4,64,768]{2,1,0:T(8,128)(2,1)}, u32[]{:S(2)}, u32[]{:S(2)}) %collective-permute-start.5) | collective-permute-done | bytes 393248 | tf_op jit(solution)/shard_map/ppermute | solution.py:33
  243.0 7.4 %conditional.1 = (bf16[128,384]{1,0:T(8,128)(2,1)S(1)}) conditional(s32[]{:T(128)} %convert_element_type.102, (bf16[128,384]{1,0:T(8,128)(2,1)S(1)}, bf16[2048,384]{1,0:T(8,128)(2,1)S(1)}, bf16[2048,384]{1,0:T(8,128)(2,1)S(1)}) %tuple.52, (s32[3]{0:T(128)S(1)}, f32[2048]{0:T(1024)S(1)}, bf16[128,384]{1,0:T(8,128)(2,1)S(1)}, ...), branch_computations={%region_1.2_spmd, %region_2.3_spmd} | conditional | bytes 73736 | solution.py:313
  243.2 7.2 %branch_1_fun.1 = bf16[128,384]{1,0:T(8,128)(2,1)S(1)} custom-call(s32[3]{0:T(128)S(1)} %get-tuple-element.52.frames, f32[8,2048]{1,0:T(8,128)S(1)} %broadcast_in_dim.89.mask, bf16[128,384]{1,0:T(8,128)(2,1)S(1)} %get-tuple-element.29.q, bf16[4,1024,384]{2,1,0:T(8,128)(2,1)S(1)} %get-tuple-element.53.k0.k1.k2, ...), custom_call_target="tpu_custom_call" | custom-call | tf_op jit(solution)/shard_map/cond/branch_1_fun/pallas_call | solution.py:117
  251.6 7.3 %all-to-all-start = ((bf16[8,128,384]{1,2,0:T(8,128)(2,1)}), bf16[8,128,384]{1,2,0:T(8,128)(2,1)S(1)}, u32[]{:S(2)}, u32[]{:S(2)}) async-start(bf16[8,128,384]{1,2,0:T(8,128)(2,1)} %broadcast_in_dim.39), calls=%async_computation | async-start | bytes 1572864 | tf_op jit(solution)/shard_map/all_to_all | solution.py:67
  263.4 4.4 all-to-all-done
  276.6 4.7 all-to-all-start.1
  282.1 17.4 %all-to-all-done.1 = bf16[8,128,640]{2,1,0:T(8,128)(2,1)S(1)} async-done(((bf16[8,128,640]{2,1,0:T(8,128)(2,1)}), bf16[8,128,640]{2,1,0:T(8,128)(2,1)S(1)}, u32[]{:S(2)}, u32[]{:S(2)}) %all-to-all-start.1) | async-done | bytes 1310752 | tf_op jit(solution)/shard_map/all_to_all | solution.py:67
  300.1 6.5 %convolution_convert_fusion = bf16[128,1152]{1,0:T(8,128)(2,1)S(1)} fusion(bf16[5120,1152]{1,0:T(8,128)(2,1)} %all-gather.4.cloned.1.call-done, bf16[128,5120]{1,0:T(8,128)(2,1)S(1)} %bitcast.207, f32[128]{0:T(128)S(1)} %add_rsqrt_fusion, f32[5120]{0:T(1024)S(1)} %bitcast.233), kind=kOutput, calls=%fused_computation.22 | convolution fusion | flops 1512718336 | bytes 13423104 | tf_op jit(solution)/shard_map/dot_general | solution.py:267
  322.0 8.4 %reduce-scatter.2.cloned.1.call-done = f32[384,128]{1,0:T(8,128)} async-done(((f32[3072,128]{1,0:T(8,128)}), f32[384,128]{1,0:T(8,128)}) %reduce-scatter.2.cloned.1.call-update) | async-done | bytes 196624 | tf_op jit(solution)/shard_map/reduce_scatter | solution.py:331
  344.6 6.3 %all-to-all-start.2 = ((f32[8,2,128,128]{3,2,1,0:T(8,128)}), f32[8,2,128,128]{3,2,1,0:T(8,128)}, u32[]{:S(2)}, u32[]{:S(2)}) async-start(f32[8,2,128,128]{3,2,1,0:T(8,128)} %broadcast_in_dim.41), calls=%async_computation.3 | async-start | bytes 2097152 | tf_op jit(solution)/shard_map/all_to_all | solution.py:67
  352.7 5.9 %collective-permute-start.9 = (bf16[4,128,192]{1,2,0:T(8,128)(2,1)S(1)}, bf16[4,128,192]{1,2,0:T(8,128)(2,1)S(1)}, u32[]{:S(2)}, u32[]{:S(2)}) collective-permute-start(bf16[4,128,192]{1,2,0:T(8,128)(2,1)S(1)} %get-tuple-element.69), channel_id=1, source_target_pairs={{0,64},{1,65},{2,66},{3,67},{4,68},{5,69},{6,70},{7,71},{8,72},{9,... | collective-permute-start | bytes 589832 | tf_op jit(solution)/shard_map/ppermute | solution.py:33
  360.9 4.8 collective-permute-start.10
  365.7 8.1 %collective-permute-done.8 = bf16[4,128,192]{1,2,0:T(8,128)(2,1)S(1)} collective-permute-done((bf16[4,128,192]{1,2,0:T(8,128)(2,1)S(1)}, bf16[4,128,192]{1,2,0:T(8,128)(2,1)S(1)}, u32[]{:S(2)}, u32[]{:S(2)}) %collective-permute-start.8) | collective-permute-done | bytes 196640 | tf_op jit(solution)/shard_map/ppermute | solution.py:33
  373.9 6.0 %collective-permute-start.13 = (bf16[4,128,192]{1,2,0:T(8,128)(2,1)S(1)}, bf16[4,128,192]{1,2,0:T(8,128)(2,1)S(1)}, u32[]{:S(2)}, u32[]{:S(2)}) collective-permute-start(bf16[4,128,192]{1,2,0:T(8,128)(2,1)S(1)} %get-tuple-element.65), channel_id=1, source_target_pairs={{0,24},{1,25},{2,26},{3,27},{4,28},{5,29},{6,30},{7,31},{8,0},{9,1... | collective-permute-start | bytes 589832 | tf_op jit(solution)/shard_map/ppermute | solution.py:33
  379.9 4.7 collective-permute-start.12
  408.7 7.6 %all-to-all-start.3 = ((bf16[16,128,256]{2,1,0:T(8,128)(2,1)}), bf16[16,128,256]{2,1,0:T(8,128)(2,1)S(1)}, u32[]{:S(2)}, u32[]{:S(2)}) async-start(bf16[16,128,256]{2,1,0:T(8,128)(2,1)} %broadcast_in_dim.43), calls=%async_computation.4 | async-start | bytes 2097152 | tf_op jit(solution)/shard_map/all_to_all | solution.py:67
  419.2 25.7 %all-to-all-done.3.sent = bf16[16,128,256]{2,1,0:T(8,128)(2,1)S(1)} async-done(((bf16[16,128,256]{2,1,0:T(8,128)(2,1)}), bf16[16,128,256]{2,1,0:T(8,128)(2,1)S(1)}, u32[]{:S(2)}, u32[]{:S(2)}) %all-to-all-start.3) | async-done | bytes 1048608 | tf_op jit(solution)/shard_map/all_to_all | solution.py:67
  450.0 7.6 %fusion.15 = bf16[8,128,640]{1,2,0:T(8,128)(2,1)S(1)} fusion(bf16[8,640,1152]{2,1,0:T(8,128)(2,1)} %bitcast.234, bf16[128,384]{1,0:T(8,128)(2,1)S(1)} %get-tuple-element.47, bf16[128,384]{1,0:T(8,128)(2,1)S(1)} %get-tuple-element.46, bf16[128,384]{1,0:T(8,128)(2,1)S(1)} %copy-done.5), kind=kOutput, calls=%fused_computation.32 | convolution fusion | flops 1511489536 | bytes 13402112 | tf_op jit(solution)/shard_map/tk,bnk->btn/dot_general | solution.py:362
  459.2 7.3 %all-to-all-start.4 = ((bf16[8,128,1024]{1,2,0:T(8,128)(2,1)}), bf16[8,128,1024]{1,2,0:T(8,128)(2,1)S(1)}, u32[]{:S(2)}, u32[]{:S(2)}) async-start(bf16[8,128,1024]{1,2,0:T(8,128)(2,1)} %pad_maximum_fusion.3), calls=%async_computation.5 | async-start | bytes 4194304 | tf_op jit(solution)/shard_map/all_to_all | solution.py:370
  467.3 25.4 %all-to-all-done.4 = bf16[8,128,1024]{1,2,0:T(8,128)(2,1)S(1)} async-done(((bf16[8,128,1024]{1,2,0:T(8,128)(2,1)}), bf16[8,128,1024]{1,2,0:T(8,128)(2,1)S(1)}, u32[]{:S(2)}, u32[]{:S(2)}) %all-to-all-start.4) | async-done | bytes 2097184 | tf_op jit(solution)/shard_map/all_to_all | solution.py:370
  496.0 4.3 all-to-all-start.5
  506.2 22.9 %collective-permute-done.30 = bf16[4,128,640]{2,1,0:T(8,128)(2,1)S(1)} collective-permute-done((bf16[4,128,640]{2,1,0:T(8,128)(2,1)S(1)}, bf16[4,128,640]{2,1,0:T(8,128)(2,1)S(1)}, u32[]{:S(2)}, u32[]{:S(2)}) %collective-permute-start.30) | collective-permute-done | bytes 655392 | tf_op jit(solution)/shard_map/ppermute | solution.py:33
  529.2 6.5 %collective-permute-start.33 = (bf16[4,128,640]{2,1,0:T(8,128)(2,1)S(1)}, bf16[4,128,640]{2,1,0:T(8,128)(2,1)}, u32[]{:S(2)}, u32[]{:S(2)}) collective-permute-start(bf16[4,128,640]{2,1,0:T(8,128)(2,1)S(1)} %collective-permute-done.30), channel_id=1, source_target_pairs={{0,96},{1,97},{2,98},{3,99},{4,100},{5,101},{6,102},{7,103},{8,104... | collective-permute-start | bytes 1966088 | tf_op jit(solution)/shard_map/ppermute | solution.py:33
  550.8 6.0 %collective-permute-done.31 = bf16[4,128,640]{2,1,0:T(8,128)(2,1)} collective-permute-done((bf16[4,128,640]{2,1,0:T(8,128)(2,1)S(1)}, bf16[4,128,640]{2,1,0:T(8,128)(2,1)}, u32[]{:S(2)}, u32[]{:S(2)}) %collective-permute-start.31) | collective-permute-done | bytes 655392 | tf_op jit(solution)/shard_map/ppermute | solution.py:33
  (209 shorter events, 131.9 us)
Async XLA Ops:
  7.2 156.2 %all-gather.4.cloned.1.call-start = ((), (), s32[]{:S(2)}) async-start(), calls=%async_computation.7 | async-start | bytes 12533760 | tf_op jit(solution)/shard_map/all_gather | solution.py:301
  9.6 249.3 %all-gather.6.cloned.1.call-start = ((), (), s32[]{:S(2)}) async-start(), calls=%async_computation.9 | async-start | bytes 4177920 | tf_op jit(solution)/shard_map/all_gather | solution.py:302
  170.1 10.2 %collective-permute-start = (bf16[128,768]{1,0:T(8,128)(2,1)S(1)}, bf16[128,768]{1,0:T(8,128)(2,1)S(1)}, u32[]{:S(2)}, u32[]{:S(2)}) collective-permute-start(bf16[128,768]{1,0:T(8,128)(2,1)S(1)} %get-tuple-element.87), channel_id=1, source_target_pairs={{0,8},{1,9},{2,10},{3,11},{4,12},{5,13},{6,14},{7,15},{8,16},{9,17... | collective-permute-start | bytes 589832 | tf_op jit(solution)/shard_map/ppermute | solution.py:33
  170.2 15.5 %collective-permute-start.2 = (bf16[128,768]{1,0:T(8,128)(2,1)S(1)}, bf16[128,768]{1,0:T(8,128)(2,1)S(1)}, u32[]{:S(2)}, u32[]{:S(2)}) collective-permute-start(bf16[128,768]{1,0:T(8,128)(2,1)S(1)} %get-tuple-element.87), channel_id=1, source_target_pairs={{0,24},{1,25},{2,26},{3,27},{4,28},{5,29},{6,30},{7,31},{8,0},{9,1... | collective-permute-start | bytes 589832 | tf_op jit(solution)/shard_map/ppermute | solution.py:33
  180.4 12.4 %collective-permute-start.1 = (bf16[64,768]{1,0:T(8,128)(2,1)S(1)}, bf16[64,768]{1,0:T(8,128)(2,1)S(1)}, u32[]{:S(2)}, u32[]{:S(2)}) collective-permute-start(bf16[64,768]{1,0:T(8,128)(2,1)S(1)} %slice.171), channel_id=1, source_target_pairs={{0,8},{1,9},{2,10},{3,11},{4,12},{5,13},{6,14},{7,15},{8,16},{9,17... | collective-permute-start | bytes 294920 | tf_op jit(solution)/shard_map/ppermute | solution.py:33
  185.7 11.9 %collective-permute-start.3 = (bf16[64,768]{1,0:T(8,128)(2,1)S(1)}, bf16[64,768]{1,0:T(8,128)(2,1)S(1)}, u32[]{:S(2)}, u32[]{:S(2)}) collective-permute-start(bf16[64,768]{1,0:T(8,128)(2,1)S(1)} %slice.172), channel_id=1, source_target_pairs={{0,24},{1,25},{2,26},{3,27},{4,28},{5,29},{6,30},{7,31},{8,0},{9,1... | collective-permute-start | bytes 294920 | tf_op jit(solution)/shard_map/ppermute | solution.py:33
  197.7 25.8 %collective-permute-start.4 = (bf16[4,128,768]{2,1,0:T(8,128)(2,1)S(1)}, bf16[4,128,768]{2,1,0:T(8,128)(2,1)S(1)}, u32[]{:S(2)}, u32[]{:S(2)}) collective-permute-start(bf16[4,128,768]{2,1,0:T(8,128)(2,1)S(1)} %get-tuple-element.73), channel_id=1, source_target_pairs={{0,32},{1,33},{2,34},{3,35},{4,36},{5,37},{6,38},{7,39},{8,40},{9,... | collective-permute-start | bytes 2359304 | tf_op jit(solution)/shard_map/ppermute | solution.py:33
  198.2 28.0 %collective-permute-start.6 = (bf16[4,128,768]{2,1,0:T(8,128)(2,1)S(1)}, bf16[4,128,768]{2,1,0:T(8,128)(2,1)S(1)}, u32[]{:S(2)}, u32[]{:S(2)}) collective-permute-start(bf16[4,128,768]{2,1,0:T(8,128)(2,1)S(1)} %get-tuple-element.73), channel_id=1, source_target_pairs={{0,96},{1,97},{2,98},{3,99},{4,100},{5,101},{6,102},{7,103},{8,104... | collective-permute-start | bytes 2359304 | tf_op jit(solution)/shard_map/ppermute | solution.py:33
  223.6 13.3 %collective-permute-start.5 = (bf16[4,64,768]{2,1,0:T(8,128)(2,1)S(1)}, bf16[4,64,768]{2,1,0:T(8,128)(2,1)}, u32[]{:S(2)}, u32[]{:S(2)}) collective-permute-start(bf16[4,64,768]{2,1,0:T(8,128)(2,1)S(1)} %slice.173), channel_id=1, source_target_pairs={{0,32},{1,33},{2,34},{3,35},{4,36},{5,37},{6,38},{7,39},{8,40},{9,... | collective-permute-start | bytes 1179656 | tf_op jit(solution)/shard_map/ppermute | solution.py:33
  226.9 12.5 %collective-permute-start.7 = (bf16[4,64,768]{2,1,0:T(8,128)(2,1)}, bf16[4,64,768]{2,1,0:T(8,128)(2,1)}, u32[]{:S(2)}, u32[]{:S(2)}) collective-permute-start(bf16[4,64,768]{2,1,0:T(8,128)(2,1)} %slice.174), channel_id=1, source_target_pairs={{0,96},{1,97},{2,98},{3,99},{4,100},{5,101},{6,102},{7,103},{8,104... | collective-permute-start | bytes 1179656 | tf_op jit(solution)/shard_map/ppermute | solution.py:33
  251.6 16.3 %all-to-all-start = ((bf16[8,128,384]{1,2,0:T(8,128)(2,1)}), bf16[8,128,384]{1,2,0:T(8,128)(2,1)S(1)}, u32[]{:S(2)}, u32[]{:S(2)}) async-start(bf16[8,128,384]{1,2,0:T(8,128)(2,1)} %broadcast_in_dim.39), calls=%async_computation | async-start | bytes 1572864 | tf_op jit(solution)/shard_map/all_to_all | solution.py:67
  276.6 22.9 %all-to-all-start.1 = ((bf16[8,128,640]{2,1,0:T(8,128)(2,1)}), bf16[8,128,640]{2,1,0:T(8,128)(2,1)S(1)}, u32[]{:S(2)}, u32[]{:S(2)}) async-start(bf16[8,128,640]{2,1,0:T(8,128)(2,1)} %broadcast_in_dim.40), calls=%async_computation.1 | async-start | bytes 2621440 | tf_op jit(solution)/shard_map/all_to_all | solution.py:67
  281.4 49.0 %reduce-scatter.2.cloned.1.call-start = ((), (), s32[]{:S(2)}) async-start(), calls=%async_computation.8 | async-start | bytes 1769472 | tf_op jit(solution)/shard_map/reduce_scatter | solution.py:331
  312.2 20.2 %collective-permute-start.24 = (bf16[4,128,512]{2,1,0:T(8,128)(2,1)S(1)}, bf16[4,128,512]{2,1,0:T(8,128)(2,1)}, u32[]{:S(2)}, u32[]{:S(2)}) collective-permute-start(bf16[4,128,512]{2,1,0:T(8,128)(2,1)S(1)} %get-tuple-element.80), channel_id=1, source_target_pairs={{128,136},{129,137},{130,138},{131,139},{132,140},{133,141},{134,1... | collective-permute-start | bytes 1572872 | tf_op jit(solution)/shard_map/ppermute | solution.py:33
  313.7 18.7 %collective-permute-start.26 = (bf16[4,128,512]{2,1,0:T(8,128)(2,1)S(1)}, bf16[4,128,512]{2,1,0:T(8,128)(2,1)}, u32[]{:S(2)}, u32[]{:S(2)}) collective-permute-start(bf16[4,128,512]{2,1,0:T(8,128)(2,1)S(1)} %get-tuple-element.80), channel_id=1, source_target_pairs={{128,152},{129,153},{130,154},{131,155},{132,156},{133,157},{134,1... | collective-permute-start | bytes 1572872 | tf_op jit(solution)/shard_map/ppermute | solution.py:33
  316.1 18.0 %collective-permute-start.19 = (bf16[4,128,640]{2,1,0:T(8,128)(2,1)}, bf16[4,128,640]{2,1,0:T(8,128)(2,1)}, u32[]{:S(2)}, u32[]{:S(2)}) collective-permute-start(bf16[4,128,640]{2,1,0:T(8,128)(2,1)} %get-tuple-element.78), channel_id=1, source_target_pairs={{128,192},{129,193},{130,194},{131,195},{132,196},{133,197},{134,1... | collective-permute-start | bytes 1966088 | tf_op jit(solution)/shard_map/ppermute | solution.py:33
  317.7 16.5 %collective-permute-start.18 = (bf16[4,128,640]{2,1,0:T(8,128)(2,1)}, bf16[4,128,640]{2,1,0:T(8,128)(2,1)}, u32[]{:S(2)}, u32[]{:S(2)}) collective-permute-start(bf16[4,128,640]{2,1,0:T(8,128)(2,1)} %get-tuple-element.78), channel_id=1, source_target_pairs={{128,160},{129,161},{130,162},{131,163},{132,164},{133,165},{134,1... | collective-permute-start | bytes 1966088 | tf_op jit(solution)/shard_map/ppermute | solution.py:33
  319.1 15.0 %collective-permute-start.20 = (bf16[4,128,640]{2,1,0:T(8,128)(2,1)}, bf16[4,128,640]{2,1,0:T(8,128)(2,1)}, u32[]{:S(2)}, u32[]{:S(2)}) collective-permute-start(bf16[4,128,640]{2,1,0:T(8,128)(2,1)} %get-tuple-element.78), channel_id=1, source_target_pairs={{128,224},{129,225},{130,226},{131,227},{132,228},{133,229},{134,2... | collective-permute-start | bytes 1966088 | tf_op jit(solution)/shard_map/ppermute | solution.py:33
  344.6 56.9 %all-to-all-start.2 = ((f32[8,2,128,128]{3,2,1,0:T(8,128)}), f32[8,2,128,128]{3,2,1,0:T(8,128)}, u32[]{:S(2)}, u32[]{:S(2)}) async-start(f32[8,2,128,128]{3,2,1,0:T(8,128)} %broadcast_in_dim.41), calls=%async_computation.3 | async-start | bytes 2097152 | tf_op jit(solution)/shard_map/all_to_all | solution.py:67
  352.7 12.9 %collective-permute-start.9 = (bf16[4,128,192]{1,2,0:T(8,128)(2,1)S(1)}, bf16[4,128,192]{1,2,0:T(8,128)(2,1)S(1)}, u32[]{:S(2)}, u32[]{:S(2)}) collective-permute-start(bf16[4,128,192]{1,2,0:T(8,128)(2,1)S(1)} %get-tuple-element.69), channel_id=1, source_target_pairs={{0,64},{1,65},{2,66},{3,67},{4,68},{5,69},{6,70},{7,71},{8,72},{9,... | collective-permute-start | bytes 589832 | tf_op jit(solution)/shard_map/ppermute | solution.py:33
  358.6 15.2 %collective-permute-start.8 = (bf16[4,128,192]{1,2,0:T(8,128)(2,1)S(1)}, bf16[4,128,192]{1,2,0:T(8,128)(2,1)S(1)}, u32[]{:S(2)}, u32[]{:S(2)}) collective-permute-start(bf16[4,128,192]{1,2,0:T(8,128)(2,1)S(1)} %get-tuple-element.70), channel_id=1, source_target_pairs={{0,32},{1,33},{2,34},{3,35},{4,36},{5,37},{6,38},{7,39},{8,40},{9,... | collective-permute-start | bytes 589832 | tf_op jit(solution)/shard_map/ppermute | solution.py:33
  360.9 12.9 %collective-permute-start.10 = (bf16[4,128,192]{1,2,0:T(8,128)(2,1)S(1)}, bf16[4,128,192]{1,2,0:T(8,128)(2,1)S(1)}, u32[]{:S(2)}, u32[]{:S(2)}) collective-permute-start(bf16[4,128,192]{1,2,0:T(8,128)(2,1)S(1)} %get-tuple-element.71), channel_id=1, source_target_pairs={{0,96},{1,97},{2,98},{3,99},{4,100},{5,101},{6,102},{7,103},{8,104... | collective-permute-start | bytes 589832 | tf_op jit(solution)/shard_map/ppermute | solution.py:33
  373.9 14.3 %collective-permute-start.13 = (bf16[4,128,192]{1,2,0:T(8,128)(2,1)S(1)}, bf16[4,128,192]{1,2,0:T(8,128)(2,1)S(1)}, u32[]{:S(2)}, u32[]{:S(2)}) collective-permute-start(bf16[4,128,192]{1,2,0:T(8,128)(2,1)S(1)} %get-tuple-element.65), channel_id=1, source_target_pairs={{0,24},{1,25},{2,26},{3,27},{4,28},{5,29},{6,30},{7,31},{8,0},{9,1... | collective-permute-start | bytes 589832 | tf_op jit(solution)/shard_map/ppermute | solution.py:33
  379.9 12.4 %collective-permute-start.12 = (bf16[4,128,192]{1,2,0:T(8,128)(2,1)S(1)}, bf16[4,128,192]{1,2,0:T(8,128)(2,1)S(1)}, u32[]{:S(2)}, u32[]{:S(2)}) collective-permute-start(bf16[4,128,192]{1,2,0:T(8,128)(2,1)S(1)} %get-tuple-element.66), channel_id=1, source_target_pairs={{0,16},{1,17},{2,18},{3,19},{4,20},{5,21},{6,22},{7,23},{8,24},{9,... | collective-permute-start | bytes 589832 | tf_op jit(solution)/shard_map/ppermute | solution.py:33
  384.6 11.1 %collective-permute-start.11 = (bf16[4,128,192]{1,2,0:T(8,128)(2,1)S(1)}, bf16[4,128,192]{1,2,0:T(8,128)(2,1)S(1)}, u32[]{:S(2)}, u32[]{:S(2)}) collective-permute-start(bf16[4,128,192]{1,2,0:T(8,128)(2,1)S(1)} %get-tuple-element.67), channel_id=1, source_target_pairs={{0,8},{1,9},{2,10},{3,11},{4,12},{5,13},{6,14},{7,15},{8,16},{9,17... | collective-permute-start | bytes 589832 | tf_op jit(solution)/shard_map/ppermute | solution.py:33
  408.7 36.2 %all-to-all-start.3 = ((bf16[16,128,256]{2,1,0:T(8,128)(2,1)}), bf16[16,128,256]{2,1,0:T(8,128)(2,1)S(1)}, u32[]{:S(2)}, u32[]{:S(2)}) async-start(bf16[16,128,256]{2,1,0:T(8,128)(2,1)} %broadcast_in_dim.43), calls=%async_computation.4 | async-start | bytes 2097152 | tf_op jit(solution)/shard_map/all_to_all | solution.py:67
  459.2 33.4 %all-to-all-start.4 = ((bf16[8,128,1024]{1,2,0:T(8,128)(2,1)}), bf16[8,128,1024]{1,2,0:T(8,128)(2,1)S(1)}, u32[]{:S(2)}, u32[]{:S(2)}) async-start(bf16[8,128,1024]{1,2,0:T(8,128)(2,1)} %pad_maximum_fusion.3), calls=%async_computation.5 | async-start | bytes 4194304 | tf_op jit(solution)/shard_map/all_to_all | solution.py:370
  496.0 51.3 %all-to-all-start.5 = ((bf16[16,192,128]{2,1,0:T(8,128)(2,1)}), bf16[16,192,128]{2,1,0:T(8,128)(2,1)}, u32[]{:S(2)}, u32[]{:S(2)}) async-start(bf16[16,192,128]{2,1,0:T(8,128)(2,1)} %bitcast.204), calls=%async_computation.6 | async-start | bytes 1572864 | tf_op jit(solution)/shard_map/all_to_all | solution.py:377
  504.9 24.2 %collective-permute-start.30 = (bf16[4,128,640]{2,1,0:T(8,128)(2,1)S(1)}, bf16[4,128,640]{2,1,0:T(8,128)(2,1)S(1)}, u32[]{:S(2)}, u32[]{:S(2)}) collective-permute-start(bf16[4,128,640]{2,1,0:T(8,128)(2,1)S(1)} %pad_maximum_fusion.10), channel_id=1, source_target_pairs={{128,0},{129,1},{130,2},{131,3},{132,4},{133,5},{134,6},{135,7},{1... | collective-permute-start | bytes 1966088 | tf_op jit(solution)/shard_map/ppermute | solution.py:33
  529.2 21.6 %collective-permute-start.33 = (bf16[4,128,640]{2,1,0:T(8,128)(2,1)S(1)}, bf16[4,128,640]{2,1,0:T(8,128)(2,1)}, u32[]{:S(2)}, u32[]{:S(2)}) collective-permute-start(bf16[4,128,640]{2,1,0:T(8,128)(2,1)S(1)} %collective-permute-done.30), channel_id=1, source_target_pairs={{0,96},{1,97},{2,98},{3,99},{4,100},{5,101},{6,102},{7,103},{8,104... | collective-permute-start | bytes 1966088 | tf_op jit(solution)/shard_map/ppermute | solution.py:33
  535.7 15.1 %collective-permute-start.32 = (bf16[4,128,640]{2,1,0:T(8,128)(2,1)S(1)}, bf16[4,128,640]{2,1,0:T(8,128)(2,1)}, u32[]{:S(2)}, u32[]{:S(2)}) collective-permute-start(bf16[4,128,640]{2,1,0:T(8,128)(2,1)S(1)} %collective-permute-done.30), channel_id=1, source_target_pairs={{0,64},{1,65},{2,66},{3,67},{4,68},{5,69},{6,70},{7,71},{8,72},{9,... | collective-permute-start | bytes 1966088 | tf_op jit(solution)/shard_map/ppermute | solution.py:33
  538.4 18.4 %collective-permute-start.31 = (bf16[4,128,640]{2,1,0:T(8,128)(2,1)S(1)}, bf16[4,128,640]{2,1,0:T(8,128)(2,1)}, u32[]{:S(2)}, u32[]{:S(2)}) collective-permute-start(bf16[4,128,640]{2,1,0:T(8,128)(2,1)S(1)} %collective-permute-done.30), channel_id=1, source_target_pairs={{0,32},{1,33},{2,34},{3,35},{4,36},{5,37},{6,38},{7,39},{8,40},{9,... | collective-permute-start | bytes 1966088 | tf_op jit(solution)/shard_map/ppermute | solution.py:33
  (42 other events, 937.1 us)
Sparse Core Ops, SparseCore 0:
  10.5 152.8 all-gather.3
  165.9 77.5 all-gather.5
  284.7 45.5 reduce-scatter.1

commit v8 on v6

--- a/solution.py
+++ b/solution.py
@@ -6,6 +6,7 @@
 from jax.sharding import PartitionSpec as P
 
 HD = 128
+STATS = 32
 EPS = 1e-06
 NEG = -1e30
 AXES = ("grp", "seq", "fsdp")
@@ -197,8 +198,8 @@
             term = stat.astype(BF16).astype(F32)
             table = jnp.where(lane == 3 * i + j, term, table)
             stat = stat - term
-    sent[:, :HD] = unit
-    sent[:, HD:] = table.astype(BF16)
+    sent[:HD, :] = unit
+    sent[HD:, :] = table.T[:STATS, :].astype(BF16)
 
 
 def query_grads(query, lead, tail, lse, unit, high, low, score):
@@ -207,13 +208,13 @@
         query_kernel,
         out_shape=(
             jax.ShapeDtypeStruct((rows, width), BF16),
-            jax.ShapeDtypeStruct((rows, 2 * HD), BF16),
+            jax.ShapeDtypeStruct((rows + STATS, HD), BF16),
         ),
         compiler_params=VMEM,
     )(query, lead, tail, lse, unit, high, low, score)
 
 
-def key_kernel(at, k, v, tail, sent, high, low, key_grad, value_grad, ordered_sent):
+def key_kernel(at, k, v, tail, sent, high, low, key_grad, value_grad, units, table_of):
     scale = HD ** (-0.5)
     rows, width = k.shape
     y, z = at[0] // 4, at[0] % 4
@@ -221,9 +222,11 @@
         for dz in range(4):
             place = ((y + 4 - dy) % 4) * 4 + (z + 4 - dz) % 4
             block = (4 * dy + dz) * rows
-            ordered_sent[block : block + rows, :] = sent[pl.ds(place, 1)][0]
-    unit = ordered_sent[:, :HD]
-    table = ordered_sent[:, HD:].astype(F32)
+            came = sent[pl.ds(place, 1)][0]
+            units[block : block + rows, :] = came[:rows, :]
+            table_of[block : block + rows, :] = came[rows:, :].astype(F32).T
+    unit = units[...]
+    table = table_of[...]
 
     def stat(i):
         return table[:, 3 * i : 3 * i + 1] + table[:, 3 * i + 1 : 3 * i + 2] + table[:, 3 * i + 2 : 3 * i + 3]
@@ -247,7 +250,10 @@
         key_kernel,
         in_specs=[pl.BlockSpec(memory_space=pltpu.SMEM)] + [whole] * 6,
         out_shape=(shape, shape),
-        scratch_shapes=[pltpu.VMEM((tail.shape[0], sent.shape[-1]), BF16)],
+        scratch_shapes=[
+            pltpu.VMEM((tail.shape[0], HD), BF16),
+            pltpu.VMEM((tail.shape[0], STATS), F32),
+        ],
         compiler_params=VMEM,
     )(at, keys, values, tail, sent, high, low)
 
@@ -349,7 +355,8 @@
     second_heads, lse = critic_attention(second_q, every_lead, every_tail)
     second_cols = lax.dynamic_slice_in_dim(second_rows, start, cols, 1)
     units = jnp.stack([units_of(real_cols, after(first_heads, second_heads)), units_of(second_cols, second_heads)])
-    units = after(jnp.sum(spread(units, "fsdp"), axis=0), gen_heads)
+    units = spread(units.astype(BF16), "fsdp").astype(F32)
+    units = after(jnp.sum(units, axis=0), gen_heads)
     real_score, real_unit = unit_terms(units[0], head_out)
     fake_score, fake_unit = unit_terms(units[1], head_out)
     query_grad, sent = query_grads(
@@ -378,8 +385,8 @@
     back = back.reshape(tokens, cols)
     term_gen = mm(gen_heads, back, 0, 0)
 
-    stats = sent[:, :, HD:].astype(F32)
-    margin = jnp.sum(stats[:, :, 18:21]) / tokens
+    stats = sent[:, rows:, :].astype(F32)
+    margin = jnp.sum(stats[:, 18:21, :]) / tokens
     margin_back = across(jnp.broadcast_to(margin, (8, HD)), CRIT)[0, 0]
     margin = jnp.where(is_gen, margin_back, margin)
     signed = jnp.where(is_gen, margin, -margin)

time: 572 us -> 555 us (0.970)
  waiting for transfers between devices: 324 us -> 314 us
    ppermute x35, waiting for transfers between devices: 101 us -> 91.2 us  [moved(): return lax.ppermute(value, AXES, pairs)]
  transfers between devices with their start and end apart: 45 -> 45, of which waited for: 22 -> 20; matrix products, arithmetic and copies ran while one was open for 10% -> 11% of each run, Pallas kernels for 2% -> 3%
where the time goes in v8:
time: 555 us; the launch traced here: 546 us
  waiting for transfers between devices  314 us (57%)
  starting transfers between devices  118 us (21%)
  matrix products  36.4 us (7%)
  between operations  19.8 us (4%)
  other arithmetic  19.7 us (4%)
  Pallas kernels  19.2 us (3%)
  local copies, waits for them, and re-layouts  18.7 us (3%)
    all_gather x1, waiting for transfers between devices, local(): weights = lax.all_gather(shard, 'seq', axis=0, tiled=True)  150 us
    ppermute x35, waiting for transfers between devices, moved(): return lax.ppermute(value, AXES, pairs)  91.2 us
    ppermute x35, starting transfers between devices, moved(): return lax.ppermute(value, AXES, pairs)  76.6 us
    all_to_all x5, waiting for transfers between devices, spread(): lax.all_to_all(jnp.broadcast_to(value[None], (count,) + value.shape), axi...  42.9 us
    all_to_all x5, starting transfers between devices, spread(): lax.all_to_all(jnp.broadcast_to(value[None], (count,) + value.shape), axi...  31.1 us
    all_to_all x1, waiting for transfers between devices, local(): row_terms = lax.all_to_all(row_terms.astype(BF16), 'fsdp', 0, 0)  15.3 us
    reduce_scatter x1, waiting for transfers between devices, local(): lax.psum_scatter(joint, 'fsdp', scatter_dimension=0, tiled=True)  13.5 us
    dot_general x2, matrix products, times(): return jnp.dot(a, b, preferred_element_type=F32).astype(BF16)  13.1 us
  transfers between devices with their start and end apart: 45, of which 20 were waited for; matrix products, arithmetic and copies ran while one was open for 11% of the time, Pallas kernels for 3%

profile of v8, /device:TPU:32, one launch (start us, length us, event | category | flops | bytes accessed | tf_op | source)
XLA Modules:
  0.0 546.3 jit_solution(12416280639911456883)
XLA Ops:
  13.8 149.6 %all-gather.4.cloned.1.call-done = bf16[5120,1152]{1,0:T(8,128)(2,1)} async-done(((bf16[320,1152]{1,0:T(8,128)(2,1)}), bf16[5120,1152]{1,0:T(8,128)(2,1)}) %all-gather.4.cloned.1.call-update) | async-done | bytes 11796496 | tf_op jit(solution)/shard_map/all_gather | solution.py:307
  163.4 6.7 %convolution_convert_fusion.1 = bf16[128,1152]{1,0:T(8,128)(2,1)S(1)} fusion(bf16[5120,1152]{1,0:T(8,128)(2,1)} %all-gather.4.cloned.1.call-done, bf16[128,5120]{1,0:T(8,128)(2,1)} %get-tuple-element.58, f32[5120]{0:T(1024)S(1)} %bitcast.223, f32[128]{0:T(128)S(1)} %add_rsqrt_fusion.1), kind=kOutput, calls=%fused_computation.23 | convolution fusion | flops 1512718336 | bytes 13423104 | tf_op jit(solution)/shard_map/dot_general | solution.py:273
  174.4 6.0 %collective-permute-done = bf16[128,768]{1,0:T(8,128)(2,1)S(1)} collective-permute-done((bf16[128,768]{1,0:T(8,128)(2,1)S(1)}, bf16[128,768]{1,0:T(8,128)(2,1)S(1)}, u32[]{:S(2)}, u32[]{:S(2)}) %collective-permute-start) | collective-permute-done | bytes 196640 | tf_op jit(solution)/shard_map/ppermute | solution.py:34
  180.4 4.9 collective-permute-start.1
  185.7 4.8 collective-permute-start.3
  192.8 4.7 collective-permute-done.3
  201.1 22.5 %collective-permute-done.4 = bf16[4,128,768]{2,1,0:T(8,128)(2,1)S(1)} collective-permute-done((bf16[4,128,768]{2,1,0:T(8,128)(2,1)S(1)}, bf16[4,128,768]{2,1,0:T(8,128)(2,1)S(1)}, u32[]{:S(2)}, u32[]{:S(2)}) %collective-permute-start.4) | collective-permute-done | bytes 786464 | tf_op jit(solution)/shard_map/ppermute | solution.py:34
  229.1 7.8 %collective-permute-done.5 = bf16[4,64,768]{2,1,0:T(8,128)(2,1)} collective-permute-done((bf16[4,64,768]{2,1,0:T(8,128)(2,1)S(1)}, bf16[4,64,768]{2,1,0:T(8,128)(2,1)}, u32[]{:S(2)}, u32[]{:S(2)}) %collective-permute-start.5) | collective-permute-done | bytes 393248 | tf_op jit(solution)/shard_map/ppermute | solution.py:34
  243.0 7.4 %conditional.1 = (bf16[128,384]{1,0:T(8,128)(2,1)S(1)}) conditional(s32[]{:T(128)} %convert_element_type.108, (bf16[128,384]{1,0:T(8,128)(2,1)S(1)}, bf16[2048,384]{1,0:T(8,128)(2,1)S(1)}, bf16[2048,384]{1,0:T(8,128)(2,1)S(1)}) %tuple.48, (s32[3]{0:T(128)S(1)}, f32[2048]{0:T(1024)S(1)}, bf16[128,384]{1,0:T(8,128)(2,1)S(1)}, ...), branch_computations={%region_1.2_spmd, %region_2.3_spmd} | conditional | bytes 73736 | solution.py:319
  243.2 7.2 %branch_1_fun.1 = bf16[128,384]{1,0:T(8,128)(2,1)S(1)} custom-call(s32[3]{0:T(128)S(1)} %get-tuple-element.52.frames, f32[8,2048]{1,0:T(8,128)S(1)} %broadcast_in_dim.89.mask, bf16[128,384]{1,0:T(8,128)(2,1)S(1)} %get-tuple-element.29.q, bf16[4,1024,384]{2,1,0:T(8,128)(2,1)S(1)} %get-tuple-element.53.k0.k1.k2, ...), custom_call_target="tpu_custom_call" | custom-call | tf_op jit(solution)/shard_map/cond/branch_1_fun/pallas_call | solution.py:118
  251.6 8.0 %all-to-all-start = ((bf16[8,128,384]{1,2,0:T(8,128)(2,1)}), bf16[8,128,384]{1,2,0:T(8,128)(2,1)}, u32[]{:S(2)}, u32[]{:S(2)}) async-start(bf16[8,128,384]{1,2,0:T(8,128)(2,1)} %broadcast_in_dim.39), calls=%async_computation | async-start | bytes 1572864 | tf_op jit(solution)/shard_map/all_to_all | solution.py:68
  264.1 4.5 all-to-all-done
  276.6 4.7 all-to-all-start.1
  282.1 17.4 %all-to-all-done.1 = bf16[8,128,640]{2,1,0:T(8,128)(2,1)S(1)} async-done(((bf16[8,128,640]{2,1,0:T(8,128)(2,1)}), bf16[8,128,640]{2,1,0:T(8,128)(2,1)S(1)}, u32[]{:S(2)}, u32[]{:S(2)}) %all-to-all-start.1) | async-done | bytes 1310752 | tf_op jit(solution)/shard_map/all_to_all | solution.py:68
  300.0 6.5 %convolution_convert_fusion = bf16[128,1152]{1,0:T(8,128)(2,1)S(1)} fusion(bf16[5120,1152]{1,0:T(8,128)(2,1)} %all-gather.4.cloned.1.call-done, bf16[128,5120]{1,0:T(8,128)(2,1)S(1)} %bitcast.200, f32[128]{0:T(128)S(1)} %add_rsqrt_fusion, f32[5120]{0:T(1024)S(1)} %bitcast.224), kind=kOutput, calls=%fused_computation.22 | convolution fusion | flops 1512718336 | bytes 13423104 | tf_op jit(solution)/shard_map/dot_general | solution.py:273
  316.2 13.5 %reduce-scatter.2.cloned.1.call-done = f32[384,128]{1,0:T(8,128)} async-done(((f32[3072,128]{1,0:T(8,128)}), f32[384,128]{1,0:T(8,128)}) %reduce-scatter.2.cloned.1.call-update) | async-done | bytes 196624 | tf_op jit(solution)/shard_map/reduce_scatter | solution.py:337
  338.0 5.2 collective-permute-start.9
  347.5 4.6 collective-permute-start.10
  360.9 7.1 %all-to-all-start.2 = ((bf16[8,2,128,128]{3,2,1,0:T(8,128)(2,1)}), bf16[8,2,128,128]{3,2,1,0:T(8,128)(2,1)}, u32[]{:S(2)}, u32[]{:S(2)}) async-start(bf16[8,2,128,128]{3,2,1,0:T(8,128)(2,1)} %broadcast_in_dim.41), calls=%async_computation.3 | async-start | bytes 1048576 | tf_op jit(solution)/shard_map/all_to_all | solution.py:68
  369.3 4.8 collective-permute-start.13
  374.0 6.7 %collective-permute-start.12 = (bf16[4,128,192]{1,2,0:T(8,128)(2,1)S(1)}, bf16[4,128,192]{1,2,0:T(8,128)(2,1)S(1)}, u32[]{:S(2)}, u32[]{:S(2)}) collective-permute-start(bf16[4,128,192]{1,2,0:T(8,128)(2,1)S(1)} %get-tuple-element.63), channel_id=1, source_target_pairs={{0,16},{1,17},{2,18},{3,19},{4,20},{5,21},{6,22},{7,23},{8,24},{9,... | collective-permute-start | bytes 589832 | tf_op jit(solution)/shard_map/ppermute | solution.py:34
  384.6 4.2 collective-permute-done.12
  404.5 5.1 all-to-all-start.3
  410.9 20.9 %all-to-all-done.3.sent = bf16[16,160,128]{2,1,0:T(8,128)(2,1)S(1)} async-done(((bf16[16,160,128]{2,1,0:T(8,128)(2,1)}), bf16[16,160,128]{2,1,0:T(8,128)(2,1)S(1)}, u32[]{:S(2)}, u32[]{:S(2)}) %all-to-all-start.3) | async-done | bytes 655392 | tf_op jit(solution)/shard_map/all_to_all | solution.py:68
  432.9 6.3 %all-to-all-start.5 = ((bf16[8,384,128]{2,1,0:T(8,128)(2,1)}), bf16[8,384,128]{2,1,0:T(8,128)(2,1)}, u32[]{:S(2)}, u32[]{:S(2)}) async-start(bf16[8,384,128]{2,1,0:T(8,128)(2,1)} %broadcast_in_dim.44), calls=%async_computation.6 | async-start | bytes 1572864 | tf_op jit(solution)/shard_map/all_to_all | solution.py:68
  443.1 8.7 %fusion.15 = bf16[8,128,640]{1,2,0:T(8,128)(2,1)} fusion(bf16[8,640,1152]{2,1,0:T(8,128)(2,1)} %bitcast.225, bf16[128,384]{1,0:T(8,128)(2,1)S(1)} %get-tuple-element.47, bf16[128,384]{1,0:T(8,128)(2,1)S(1)} %get-tuple-element.46, bf16[128,384]{1,0:T(8,128)(2,1)S(1)} %get-tuple-element.44), kind=kOutput, calls=%fused_computation.31 | convolution fusion | flops 1511489536 | bytes 13402112 | tf_op jit(solution)/shard_map/tk,bnk->btn/dot_general | solution.py:369
  451.7 5.7 %all-to-all-start.4 = ((bf16[8,128,640]{1,2,0:T(8,128)(2,1)}), bf16[8,128,640]{1,2,0:T(8,128)(2,1)S(1)}, u32[]{:S(2)}, u32[]{:S(2)}) async-start(bf16[8,128,640]{1,2,0:T(8,128)(2,1)} %fusion.15), calls=%async_computation.5 | async-start | bytes 2621440 | tf_op jit(solution)/shard_map/all_to_all | solution.py:372
  458.1 15.3 %all-to-all-done.4 = bf16[8,128,640]{1,2,0:T(8,128)(2,1)S(1)} async-done(((bf16[8,128,640]{1,2,0:T(8,128)(2,1)}), bf16[8,128,640]{1,2,0:T(8,128)(2,1)S(1)}, u32[]{:S(2)}, u32[]{:S(2)}) %all-to-all-start.4) | async-done | bytes 1310752 | tf_op jit(solution)/shard_map/all_to_all | solution.py:372
  473.4 4.8 all-to-all-start.6
  484.1 25.1 %collective-permute-done.30 = bf16[4,128,640]{2,1,0:T(8,128)(2,1)} collective-permute-done((bf16[4,128,640]{2,1,0:T(8,128)(2,1)S(1)}, bf16[4,128,640]{2,1,0:T(8,128)(2,1)}, u32[]{:S(2)}, u32[]{:S(2)}) %collective-permute-start.30) | collective-permute-done | bytes 655392 | tf_op jit(solution)/shard_map/ppermute | solution.py:34
  509.2 4.4 collective-permute-start.33
  529.0 5.9 %collective-permute-done.31 = bf16[4,128,640]{2,1,0:T(8,128)(2,1)} collective-permute-done((bf16[4,128,640]{2,1,0:T(8,128)(2,1)}, bf16[4,128,640]{2,1,0:T(8,128)(2,1)}, u32[]{:S(2)}, u32[]{:S(2)}) %collective-permute-start.31) | collective-permute-done | bytes 655392 | tf_op jit(solution)/shard_map/ppermute | solution.py:34
  (191 shorter events, 122.8 us)
Async XLA Ops:
  7.2 156.2 %all-gather.4.cloned.1.call-start = ((), (), s32[]{:S(2)}) async-start(), calls=%async_computation.8 | async-start | bytes 12533760 | tf_op jit(solution)/shard_map/all_gather | solution.py:307
  9.6 250.0 %all-gather.6.cloned.1.call-start = ((), (), s32[]{:S(2)}) async-start(), calls=%async_computation.10 | async-start | bytes 4177920 | tf_op jit(solution)/shard_map/all_gather | solution.py:308
  170.2 15.5 %collective-permute-start.2 = (bf16[128,768]{1,0:T(8,128)(2,1)S(1)}, bf16[128,768]{1,0:T(8,128)(2,1)S(1)}, u32[]{:S(2)}, u32[]{:S(2)}) collective-permute-start(bf16[128,768]{1,0:T(8,128)(2,1)S(1)} %get-tuple-element.84), channel_id=1, source_target_pairs={{0,24},{1,25},{2,26},{3,27},{4,28},{5,29},{6,30},{7,31},{8,0},{9,1... | collective-permute-start | bytes 589832 | tf_op jit(solution)/shard_map/ppermute | solution.py:34
  180.4 12.4 %collective-permute-start.1 = (bf16[64,768]{1,0:T(8,128)(2,1)S(1)}, bf16[64,768]{1,0:T(8,128)(2,1)S(1)}, u32[]{:S(2)}, u32[]{:S(2)}) collective-permute-start(bf16[64,768]{1,0:T(8,128)(2,1)S(1)} %slice.140), channel_id=1, source_target_pairs={{0,8},{1,9},{2,10},{3,11},{4,12},{5,13},{6,14},{7,15},{8,16},{9,17... | collective-permute-start | bytes 294920 | tf_op jit(solution)/shard_map/ppermute | solution.py:34
  197.7 25.8 %collective-permute-start.4 = (bf16[4,128,768]{2,1,0:T(8,128)(2,1)S(1)}, bf16[4,128,768]{2,1,0:T(8,128)(2,1)S(1)}, u32[]{:S(2)}, u32[]{:S(2)}) collective-permute-start(bf16[4,128,768]{2,1,0:T(8,128)(2,1)S(1)} %get-tuple-element.70), channel_id=1, source_target_pairs={{0,32},{1,33},{2,34},{3,35},{4,36},{5,37},{6,38},{7,39},{8,40},{9,... | collective-permute-start | bytes 2359304 | tf_op jit(solution)/shard_map/ppermute | solution.py:34
  198.2 28.0 %collective-permute-start.6 = (bf16[4,128,768]{2,1,0:T(8,128)(2,1)S(1)}, bf16[4,128,768]{2,1,0:T(8,128)(2,1)S(1)}, u32[]{:S(2)}, u32[]{:S(2)}) collective-permute-start(bf16[4,128,768]{2,1,0:T(8,128)(2,1)S(1)} %get-tuple-element.70), channel_id=1, source_target_pairs={{0,96},{1,97},{2,98},{3,99},{4,100},{5,101},{6,102},{7,103},{8,104... | collective-permute-start | bytes 2359304 | tf_op jit(solution)/shard_map/ppermute | solution.py:34
  223.6 13.3 %collective-permute-start.5 = (bf16[4,64,768]{2,1,0:T(8,128)(2,1)S(1)}, bf16[4,64,768]{2,1,0:T(8,128)(2,1)}, u32[]{:S(2)}, u32[]{:S(2)}) collective-permute-start(bf16[4,64,768]{2,1,0:T(8,128)(2,1)S(1)} %slice.142), channel_id=1, source_target_pairs={{0,32},{1,33},{2,34},{3,35},{4,36},{5,37},{6,38},{7,39},{8,40},{9,... | collective-permute-start | bytes 1179656 | tf_op jit(solution)/shard_map/ppermute | solution.py:34
  227.0 12.5 %collective-permute-start.7 = (bf16[4,64,768]{2,1,0:T(8,128)(2,1)}, bf16[4,64,768]{2,1,0:T(8,128)(2,1)}, u32[]{:S(2)}, u32[]{:S(2)}) collective-permute-start(bf16[4,64,768]{2,1,0:T(8,128)(2,1)} %slice.143), channel_id=1, source_target_pairs={{0,96},{1,97},{2,98},{3,99},{4,100},{5,101},{6,102},{7,103},{8,104... | collective-permute-start | bytes 1179656 | tf_op jit(solution)/shard_map/ppermute | solution.py:34
  251.6 17.1 %all-to-all-start = ((bf16[8,128,384]{1,2,0:T(8,128)(2,1)}), bf16[8,128,384]{1,2,0:T(8,128)(2,1)}, u32[]{:S(2)}, u32[]{:S(2)}) async-start(bf16[8,128,384]{1,2,0:T(8,128)(2,1)} %broadcast_in_dim.39), calls=%async_computation | async-start | bytes 1572864 | tf_op jit(solution)/shard_map/all_to_all | solution.py:68
  276.6 22.9 %all-to-all-start.1 = ((bf16[8,128,640]{2,1,0:T(8,128)(2,1)}), bf16[8,128,640]{2,1,0:T(8,128)(2,1)S(1)}, u32[]{:S(2)}, u32[]{:S(2)}) async-start(bf16[8,128,640]{2,1,0:T(8,128)(2,1)} %broadcast_in_dim.40), calls=%async_computation.1 | async-start | bytes 2621440 | tf_op jit(solution)/shard_map/all_to_all | solution.py:68
  281.3 48.4 %reduce-scatter.2.cloned.1.call-start = ((), (), s32[]{:S(2)}) async-start(), calls=%async_computation.9 | async-start | bytes 1769472 | tf_op jit(solution)/shard_map/reduce_scatter | solution.py:337
  310.7 24.3 %collective-permute-start.25 = (bf16[4,128,512]{2,1,0:T(8,128)(2,1)}, bf16[4,128,512]{2,1,0:T(8,128)(2,1)}, u32[]{:S(2)}, u32[]{:S(2)}) collective-permute-start(bf16[4,128,512]{2,1,0:T(8,128)(2,1)} %get-tuple-element.77), channel_id=1, source_target_pairs={{128,144},{129,145},{130,146},{131,147},{132,148},{133,149},{134,1... | collective-permute-start | bytes 1572872 | tf_op jit(solution)/shard_map/ppermute | solution.py:34
  312.2 19.4 %collective-permute-start.16 = (bf16[128,640]{1,0:T(8,128)(2,1)S(1)}, bf16[128,640]{1,0:T(8,128)(2,1)}, u32[]{:S(2)}, u32[]{:S(2)}) collective-permute-start(bf16[128,640]{1,0:T(8,128)(2,1)S(1)} %get-tuple-element.82), channel_id=1, source_target_pairs={{128,144},{129,145},{130,146},{131,147},{132,148},{133,149},{134,1... | collective-permute-start | bytes 491528 | tf_op jit(solution)/shard_map/ppermute | solution.py:34
  313.5 18.8 %collective-permute-start.15 = (bf16[128,640]{1,0:T(8,128)(2,1)S(1)}, bf16[128,640]{1,0:T(8,128)(2,1)}, u32[]{:S(2)}, u32[]{:S(2)}) collective-permute-start(bf16[128,640]{1,0:T(8,128)(2,1)S(1)} %get-tuple-element.82), channel_id=1, source_target_pairs={{128,136},{129,137},{130,138},{131,139},{132,140},{133,141},{134,1... | collective-permute-start | bytes 491528 | tf_op jit(solution)/shard_map/ppermute | solution.py:34
  314.9 17.5 %collective-permute-start.17 = (bf16[128,640]{1,0:T(8,128)(2,1)S(1)}, bf16[128,640]{1,0:T(8,128)(2,1)}, u32[]{:S(2)}, u32[]{:S(2)}) collective-permute-start(bf16[128,640]{1,0:T(8,128)(2,1)S(1)} %get-tuple-element.82), channel_id=1, source_target_pairs={{128,152},{129,153},{130,154},{131,155},{132,156},{133,157},{134,1... | collective-permute-start | bytes 491528 | tf_op jit(solution)/shard_map/ppermute | solution.py:34
  333.6 13.9 %collective-permute-start.19 = (bf16[4,128,640]{2,1,0:T(8,128)(2,1)S(1)}, bf16[4,128,640]{2,1,0:T(8,128)(2,1)S(1)}, u32[]{:S(2)}, u32[]{:S(2)}) collective-permute-start(bf16[4,128,640]{2,1,0:T(8,128)(2,1)S(1)} %get-tuple-element.75), channel_id=1, source_target_pairs={{128,192},{129,193},{130,194},{131,195},{132,196},{133,197},{134,1... | collective-permute-start | bytes 1966088 | tf_op jit(solution)/shard_map/ppermute | solution.py:34
  334.3 17.8 %collective-permute-start.18 = (bf16[4,128,640]{2,1,0:T(8,128)(2,1)S(1)}, bf16[4,128,640]{2,1,0:T(8,128)(2,1)S(1)}, u32[]{:S(2)}, u32[]{:S(2)}) collective-permute-start(bf16[4,128,640]{2,1,0:T(8,128)(2,1)S(1)} %get-tuple-element.75), channel_id=1, source_target_pairs={{128,160},{129,161},{130,162},{131,163},{132,164},{133,165},{134,1... | collective-permute-start | bytes 1966088 | tf_op jit(solution)/shard_map/ppermute | solution.py:34
  335.0 17.0 %collective-permute-start.20 = (bf16[4,128,640]{2,1,0:T(8,128)(2,1)S(1)}, bf16[4,128,640]{2,1,0:T(8,128)(2,1)S(1)}, u32[]{:S(2)}, u32[]{:S(2)}) collective-permute-start(bf16[4,128,640]{2,1,0:T(8,128)(2,1)S(1)} %get-tuple-element.75), channel_id=1, source_target_pairs={{128,224},{129,225},{130,226},{131,227},{132,228},{133,229},{134,2... | collective-permute-start | bytes 1966088 | tf_op jit(solution)/shard_map/ppermute | solution.py:34
  338.0 30.0 %collective-permute-start.9 = (bf16[4,128,192]{1,2,0:T(8,128)(2,1)}, bf16[4,128,192]{1,2,0:T(8,128)(2,1)}, u32[]{:S(2)}, u32[]{:S(2)}) collective-permute-start(bf16[4,128,192]{1,2,0:T(8,128)(2,1)} %get-tuple-element.66), channel_id=1, source_target_pairs={{0,64},{1,65},{2,66},{3,67},{4,68},{5,69},{6,70},{7,71},{8,72},{9,... | collective-permute-start | bytes 589832 | tf_op jit(solution)/shard_map/ppermute | solution.py:34
  343.3 24.7 %collective-permute-start.8 = (bf16[4,128,192]{1,2,0:T(8,128)(2,1)}, bf16[4,128,192]{1,2,0:T(8,128)(2,1)}, u32[]{:S(2)}, u32[]{:S(2)}) collective-permute-start(bf16[4,128,192]{1,2,0:T(8,128)(2,1)} %get-tuple-element.67), channel_id=1, source_target_pairs={{0,32},{1,33},{2,34},{3,35},{4,36},{5,37},{6,38},{7,39},{8,40},{9,... | collective-permute-start | bytes 589832 | tf_op jit(solution)/shard_map/ppermute | solution.py:34
  347.5 20.5 %collective-permute-start.10 = (bf16[4,128,192]{1,2,0:T(8,128)(2,1)}, bf16[4,128,192]{1,2,0:T(8,128)(2,1)}, u32[]{:S(2)}, u32[]{:S(2)}) collective-permute-start(bf16[4,128,192]{1,2,0:T(8,128)(2,1)} %get-tuple-element.68), channel_id=1, source_target_pairs={{0,96},{1,97},{2,98},{3,99},{4,100},{5,101},{6,102},{7,103},{8,104... | collective-permute-start | bytes 589832 | tf_op jit(solution)/shard_map/ppermute | solution.py:34
  360.9 36.8 %all-to-all-start.2 = ((bf16[8,2,128,128]{3,2,1,0:T(8,128)(2,1)}), bf16[8,2,128,128]{3,2,1,0:T(8,128)(2,1)}, u32[]{:S(2)}, u32[]{:S(2)}) async-start(bf16[8,2,128,128]{3,2,1,0:T(8,128)(2,1)} %broadcast_in_dim.41), calls=%async_computation.3 | async-start | bytes 1048576 | tf_op jit(solution)/shard_map/all_to_all | solution.py:68
  369.3 15.3 %collective-permute-start.13 = (bf16[4,128,192]{1,2,0:T(8,128)(2,1)S(1)}, bf16[4,128,192]{1,2,0:T(8,128)(2,1)S(1)}, u32[]{:S(2)}, u32[]{:S(2)}) collective-permute-start(bf16[4,128,192]{1,2,0:T(8,128)(2,1)S(1)} %get-tuple-element.62), channel_id=1, source_target_pairs={{0,24},{1,25},{2,26},{3,27},{4,28},{5,29},{6,30},{7,31},{8,0},{9,1... | collective-permute-start | bytes 589832 | tf_op jit(solution)/shard_map/ppermute | solution.py:34
  374.0 14.7 %collective-permute-start.12 = (bf16[4,128,192]{1,2,0:T(8,128)(2,1)S(1)}, bf16[4,128,192]{1,2,0:T(8,128)(2,1)S(1)}, u32[]{:S(2)}, u32[]{:S(2)}) collective-permute-start(bf16[4,128,192]{1,2,0:T(8,128)(2,1)S(1)} %get-tuple-element.63), channel_id=1, source_target_pairs={{0,16},{1,17},{2,18},{3,19},{4,20},{5,21},{6,22},{7,23},{8,24},{9,... | collective-permute-start | bytes 589832 | tf_op jit(solution)/shard_map/ppermute | solution.py:34
  404.5 27.3 %all-to-all-start.3 = ((bf16[16,160,128]{2,1,0:T(8,128)(2,1)}), bf16[16,160,128]{2,1,0:T(8,128)(2,1)S(1)}, u32[]{:S(2)}, u32[]{:S(2)}) async-start(bf16[16,160,128]{2,1,0:T(8,128)(2,1)} %broadcast_in_dim.43), calls=%async_computation.4 | async-start | bytes 1310720 | tf_op jit(solution)/shard_map/all_to_all | solution.py:68
  432.9 18.9 %all-to-all-start.5 = ((bf16[8,384,128]{2,1,0:T(8,128)(2,1)}), bf16[8,384,128]{2,1,0:T(8,128)(2,1)}, u32[]{:S(2)}, u32[]{:S(2)}) async-start(bf16[8,384,128]{2,1,0:T(8,128)(2,1)} %broadcast_in_dim.44), calls=%async_computation.6 | async-start | bytes 1572864 | tf_op jit(solution)/shard_map/all_to_all | solution.py:68
  451.7 21.7 %all-to-all-start.4 = ((bf16[8,128,640]{1,2,0:T(8,128)(2,1)}), bf16[8,128,640]{1,2,0:T(8,128)(2,1)S(1)}, u32[]{:S(2)}, u32[]{:S(2)}) async-start(bf16[8,128,640]{1,2,0:T(8,128)(2,1)} %fusion.15), calls=%async_computation.5 | async-start | bytes 2621440 | tf_op jit(solution)/shard_map/all_to_all | solution.py:372
  473.4 51.4 %all-to-all-start.6 = ((bf16[16,192,128]{2,1,0:T(8,128)(2,1)}), bf16[16,192,128]{2,1,0:T(8,128)(2,1)S(1)}, u32[]{:S(2)}, u32[]{:S(2)}) async-start(bf16[16,192,128]{2,1,0:T(8,128)(2,1)} %bitcast.80), calls=%async_computation.7 | async-start | bytes 1572864 | tf_op jit(solution)/shard_map/all_to_all | solution.py:380
  482.8 26.4 %collective-permute-start.30 = (bf16[4,128,640]{2,1,0:T(8,128)(2,1)S(1)}, bf16[4,128,640]{2,1,0:T(8,128)(2,1)}, u32[]{:S(2)}, u32[]{:S(2)}) collective-permute-start(bf16[4,128,640]{2,1,0:T(8,128)(2,1)S(1)} %pad_maximum_fusion.8), channel_id=1, source_target_pairs={{128,0},{129,1},{130,2},{131,3},{132,4},{133,5},{134,6},{135,7},{1... | collective-permute-start | bytes 1966088 | tf_op jit(solution)/shard_map/ppermute | solution.py:34
  509.2 19.8 %collective-permute-start.33 = (bf16[4,128,640]{2,1,0:T(8,128)(2,1)}, bf16[4,128,640]{2,1,0:T(8,128)(2,1)}, u32[]{:S(2)}, u32[]{:S(2)}) collective-permute-start(bf16[4,128,640]{2,1,0:T(8,128)(2,1)} %collective-permute-done.30), channel_id=1, source_target_pairs={{0,96},{1,97},{2,98},{3,99},{4,100},{5,101},{6,102},{7,103},{8,104... | collective-permute-start | bytes 1966088 | tf_op jit(solution)/shard_map/ppermute | solution.py:34
  513.6 15.5 %collective-permute-start.32 = (bf16[4,128,640]{2,1,0:T(8,128)(2,1)}, bf16[4,128,640]{2,1,0:T(8,128)(2,1)}, u32[]{:S(2)}, u32[]{:S(2)}) collective-permute-start(bf16[4,128,640]{2,1,0:T(8,128)(2,1)} %collective-permute-done.30), channel_id=1, source_target_pairs={{0,64},{1,65},{2,66},{3,67},{4,68},{5,69},{6,70},{7,71},{8,72},{9,... | collective-permute-start | bytes 1966088 | tf_op jit(solution)/shard_map/ppermute | solution.py:34
  516.3 18.6 %collective-permute-start.31 = (bf16[4,128,640]{2,1,0:T(8,128)(2,1)}, bf16[4,128,640]{2,1,0:T(8,128)(2,1)}, u32[]{:S(2)}, u32[]{:S(2)}) collective-permute-start(bf16[4,128,640]{2,1,0:T(8,128)(2,1)} %collective-permute-done.30), channel_id=1, source_target_pairs={{0,32},{1,33},{2,34},{3,35},{4,36},{5,37},{6,38},{7,39},{8,40},{9,... | collective-permute-start | bytes 1966088 | tf_op jit(solution)/shard_map/ppermute | solution.py:34
  (36 other events, 987.5 us)
Sparse Core Ops, SparseCore 0:
  10.5 152.8 all-gather.3
  165.9 77.5 all-gather.5
  284.7 44.9 reduce-scatter.1
